TPU v7x, 32 devices: a whole 2x2x4 slice. The times are simulated.
32 devices in a mesh: sim: 8 (over y, x, core), section: 4 (over z).
Axes of the slice: x: 2, y: 2, z: 4, core: 2. Of those that a mesh axis runs over, the one named last changes fastest.
Arguments:
- density: float32 [4, 768, 512], P(None, 'sim', 'section'), may hold values from 0.5 to 2
- momentum: float32 [3, 4, 768, 512], P(None, None, 'sim', 'section'), may hold values from -1 to 1
- energy: float32 [4, 768, 512], P(None, 'sim', 'section'), may hold values from 4 to 8
- membership: int32 [192, 128], P(('sim', 'section')), may hold values from 0 to 63
- slot_of_brick: int32 [8, 4], P('sim'), may hold values from 0 to 3, each once within a row
Outputs:
- coded: float32 [5, 4, 768, 512], P(None, None, ('sim', 'section'))
- group_peak: float32 [5, 64], replicated
Inputs may be any that keep to these rules, and one draw needn't show every extreme that they name: `slot_of_brick`: each row is a permutation of the 4 bricks.
All inputs are finite; a program needn't handle non-finite values.
Results may differ from a plain program's by a relative error of at most 0.0003.
Values sent between devices are 32-bit elements; how exact they have to be, the bound alone decides.
No kernel may reach another device: no remote copies, remote signals or barrier semaphores. Data moves between devices by JAX's collectives and lax.ppermute only.
A program may use at most 64 MiB of HBM per device.

v0:
```python
import functools

import jax
import jax.numpy as jnp
import numpy as np
from jax import lax
from jax.experimental import pallas as pl
from jax.experimental.pallas import tpu as pltpu
from jax.sharding import PartitionSpec as P

GAMMA_LESS = 0.4
COURANT = 0.05
DIFFUSE = 0.1
EPSILON = 1e-06
FIELDS = 5
PAD = 8
COLUMN_ROWS = 8
LABEL_ROWS = 8
LANES = 128
EVEN = 0.5
WIDE = float(np.sqrt(0.5) * np.cos(np.pi / 8))
NARROW = float(np.sqrt(0.5) * np.cos(3 * np.pi / 8))
VMEM_LIMIT = 48 * 1024 * 1024


def vmem():
    return pl.BlockSpec(memory_space=pltpu.VMEM)


def lanes_of(shape):
    return lax.broadcasted_iota(jnp.int32, shape, 1)


def butterfly(a, b, c, d):
    s, t, u, v = a + d, b + c, a - d, b - c
    return (
        EVEN * (s + t),
        WIDE * u + NARROW * v,
        EVEN * (s - t),
        NARROW * u - WIDE * v,
    )


def cosine(k, d):
    factor = 0.5 if k == 0 else np.sqrt(0.5)
    return float(factor * np.cos(np.pi * (2 * d + 1) * k / 8))


def write_matrix(matrix, width):
    step = 16
    row = lax.broadcasted_iota(jnp.int32, (step, width), 0)
    column = lanes_of((step, width))
    quarter = width // 4
    k, j, d = lax.div(column, quarter), lax.rem(column, quarter), lax.rem(row, 4)
    entry = jnp.zeros((step, width), jnp.float32)
    for a in range(4):
        for b in range(4):
            entry = jnp.where(jnp.logical_and(k == a, d == b), cosine(a, b), entry)
    high = entry.astype(jnp.bfloat16).astype(jnp.float32)
    low = entry - high
    zero = jnp.zeros((step, width), jnp.bfloat16)
    for start in range(0, width, step):
        own = j == lax.div(row + start, 4)
        upper = jnp.where(own, high, 0.0).astype(jnp.bfloat16)
        lower = jnp.where(own, low, 0.0).astype(jnp.bfloat16)
        matrix[start : start + step, 0:width] = upper
        matrix[start : start + step, width : 2 * width] = lower
        matrix[width + start : width + start + step, 0:width] = upper
        matrix[width + start : width + start + step, width : 2 * width] = zero


def kernel_params():
    return pltpu.CompilerParams(vmem_limit_bytes=VMEM_LIMIT)


def array(shape, dtype=jnp.float32):
    return jax.ShapeDtypeStruct(shape, dtype)


def pack_kernel(conserved, membership, slots, matrix, first_x, last_x, labels):
    fields, depth, y, width = conserved.shape
    quarter = y // 4
    lane = lanes_of((y, width))
    first = jnp.zeros((y, width), jnp.float32)
    last = jnp.zeros((y, width), jnp.float32)
    for j in range(fields * depth):
        value = conserved[j // depth, j % depth]
        first = jnp.where(lane == j, pltpu.roll(value, j, 1) if j else value, first)
        last = jnp.where(lane == j, pltpu.roll(value, j + 1, 1), last)
    rows, columns = membership.shape
    labels[...] = jnp.zeros(labels.shape, jnp.float32)
    for t in range(columns // LANES):
        part = membership[:, t * LANES : (t + 1) * LANES].astype(jnp.float32)
        labels[t * rows : (t + 1) * rows, :] = part
    labels[LABEL_ROWS - 1 : LABEL_ROWS, 0 : slots.shape[1]] = slots[...].astype(jnp.float32)
    own = labels[...]
    for column, out in ((first, first_x), (last, last_x)):
        packed = column[0:quarter]
        for c in range(1, 4):
            packed = packed + pltpu.roll(column[c * quarter : (c + 1) * quarter], 32 * c, 1)
        out[0:quarter, :] = packed
        out[quarter:, :] = own
    write_matrix(matrix, width)


def pack(conserved, membership, slots):
    y, width = conserved.shape[2:]
    shapes = [
        array((2 * width, 2 * width), jnp.bfloat16),
        array((y // 4 + LABEL_ROWS, width)),
        array((y // 4 + LABEL_ROWS, width)),
        array((LABEL_ROWS, width)),
    ]
    return pl.pallas_call(
        pack_kernel,
        out_shape=shapes,
        in_specs=[vmem()] * 3,
        out_specs=[vmem()] * 4,
        compiler_params=kernel_params(),
    )(conserved, membership, slots)


def slot_of(labels, brick):
    row = labels[LABEL_ROWS - 1 : LABEL_ROWS, :]
    return jnp.max(jnp.where(lanes_of(row.shape) == brick, row, 0.0)).astype(jnp.int32)


def fluxes(c):
    rho, mx, my, mz, e = c
    inverse = 1.0 / rho
    u, v = mx * inverse, my * inverse
    pressure = GAMMA_LESS * (e - 0.5 * (mx * mx + my * my + mz * mz) * inverse)
    total = e + pressure
    flux_x = (mx, mx * u + pressure, my * u, mz * u, total * u)
    flux_y = (my, mx * v, my * v + pressure, mz * v, total * v)
    return flux_x, flux_y


def column_terms(own, depth, sign):
    fields = [pltpu.roll(own, LANES - depth * f, 1) if f else own for f in range(FIELDS)]
    flux_x, unused = fluxes(fields)
    return [DIFFUSE * fields[f] + sign * flux_x[f] for f in range(FIELDS)]


def row_terms(c):
    rows, width = c[0].shape
    lane = lanes_of((rows, width))
    flux_x, flux_y = fluxes(c)
    terms = []
    for f in range(FIELDS):
        base = DIFFUSE * c[f]
        gx, gy = COURANT * flux_x[f], COURANT * flux_y[f]
        from_left = jnp.where(lane == 0, 0.0, pltpu.roll(base + gx, 1, 1))
        from_right = jnp.where(lane == width - 1, 0.0, pltpu.roll(base - gx, width - 1, 1))
        terms.append(((1.0 - 4.0 * DIFFUSE) * c[f] + from_left + from_right, base + gy, base - gy))
    return terms


def beside(low, high, z):
    rows, width = low.shape
    lane = lanes_of((rows, width))
    at_left = pltpu.roll(low, LANES - z, 1) if z else low
    at_right = pltpu.roll(high, LANES - 1 - z, 1)
    return jnp.where(lane == 0, at_left, jnp.where(lane == width - 1, at_right, 0.0))


def fold_rows(across, down, up, j, origin, number, stride):
    t = {}
    for o in range(-3, 7):
        t[o] = (
            across[j, pl.ds(origin + o, number, stride=stride), :]
            + down[j, pl.ds(origin + o - 1, number, stride=stride), :]
            + up[j, pl.ds(origin + o + 1, number, stride=stride), :]
        )
    residual = [
        t[m] - (9.0 / 16.0) * (t[m - 1] + t[m + 1]) + (1.0 / 16.0) * (t[m - 3] + t[m + 3])
        for m in range(4)
    ]
    return butterfly(*residual)


def halves(value):
    high = value.astype(jnp.bfloat16)
    return high, (value - high.astype(jnp.float32)).astype(jnp.bfloat16)


def over_lanes(peak):
    peak = jnp.maximum(peak, pltpu.roll(peak, 64, 1))
    return jnp.maximum(peak, pltpu.roll(peak, 32, 1))


def partner_of(me, k, count):
    if count & (count - 1) == 0:
        return me ^ k
    return lax.rem(me + k, count)


def sender_of(me, k, count):
    if count & (count - 1) == 0:
        return me ^ k
    return lax.rem(me - k + count, count)


def flux_kernel(conserved, across, down, up):
    fields, depth, y, width = conserved.shape
    step = 16

    def flux_rows(i, carry):
        r = pl.ds(pl.multiple_of(i * step, step), step)
        padded = pl.ds(pl.multiple_of(i * step + PAD, PAD), step)
        for z in range(depth):
            for f, (a, d, u) in enumerate(row_terms([conserved[f, z, r, :] for f in range(fields)])):
                j = f * depth + z
                across[j, r, :] = a
                down[j, padded, :] = d
                up[j, padded, :] = u
        return carry

    lax.fori_loop(0, y // step, flux_rows, 0)


def own_fluxes(conserved):
    fields, depth, y, width = conserved.shape
    total = fields * depth
    tall = array((total, y + 2 * PAD, width))
    return pl.pallas_call(
        flux_kernel,
        out_shape=[array((total, y, width)), tall, tall],
        in_specs=[vmem()],
        out_specs=[vmem()] * 3,
        compiler_params=kernel_params(),
        cost_estimate=pl.CostEstimate(flops=40 * total * y * width, bytes_accessed=16 * total * y * width, transcendentals=0),
    )(conserved)


def edge_kernel(conserved, left, right, first_y, last_y, columns):
    fields, depth, y, width = conserved.shape
    total, quarter = fields * depth, y // 4
    for side, column in enumerate((left, right)):
        for c in range(4):
            value = column[0:quarter, :]
            value = pltpu.roll(value, LANES - 32 * c, 1) if c else value
            columns[side, c * quarter : (c + 1) * quarter, :] = value
        place = 4 * total + 4 * side
        first_y[place : place + 4, :] = columns[side, 0:4, :]
        last_y[place : place + 4, :] = columns[side, y - 4 : y, :]
    for j in range(total):
        first_y[4 * j : 4 * j + 4, :] = conserved[j // depth, j % depth, 0:4, :]
        last_y[4 * j : 4 * j + 4, :] = conserved[j // depth, j % depth, y - 4 : y, :]


def edge_rows(conserved, left, right):
    fields, depth, y, width = conserved.shape
    message = array((4 * fields * depth + COLUMN_ROWS, width))
    return pl.pallas_call(
        edge_kernel,
        out_shape=[message, message, array((2, y, width))],
        in_specs=[vmem()] * 3,
        out_specs=[vmem()] * 3,
        compiler_params=kernel_params(),
    )(conserved, left, right)


def brick_kernel(count, *refs):
    inside, down, up, columns, matrix = refs[:5]
    outs, refs = refs[5 : 5 + count], refs[5 + count :]
    blocks, rim_a, rim_d, rim_u, across, edges, folded, split, coefficients, staged = refs
    total, y, width = inside.shape
    depth = total // FIELDS
    nb = y // 4
    rows = y // count

    for side in range(2):
        for f, value in enumerate(column_terms(columns[side], depth, COURANT if side == 0 else -COURANT)):
            edges[side, f] = value

    step = 24

    def join_rows(i, carry):
        r = pl.ds(pl.multiple_of(i * step, 8), step)
        padded = pl.ds(pl.multiple_of(i * step + PAD, PAD), step)
        for f in range(FIELDS):
            low, high = edges[0, f, r, :], edges[1, f, r, :]
            for z in range(depth):
                j = f * depth + z
                across[j, padded, :] = inside[j, r, :] + beside(low, high, z)
        return carry

    lax.fori_loop(0, y // step, join_rows, 0)

    def predict_rows(j, carry):
        for k, value in enumerate(fold_rows(across, down, up, j, PAD, nb, 4)):
            folded[j, k * nb : (k + 1) * nb, :] = value
        for source, rim in ((across, rim_a), (down, rim_d), (up, rim_u)):
            rim[j, 0:8, :] = source[j, PAD : PAD + 8, :]
            rim[j, 8:16, :] = source[j, y : y + 8, :]
        return carry

    lax.fori_loop(0, total, predict_rows, 0)

    piece = 32

    def transform_field(f, carry):
        for start in range(0, y, piece):
            values = [folded[f * depth + z, start : start + piece, :] for z in range(4)]
            for k, value in enumerate(butterfly(*values)):
                high, low = halves(value)
                split[k * y + start : k * y + start + piece, 0:width] = high
                split[k * y + start : k * y + start + piece, width : 2 * width] = low
        product = jnp.dot(split[...], matrix[...], preferred_element_type=jnp.float32)
        result = product[:, 0:width] + product[:, width : 2 * width]
        peak = None
        for k in range(4):
            for m in range(4):
                value = result[k * y + m * nb : k * y + (m + 1) * nb]
                coefficients[f * depth + k, pl.ds(m, nb, stride=4), :] = value
                size = jnp.abs(value)
                peak = size if peak is None else jnp.maximum(peak, size)
        blocks[f] = over_lanes(peak)
        return carry

    lax.fori_loop(0, FIELDS, transform_field, 0)

    me = lax.axis_index("section")
    if rows % 8 == 0:
        for k in range(count):
            p = partner_of(me, k, count)
            for j in range(total):
                outs[k][j // depth, j % depth] = coefficients[j, pl.ds(pl.multiple_of(p * rows, 8), rows), :]
    else:
        for p in range(count):
            staged[p] = coefficients[:, p * rows : (p + 1) * rows, :]
        for k in range(count):
            p = partner_of(me, k, count)
            for j in range(total):
                outs[k][j // depth, j % depth] = staged[p, j]


def transform_bricks(count, inside, down, up, columns, matrix):
    total, y, width = inside.shape
    depth = total // FIELDS
    rows, tall = y // count, y + 2 * PAD
    chunk = array((FIELDS, depth, rows, width))
    rim = array((total, 2 * PAD, width))
    results = pl.pallas_call(
        functools.partial(brick_kernel, count),
        out_shape=[chunk] * count + [array((FIELDS, y // 4, width))] + [rim] * 3,
        in_specs=[vmem()] * 5,
        out_specs=[vmem()] * (count + 4),
        scratch_shapes=[
            pltpu.VMEM((total, tall, width), jnp.float32),
            pltpu.VMEM((2, FIELDS, y, width), jnp.float32),
            pltpu.VMEM((total, y, width), jnp.float32),
            pltpu.VMEM((depth * y, 2 * width), jnp.bfloat16),
            pltpu.VMEM((total, y, width), jnp.float32),
            pltpu.VMEM((1, 1, 8, LANES) if rows % 8 == 0 else (count, total, rows, width), jnp.float32),
        ],
        compiler_params=kernel_params(),
        cost_estimate=pl.CostEstimate(flops=80 * total * y * width, bytes_accessed=16 * total * y * width, transcendentals=0),
    )(inside, down, up, columns, matrix)
    return results[:count], results[count], results[count + 1 :]


def leaving_order(count):
    return [*range(2, count), 1, 0]


def mend_kernel(count, *refs):
    chunks, refs = refs[:count], refs[count:]
    top, bottom, blocks, rim_a, rim_d, rim_u, matrix = refs[:7]
    outs, mended, refs = refs[7 : 7 + count], refs[7 + count], refs[8 + count :]
    halo, columns, across, down, up, folded, split, result, fixed = refs
    fields, depth, rows, width = chunks[0].shape
    total = fields * depth
    nb = blocks.shape[1]

    halo[...] = jnp.ones(halo.shape, jnp.float32)
    columns[...] = jnp.ones(columns.shape, jnp.float32)
    for j in range(total):
        halo[j, 4:8, :] = top[4 * j : 4 * j + 4, :]
        halo[j, 8:12, :] = bottom[4 * j : 4 * j + 4, :]
    for side in range(2):
        place = 4 * total + 4 * side
        columns[side, 4:8, :] = top[place : place + 4, :]
        columns[side, 8:12, :] = bottom[place : place + 4, :]
    low = column_terms(columns[0], depth, COURANT)
    high = column_terms(columns[1], depth, -COURANT)
    for z in range(depth):
        c = [halo[f * depth + z] for f in range(fields)]
        for f, (a, d, u) in enumerate(row_terms(c)):
            j = f * depth + z
            values = (a + beside(low[f], high[f], z), d, u)
            for value, rim, target in zip(values, (rim_a, rim_d, rim_u), (across, down, up)):
                target[j, 0:8, :] = value[0:8]
                target[j, 8:24, :] = rim[j]
                target[j, 24:32, :] = value[8:16]
    for j in range(total):
        for k, value in enumerate(fold_rows(across, down, up, j, PAD, 2, 12)):
            folded[j, 2 * k : 2 * k + 2, :] = value
    for f in range(fields):
        values = butterfly(*[folded[f * depth + z] for z in range(4)])
        for half in range(2):
            both = jnp.concatenate(values[2 * half : 2 * half + 2], axis=0)
            upper, lower = halves(both)
            place = f * 32 + half * 16
            split[place : place + 16, 0:width] = upper
            split[place : place + 16, width : 2 * width] = lower
    product = jnp.dot(split[...], matrix[...], preferred_element_type=jnp.float32)
    result[...] = product[:, 0:width] + product[:, width : 2 * width]
    for j in range(total):
        for side in range(2):
            fixed[side, j] = result[pl.ds(8 * j + side, 4, stride=2), :]
    mended[...] = blocks[...]
    for f in range(fields):
        for side in range(2):
            size = jnp.abs(fixed[side, f * depth])
            for z in range(1, depth):
                size = jnp.maximum(size, jnp.abs(fixed[side, f * depth + z]))
            peak = over_lanes(jnp.max(size, axis=0, keepdims=True))
            row = side * (nb - 1)
            mended[f, row : row + 1, :] = peak

    me = lax.axis_index("section")
    for i, k in enumerate(leaving_order(count)):
        p = partner_of(me, k, count)
        for side, start in ((0, 0), (1, rows - 4)):

            @pl.when(p == side * (count - 1))
            def replace(i=i, side=side, start=start):
                for j in range(total):
                    outs[i][j // depth, j % depth, start : start + 4, :] = fixed[side, j]


def mend(count, chunks, top, bottom, blocks, rims, matrix):
    fields, depth, rows, width = chunks[0].shape
    total = fields * depth
    tall = pltpu.VMEM((total, 4 * PAD, width), jnp.float32)
    results = pl.pallas_call(
        functools.partial(mend_kernel, count),
        out_shape=[array(chunks[0].shape)] * count + [array(blocks.shape)],
        in_specs=[vmem()] * (count + 7),
        out_specs=[vmem()] * (count + 1),
        input_output_aliases={k: k for k in range(count)},
        scratch_shapes=[
            pltpu.VMEM((total, 2 * PAD, width), jnp.float32),
            pltpu.VMEM((2, 2 * PAD, width), jnp.float32),
            tall,
            tall,
            tall,
            pltpu.VMEM((total, 8, width), jnp.float32),
            pltpu.VMEM((8 * total, 2 * width), jnp.bfloat16),
            pltpu.VMEM((8 * total, width), jnp.float32),
            pltpu.VMEM((2, total, 4, width), jnp.float32),
        ],
        compiler_params=kernel_params(),
    )(*[chunks[k] for k in leaving_order(count)], top, bottom, blocks, *rims, matrix)
    return dict(zip(leaving_order(count), results)), results[count]


def group_kernel(count, groups, own_rows, *refs):
    blocks, refs = refs[0], refs[1:]
    messages, (peaks, gathered, listed, packed, table) = refs[:count], refs[count:]
    nb = blocks.shape[1]
    me = lax.axis_index("section")
    slot = slot_of(messages[0], me)
    within = lax.rem(slot, 4) * 32
    tile = lax.div(slot, 4)
    for d, message in enumerate(messages):
        height = gathered.shape[1]
        value = message[message.shape[0] - height :, :]
        if count > 4:
            value = pltpu.roll(value, lax.rem(height - tile * own_rows, height), 0)
        gathered[lax.rem(me + count - d, count)] = value
    for q in range(count):
        listed[q * own_rows : (q + 1) * own_rows, :] = gathered[q, 0:own_rows, :]
    part = nb // 4
    band = lax.div(lanes_of((part, LANES)), 32)
    labels = jnp.zeros((part, LANES), jnp.float32)
    for c in range(4):
        turned = pltpu.roll(listed[c * part : (c + 1) * part, :], lax.rem(32 * c - within + LANES, LANES), 1)
        labels = jnp.where(band == c, turned, labels)
    for f in range(FIELDS):
        own = jnp.zeros((part, LANES), jnp.float32)
        for c in range(4):
            own = jnp.where(band == c, blocks[f, c * part : (c + 1) * part, :], own)
        packed[f, 0:part, :] = own
    lane8 = lanes_of((8, LANES))
    sub8 = lax.broadcasted_iota(jnp.int32, (8, LANES), 0)
    label_rows = [jnp.broadcast_to(labels[r : r + 1], (8, LANES)) for r in range(part)]

    def group_tile(g, carry):
        wanted = (sub8 + g * 8).astype(jnp.float32)
        matches = [label_rows[r] == wanted for r in range(part)]
        found = jnp.zeros((8, LANES), jnp.float32)
        for f in range(FIELDS):
            best = jnp.zeros((8, LANES), jnp.float32)
            for r in range(part):
                row = jnp.broadcast_to(packed[f, r : r + 1, :], (8, LANES))
                best = jnp.maximum(best, jnp.where(matches[r], row, 0.0))
            found = jnp.where(lane8 == f, jnp.max(best, axis=1, keepdims=True), found)
        table[pl.ds(pl.multiple_of(g * 8, 8), 8), :] = found
        return carry

    high = table.shape[0]
    if groups < high:
        table[...] = jnp.zeros((high, LANES), jnp.float32)
    lax.fori_loop(0, pl.cdiv(groups, 8), group_tile, 0)
    for g in range(high // LANES):
        peaks[:, g * LANES : (g + 1) * LANES] = jnp.transpose(table[g * LANES : (g + 1) * LANES, :])[0:8]


def group_maxima(count, groups, own_rows, blocks, messages):
    high = pl.cdiv(groups, LANES) * LANES
    nb = blocks.shape[1]
    return pl.pallas_call(
        functools.partial(group_kernel, count, groups, own_rows),
        out_shape=array((8, high)),
        in_specs=[vmem()] * (count + 1),
        out_specs=vmem(),
        scratch_shapes=[
            pltpu.VMEM((count, messages[0].shape[0], LANES), jnp.float32),
            pltpu.VMEM((nb, LANES), jnp.float32),
            pltpu.VMEM((FIELDS, 8, LANES), jnp.float32),
            pltpu.VMEM((high, LANES), jnp.float32),
        ],
        compiler_params=kernel_params(),
    )(blocks, *messages)


def scale_kernel(count, groups, *refs):
    chunks, refs = refs[:count], refs[count:]
    peaks, labels, coded, group_peak, wide = refs
    fields, depth, rows, width = chunks[0].shape
    nb = rows // 4
    high = peaks.shape[1]
    me = lax.axis_index("section")
    group_peak[...] = peaks[0:fields, 0:groups]
    own_labels = labels[...].astype(jnp.int32)
    lane = lanes_of((8, LANES))
    inverse = 1.0 / (peaks[...] + EPSILON)
    tables = [
        [jnp.broadcast_to(inverse[f : f + 1, g * LANES : (g + 1) * LANES], (8, LANES)) for g in range(high // LANES)]
        for f in range(fields)
    ]
    for i, k in enumerate(leaving_order(count)):
        slot = slot_of(labels, sender_of(me, k, count))
        tile = own_labels
        if count > 4:
            tile = pltpu.roll(tile, lax.rem(LABEL_ROWS - lax.div(slot, 4) * nb, LABEL_ROWS), 0)
        within = lax.rem(slot, 4) * 32 + lax.rem(lane, 32)
        own = jnp.take_along_axis(tile, within, axis=1)
        place = pl.ds(pl.multiple_of(slot * width, width), width)
        for f in range(fields):
            if high == LANES:
                found = jnp.take_along_axis(tables[f][0], own, axis=1)
            else:
                found = jnp.zeros((8, LANES), jnp.float32)
                inside = lax.rem(own, LANES)
                for g in range(high // LANES):
                    here = jnp.take_along_axis(tables[f][g], inside, axis=1)
                    found = jnp.where(lax.div(own, LANES) == g, here, found)
            for m in range(4):
                wide[i, f, pl.ds(m, nb, stride=4), :] = found[0:nb]
            factor = wide[i, f]
            for z in range(depth):
                coded[f, z, :, place] = chunks[i][f, z] * factor


def scale(count, groups, chunks, peaks, labels):
    fields, depth, rows, width = chunks[0].shape
    return pl.pallas_call(
        functools.partial(scale_kernel, count, groups),
        out_shape=[array((fields, depth, rows, width * count)), array((fields, groups))],
        in_specs=[vmem()] * (count + 2),
        out_specs=[vmem()] * 2,
        scratch_shapes=[
            pltpu.VMEM((count, fields, rows, width), jnp.float32),
        ],
        compiler_params=kernel_params(),
    )(*chunks, peaks, labels)


def ring(axis, shift):
    count = lax.axis_size(axis)
    return [(i, (i + shift) % count) for i in range(count)]


def exchange_pairs(count, k):
    if count & (count - 1) == 0:
        return [(i, i ^ k) for i in range(count)]
    return [(i, (i + k) % count) for i in range(count)]


def steps_over(axis):
    count = lax.axis_size(axis)
    span, shifts = 1, []
    while span < count:
        shifts.append(min(span, count - span))
        span += shifts[-1]
    return shifts


def with_others(value, axis, shifts):
    count = lax.axis_size(axis)
    others = [lax.ppermute(value, axis, exchange_pairs(count, k)) for k in shifts]
    return functools.reduce(jnp.maximum, others, value)


def per_device(density, momentum, energy, membership, slot_of_brick):
    count = lax.axis_size("section")
    groups = 2 * lax.axis_size("sim") * count
    conserved = jnp.concatenate([density[None], momentum, energy[None]], axis=0)
    matrix, first_x, last_x, labels = pack(conserved, membership, slot_of_brick)
    left = lax.ppermute(last_x, "section", ring("section", 1))
    right = lax.ppermute(first_x, "section", ring("section", -1))
    far = [lax.ppermute(labels, "section", ring("section", d)) for d in range(2, count - 1)]
    inside, down, up = own_fluxes(conserved)
    left, right, inside = lax.optimization_barrier((left, right, inside))
    first_y, last_y, columns = edge_rows(conserved, left, right)
    first_y, last_y, *far = lax.optimization_barrier((first_y, last_y, *far))
    top = lax.ppermute(last_y, "sim", ring("sim", 1))
    bottom = lax.ppermute(first_y, "sim", ring("sim", -1))
    chunks, blocks, rims = transform_bricks(count, inside, down, up, columns, matrix)
    chunks, blocks = mend(count, chunks, top, bottom, blocks, rims, matrix)
    moved = {0: chunks[0]}
    for k in leaving_order(count)[:-1]:
        moved[k] = lax.ppermute(chunks[k], "section", exchange_pairs(count, k))
    peaks = group_maxima(count, groups, membership.shape[0], blocks, [labels, left, *far, right])
    for shift in steps_over("sim"):
        peaks = with_others(peaks, "sim", [shift])
    for shift in steps_over("section"):
        peaks = with_others(peaks, "section", [shift])
    return tuple(scale(count, groups, [moved[k] for k in leaving_order(count)], peaks, labels))


def solution(mesh):
    placed = (
        P(None, "sim", "section"),
        P(None, None, "sim", "section"),
        P(None, "sim", "section"),
        P(("sim", "section"), None),
        P("sim", None),
    )
    return jax.shard_map(
        per_device,
        mesh=mesh,
        in_specs=placed,
        out_specs=(P(None, None, ("sim", "section"), None), P()),
        check_vma=False,
    )
```

profile of v0, /device:TPU:0, one launch (start us, length us, event | category | flops | bytes accessed | tf_op | source)
XLA Modules:
  0.0 44.3 jit_solution(5869611741476713971)
XLA Ops:
  0.6 0.0 copy-start
  0.6 0.0 copy-start.1
  0.7 1.3 %pad_maximum_fusion.conserved = f32[5,4,96,128]{3,2,1,0:T(8,128)S(1)} fusion(f32[1,4,96,128]{3,2,1,0:T(8,128)} %bitcast.2, f32[3,4,96,128]{3,2,1,0:T(8,128)} %param.6, f32[1,4,96,128]{3,2,1,0:T(8,128)} %bitcast.3), kind=kLoop, calls=%fused_computation | loop fusion | flops 491520 | bytes 1966080 | tf_op jit(solution)/shard_map/concatenate | solution.py:612
  2.0 0.0 copy-done
  2.0 0.0 copy-done.1
  2.0 0.6 %shard_map.68 = (bf16[256,256]{1,0:T(8,128)(2,1)S(1)}, f32[32,128]{1,0:T(8,128)S(1)}, f32[32,128]{1,0:T(8,128)S(1)}, f32[8,128]{1,0:T(8,128)S(1)}) custom-call(f32[5,4,96,128]{3,2,1,0:T(8,128)S(1)} %pad_maximum_fusion.conserved, s32[6,128]{1,0:T(8,128)S(1)} %copy-done, s32[1,4]{1,0:T(1,128)S(1)} %copy-done.1), custom_call_target="tpu_custom_call" | custom-call | tf_op jit(solution)/shard_map/pallas_call | solution.py:114
  2.6 3.1 %collective-permute-start = (f32[32,128]{1,0:T(8,128)S(1)}, f32[32,128]{1,0:T(8,128)S(1)}, u32[]{:S(2)}, u32[]{:S(2)}) collective-permute-start(f32[32,128]{1,0:T(8,128)S(1)} %get-tuple-element.31), channel_id=1, source_target_pairs={{0,1},{1,2},{2,3},{3,0},{4,5},{5,6},{6,7},{7,4},{8,9},{9,10},{10,1... | collective-permute-start | bytes 49160 | tf_op jit(solution)/shard_map/ppermute | solution.py:614
  5.7 2.1 %collective-permute-start.1 = (f32[32,128]{1,0:T(8,128)S(1)}, f32[32,128]{1,0:T(8,128)S(1)}, u32[]{:S(2)}, u32[]{:S(2)}) collective-permute-start(f32[32,128]{1,0:T(8,128)S(1)} %get-tuple-element.32), channel_id=1, source_target_pairs={{0,3},{1,0},{2,1},{3,2},{4,7},{5,4},{6,5},{7,6},{8,11},{9,8},{10,9... | collective-permute-start | bytes 49160 | tf_op jit(solution)/shard_map/ppermute | solution.py:615
  7.7 0.9 %collective-permute-start.2 = (f32[8,128]{1,0:T(8,128)S(1)}, f32[8,128]{1,0:T(8,128)S(1)}, u32[]{:S(2)}, u32[]{:S(2)}) collective-permute-start(f32[8,128]{1,0:T(8,128)S(1)} %get-tuple-element.47.refs_1_.refs_5_), channel_id=1, source_target_pairs={{0,2},{1,3},{2,0},{3,1},{4,6},{5,7},{6,4},{7,5},{8,10},{9,11},{10,... | collective-permute-start | bytes 12296 | tf_op jit(solution)/shard_map/ppermute | solution.py:616
  8.7 0.9 %shard_map.69 = (f32[20,96,128]{2,1,0:T(8,128)S(1)}, f32[20,112,128]{2,1,0:T(8,128)S(1)}, f32[20,112,128]{2,1,0:T(8,128)S(1)}) custom-call(f32[5,4,96,128]{3,2,1,0:T(8,128)S(1)} %pad_maximum_fusion.conserved), custom_call_target="tpu_custom_call" | custom-call | flops 9830400 | bytes 3932160 | tf_op jit(solution)/shard_map/pallas_call | solution.py:226
  9.6 0.0 collective-permute-done.left.refs_2_
  9.7 0.0 collective-permute-done.1.right.refs_4_
  9.7 0.1 shard_map.70
  9.8 2.5 %collective-permute-done.2.refs_3_ = f32[8,128]{1,0:T(8,128)S(1)} collective-permute-done((f32[8,128]{1,0:T(8,128)S(1)}, f32[8,128]{1,0:T(8,128)S(1)}, u32[]{:S(2)}, u32[]{:S(2)}) %collective-permute-start.2) | collective-permute-done | bytes 4128 | tf_op jit(solution)/shard_map/ppermute | solution.py:616
  12.2 0.0 collective-permute-start.3
  12.3 2.6 %collective-permute-start.4 = (f32[88,128]{1,0:T(8,128)S(1)}, f32[88,128]{1,0:T(8,128)S(1)}, u32[]{:S(2)}, u32[]{:S(2)}) collective-permute-start(f32[88,128]{1,0:T(8,128)S(1)} %get-tuple-element.49), channel_id=1, source_target_pairs={{0,28},{4,0},{8,4},{12,8},{16,12},{20,16},{24,20},{28,24},{1,29},{... | collective-permute-start | bytes 135176 | tf_op jit(solution)/shard_map/ppermute | solution.py:622
  14.9 3.4 %shard_map.71 = (f32[5,4,24,128]{3,2,1,0:T(8,128)S(1)}, f32[5,4,24,128]{3,2,1,0:T(8,128)S(1)}, f32[5,4,24,128]{3,2,1,0:T(8,128)S(1)}, f32[5,4,24,128]{3,2,1,0:T(...) custom-call(f32[20,96,128]{2,1,0:T(8,128)S(1)} %get-tuple-element.34, ...), custom_call_target="tpu_custom_call" | custom-call | flops 19660800 | bytes 3932160 | tf_op jit(solution)/shard_map/pallas_call | solution.py:345
  18.3 0.0 collective-permute-done.3.refs_4_
  18.3 0.0 collective-permute-done.4.refs_5_
  18.3 0.8 %shard_map.72 = (f32[5,4,24,128]{3,2,1,0:T(8,128)S(1)}, f32[5,4,24,128]{3,2,1,0:T(8,128)S(1)}, f32[5,4,24,128]{3,2,1,0:T(8,128)S(1)}, f32[5,4,24,128]{3,2,1,0:T(8,128)S(1)}, f32[5,24,128]{2,1,0:T(8,128)S(1)}) custom-call(f32[5,4,24,128]{3,2,1,0:T(8,128)S(1)} %get-tuple-element.41.refs_0_, ...), custom_call_target="tpu_custom_call", output_to_operand_aliasing={{0}: (0, {}), {1}: (1, {}), {2}: (2, {}), {3}: (3, {})} | custom-call | tf_op jit(solution)/shard_map/pallas_call | solution.py:438
  19.2 1.0 %collective-permute-start.5 = (f32[5,4,24,128]{3,2,1,0:T(8,128)S(1)}, f32[5,4,24,128]{3,2,1,0:T(8,128)S(1)}, u32[]{:S(2)}, u32[]{:S(2)}) collective-permute-start(f32[5,4,24,128]{3,2,1,0:T(8,128)S(1)} %get-tuple-element.54), channel_id=1, source_target_pairs={{0,2},{1,3},{2,0},{3,1},{4,6},{5,7},{6,4},{7,5},{8,10},{9,11},{10,... | collective-permute-start | bytes 737288 | tf_op jit(solution)/shard_map/ppermute | solution.py:627
  20.2 1.4 %collective-permute-start.6 = (f32[5,4,24,128]{3,2,1,0:T(8,128)S(1)}, f32[5,4,24,128]{3,2,1,0:T(8,128)S(1)}, u32[]{:S(2)}, u32[]{:S(2)}) collective-permute-start(f32[5,4,24,128]{3,2,1,0:T(8,128)S(1)} %get-tuple-element.55), channel_id=1, source_target_pairs={{0,3},{1,2},{2,1},{3,0},{4,7},{5,6},{6,5},{7,4},{8,11},{9,10},{10,... | collective-permute-start | bytes 737288 | tf_op jit(solution)/shard_map/ppermute | solution.py:627
  21.5 1.2 %collective-permute-start.7 = (f32[5,4,24,128]{3,2,1,0:T(8,128)S(1)}, f32[5,4,24,128]{3,2,1,0:T(8,128)S(1)}, u32[]{:S(2)}, u32[]{:S(2)}) collective-permute-start(f32[5,4,24,128]{3,2,1,0:T(8,128)S(1)} %get-tuple-element.56), channel_id=1, source_target_pairs={{0,1},{1,0},{2,3},{3,2},{4,5},{5,4},{6,7},{7,6},{8,9},{9,8},{10,11... | collective-permute-start | bytes 737288 | tf_op jit(solution)/shard_map/ppermute | solution.py:627
  22.7 1.0 %shard_map.73 = f32[8,128]{1,0:T(8,128)S(1)} custom-call(f32[5,24,128]{2,1,0:T(8,128)S(1)} %get-tuple-element.58.refs_0_, f32[8,128]{1,0:T(8,128)S(1)} %get-tuple-element.47.refs_1_.refs_5_, f32[32,128]{1,0:T(8,128)S(1)} %collective-permute-done.left.refs_2_, f32[8,128]{1,0:T(8,128)S(1)} %collective-permute-done.2.refs_3_, ...), custom_call_target="tpu_custom_call" | custom-call | tf_op jit(solution)/shard_map/pallas_call | solution.py:515
  23.7 0.0 collective-permute-start.8
  23.7 1.2 %collective-permute-done.8 = f32[8,128]{1,0:T(8,128)S(1)} collective-permute-done((f32[8,128]{1,0:T(8,128)S(1)}, f32[8,128]{1,0:T(8,128)S(1)}, u32[]{:S(2)}, u32[]{:S(2)}) %collective-permute-start.8) | collective-permute-done | bytes 4128 | tf_op jit(solution)/shard_map/ppermute | solution.py:605
  24.9 0.7 %collective-permute-start.9 = (f32[8,128]{1,0:T(8,128)S(1)}, f32[8,128]{1,0:T(8,128)S(1)}, u32[]{:S(2)}, u32[]{:S(2)}) collective-permute-start(f32[8,128]{1,0:T(8,128)S(1)} %max.15), channel_id=1, source_target_pairs={{0,8},{4,12},{8,0},{12,4},{16,24},{20,28},{24,16},{28,20},{1,9},{5... | collective-permute-start | bytes 12296 | tf_op jit(solution)/shard_map/ppermute | solution.py:605
  25.6 2.9 %collective-permute-done.9 = f32[8,128]{1,0:T(8,128)S(1)} collective-permute-done((f32[8,128]{1,0:T(8,128)S(1)}, f32[8,128]{1,0:T(8,128)S(1)}, u32[]{:S(2)}, u32[]{:S(2)}) %collective-permute-start.9) | collective-permute-done | bytes 4128 | tf_op jit(solution)/shard_map/ppermute | solution.py:605
  28.5 1.7 %collective-permute-start.10 = (f32[8,128]{1,0:T(8,128)S(1)}, f32[8,128]{1,0:T(8,128)S(1)}, u32[]{:S(2)}, u32[]{:S(2)}) collective-permute-start(f32[8,128]{1,0:T(8,128)S(1)} %max.16), channel_id=1, source_target_pairs={{0,16},{4,20},{8,24},{12,28},{16,0},{20,4},{24,8},{28,12},{1,17},{... | collective-permute-start | bytes 12296 | tf_op jit(solution)/shard_map/ppermute | solution.py:605
  30.2 1.9 %collective-permute-done.10 = f32[8,128]{1,0:T(8,128)S(1)} collective-permute-done((f32[8,128]{1,0:T(8,128)S(1)}, f32[8,128]{1,0:T(8,128)S(1)}, u32[]{:S(2)}, u32[]{:S(2)}) %collective-permute-start.10) | collective-permute-done | bytes 4128 | tf_op jit(solution)/shard_map/ppermute | solution.py:605
  32.1 0.8 %collective-permute-start.11 = (f32[8,128]{1,0:T(8,128)S(1)}, f32[8,128]{1,0:T(8,128)S(1)}, u32[]{:S(2)}, u32[]{:S(2)}) collective-permute-start(f32[8,128]{1,0:T(8,128)S(1)} %max.17), channel_id=1, source_target_pairs={{0,1},{1,0},{2,3},{3,2},{4,5},{5,4},{6,7},{7,6},{8,9},{9,8},{10,11... | collective-permute-start | bytes 12296 | tf_op jit(solution)/shard_map/ppermute | solution.py:605
  33.0 5.4 %collective-permute-done.11 = f32[8,128]{1,0:T(8,128)S(1)} collective-permute-done((f32[8,128]{1,0:T(8,128)S(1)}, f32[8,128]{1,0:T(8,128)S(1)}, u32[]{:S(2)}, u32[]{:S(2)}) %collective-permute-start.11) | collective-permute-done | bytes 4128 | tf_op jit(solution)/shard_map/ppermute | solution.py:605
  38.4 0.5 %collective-permute-start.12 = (f32[8,128]{1,0:T(8,128)S(1)}, f32[8,128]{1,0:T(8,128)S(1)}, u32[]{:S(2)}, u32[]{:S(2)}) collective-permute-start(f32[8,128]{1,0:T(8,128)S(1)} %max.18), channel_id=1, source_target_pairs={{0,2},{1,3},{2,0},{3,1},{4,6},{5,7},{6,4},{7,5},{8,10},{9,11},{10,... | collective-permute-start | bytes 12296 | tf_op jit(solution)/shard_map/ppermute | solution.py:605
  38.9 4.0 %collective-permute-done.12 = f32[8,128]{1,0:T(8,128)S(1)} collective-permute-done((f32[8,128]{1,0:T(8,128)S(1)}, f32[8,128]{1,0:T(8,128)S(1)}, u32[]{:S(2)}, u32[]{:S(2)}) %collective-permute-start.12) | collective-permute-done | bytes 4128 | tf_op jit(solution)/shard_map/ppermute | solution.py:605
  42.9 0.0 collective-permute-done.5.refs_0_
  42.9 0.0 collective-permute-done.6.refs_1_
  42.9 0.0 collective-permute-done.7.refs_2_
  42.9 1.4 %shard_map.74 = (f32[5,4,24,512]{3,2,1,0:T(8,128)}, f32[5,64]{1,0:T(8,128)}) custom-call(f32[5,4,24,128]{3,2,1,0:T(8,128)S(1)} %collective-permute-done.5.refs_0_, f32[5,4,24,128]{3,2,1,0:T(8,128)S(1)} %collective-permute-done.6.refs_1_, f32[5,4,24,128]{3,2,1,0:T(8,128)S(1)} %collective-permute-done.7.refs_2_, ...), custom_call_target="tpu_custom_call" | custom-call | tf_op jit(solution)/shard_map/pallas_call | solution.py:571
  (5 shorter events, 0.0 us)
Async XLA Ops:
  0.6 1.3 %copy-start = (s32[6,128]{1,0:T(8,128)S(1)}, s32[6,128]{1,0:T(8,128)}, u32[]{:S(2)}) copy-start(s32[6,128]{1,0:T(8,128)} %membership.1) | copy-start | bytes 9220
  0.6 1.3 %copy-start.1 = (s32[1,4]{1,0:T(1,128)S(1)}, s32[1,4]{1,0:T(1,128)}, u32[]{:S(2)}) copy-start(s32[1,4]{1,0:T(1,128)} %slots.1) | copy-start | bytes 52
  2.6 7.1 %collective-permute-start = (f32[32,128]{1,0:T(8,128)S(1)}, f32[32,128]{1,0:T(8,128)S(1)}, u32[]{:S(2)}, u32[]{:S(2)}) collective-permute-start(f32[32,128]{1,0:T(8,128)S(1)} %get-tuple-element.31), channel_id=1, source_target_pairs={{0,1},{1,2},{2,3},{3,0},{4,5},{5,6},{6,7},{7,4},{8,9},{9,10},{10,1... | collective-permute-start | bytes 49160 | tf_op jit(solution)/shard_map/ppermute | solution.py:614
  5.7 4.0 %collective-permute-start.1 = (f32[32,128]{1,0:T(8,128)S(1)}, f32[32,128]{1,0:T(8,128)S(1)}, u32[]{:S(2)}, u32[]{:S(2)}) collective-permute-start(f32[32,128]{1,0:T(8,128)S(1)} %get-tuple-element.32), channel_id=1, source_target_pairs={{0,3},{1,0},{2,1},{3,2},{4,7},{5,4},{6,5},{7,6},{8,11},{9,8},{10,9... | collective-permute-start | bytes 49160 | tf_op jit(solution)/shard_map/ppermute | solution.py:615
  7.7 4.5 %collective-permute-start.2 = (f32[8,128]{1,0:T(8,128)S(1)}, f32[8,128]{1,0:T(8,128)S(1)}, u32[]{:S(2)}, u32[]{:S(2)}) collective-permute-start(f32[8,128]{1,0:T(8,128)S(1)} %get-tuple-element.47.refs_1_.refs_5_), channel_id=1, source_target_pairs={{0,2},{1,3},{2,0},{3,1},{4,6},{5,7},{6,4},{7,5},{8,10},{9,11},{10,... | collective-permute-start | bytes 12296 | tf_op jit(solution)/shard_map/ppermute | solution.py:616
  12.2 6.1 %collective-permute-start.3 = (f32[88,128]{1,0:T(8,128)S(1)}, f32[88,128]{1,0:T(8,128)S(1)}, u32[]{:S(2)}, u32[]{:S(2)}) collective-permute-start(f32[88,128]{1,0:T(8,128)S(1)} %get-tuple-element.48), channel_id=1, source_target_pairs={{0,4},{4,8},{8,12},{12,16},{16,20},{20,24},{24,28},{28,0},{1,5},{5... | collective-permute-start | bytes 135176 | tf_op jit(solution)/shard_map/ppermute | solution.py:621
  12.3 6.1 %collective-permute-start.4 = (f32[88,128]{1,0:T(8,128)S(1)}, f32[88,128]{1,0:T(8,128)S(1)}, u32[]{:S(2)}, u32[]{:S(2)}) collective-permute-start(f32[88,128]{1,0:T(8,128)S(1)} %get-tuple-element.49), channel_id=1, source_target_pairs={{0,28},{4,0},{8,4},{12,8},{16,12},{20,16},{24,20},{28,24},{1,29},{... | collective-permute-start | bytes 135176 | tf_op jit(solution)/shard_map/ppermute | solution.py:622
  19.2 23.8 %collective-permute-start.5 = (f32[5,4,24,128]{3,2,1,0:T(8,128)S(1)}, f32[5,4,24,128]{3,2,1,0:T(8,128)S(1)}, u32[]{:S(2)}, u32[]{:S(2)}) collective-permute-start(f32[5,4,24,128]{3,2,1,0:T(8,128)S(1)} %get-tuple-element.54), channel_id=1, source_target_pairs={{0,2},{1,3},{2,0},{3,1},{4,6},{5,7},{6,4},{7,5},{8,10},{9,11},{10,... | collective-permute-start | bytes 737288 | tf_op jit(solution)/shard_map/ppermute | solution.py:627
  20.2 22.8 %collective-permute-start.6 = (f32[5,4,24,128]{3,2,1,0:T(8,128)S(1)}, f32[5,4,24,128]{3,2,1,0:T(8,128)S(1)}, u32[]{:S(2)}, u32[]{:S(2)}) collective-permute-start(f32[5,4,24,128]{3,2,1,0:T(8,128)S(1)} %get-tuple-element.55), channel_id=1, source_target_pairs={{0,3},{1,2},{2,1},{3,0},{4,7},{5,6},{6,5},{7,4},{8,11},{9,10},{10,... | collective-permute-start | bytes 737288 | tf_op jit(solution)/shard_map/ppermute | solution.py:627
  21.5 21.4 %collective-permute-start.7 = (f32[5,4,24,128]{3,2,1,0:T(8,128)S(1)}, f32[5,4,24,128]{3,2,1,0:T(8,128)S(1)}, u32[]{:S(2)}, u32[]{:S(2)}) collective-permute-start(f32[5,4,24,128]{3,2,1,0:T(8,128)S(1)} %get-tuple-element.56), channel_id=1, source_target_pairs={{0,1},{1,0},{2,3},{3,2},{4,5},{5,4},{6,7},{7,6},{8,9},{9,8},{10,11... | collective-permute-start | bytes 737288 | tf_op jit(solution)/shard_map/ppermute | solution.py:627
  23.7 1.2 %collective-permute-start.8 = (f32[8,128]{1,0:T(8,128)S(1)}, f32[8,128]{1,0:T(8,128)S(1)}, u32[]{:S(2)}, u32[]{:S(2)}) collective-permute-start(f32[8,128]{1,0:T(8,128)S(1)} %shard_map.73), channel_id=1, source_target_pairs={{0,4},{4,0},{8,12},{12,8},{16,20},{20,16},{24,28},{28,24},{1,5},{5... | collective-permute-start | bytes 12296 | tf_op jit(solution)/shard_map/ppermute | solution.py:605
  24.9 3.6 %collective-permute-start.9 = (f32[8,128]{1,0:T(8,128)S(1)}, f32[8,128]{1,0:T(8,128)S(1)}, u32[]{:S(2)}, u32[]{:S(2)}) collective-permute-start(f32[8,128]{1,0:T(8,128)S(1)} %max.15), channel_id=1, source_target_pairs={{0,8},{4,12},{8,0},{12,4},{16,24},{20,28},{24,16},{28,20},{1,9},{5... | collective-permute-start | bytes 12296 | tf_op jit(solution)/shard_map/ppermute | solution.py:605
  28.5 3.6 %collective-permute-start.10 = (f32[8,128]{1,0:T(8,128)S(1)}, f32[8,128]{1,0:T(8,128)S(1)}, u32[]{:S(2)}, u32[]{:S(2)}) collective-permute-start(f32[8,128]{1,0:T(8,128)S(1)} %max.16), channel_id=1, source_target_pairs={{0,16},{4,20},{8,24},{12,28},{16,0},{20,4},{24,8},{28,12},{1,17},{... | collective-permute-start | bytes 12296 | tf_op jit(solution)/shard_map/ppermute | solution.py:605
  32.1 6.3 %collective-permute-start.11 = (f32[8,128]{1,0:T(8,128)S(1)}, f32[8,128]{1,0:T(8,128)S(1)}, u32[]{:S(2)}, u32[]{:S(2)}) collective-permute-start(f32[8,128]{1,0:T(8,128)S(1)} %max.17), channel_id=1, source_target_pairs={{0,1},{1,0},{2,3},{3,2},{4,5},{5,4},{6,7},{7,6},{8,9},{9,8},{10,11... | collective-permute-start | bytes 12296 | tf_op jit(solution)/shard_map/ppermute | solution.py:605
  38.4 4.5 %collective-permute-start.12 = (f32[8,128]{1,0:T(8,128)S(1)}, f32[8,128]{1,0:T(8,128)S(1)}, u32[]{:S(2)}, u32[]{:S(2)}) collective-permute-start(f32[8,128]{1,0:T(8,128)S(1)} %max.18), channel_id=1, source_target_pairs={{0,2},{1,3},{2,0},{3,1},{4,6},{5,7},{6,4},{7,5},{8,10},{9,11},{10,... | collective-permute-start | bytes 12296 | tf_op jit(solution)/shard_map/ppermute | solution.py:605
where the time goes:
time: 44.4 us; the launch traced here: 44.3 us
  waiting for transfers between devices  17.9 us (40%)
  starting transfers between devices  16.1 us (36%)
  Pallas kernels  8.23 us (19%)
  other arithmetic  1.31 us (3%)
  between operations  0.76 us (2%)
    ppermute x5, waiting for transfers between devices, with_others(): lax.ppermute(value, axis, exchange_pairs(count, k))  15.4 us
    ppermute x5, starting transfers between devices, with_others(): lax.ppermute(value, axis, exchange_pairs(count, k))  3.79 us
    ppermute x3, starting transfers between devices, per_device(): moved[k] = lax.ppermute(chunks[k], 'section', exchange_pairs(count, k))  3.55 us
    pallas_call x1, Pallas kernels, transform_bricks(): pl.pallas_call(functools.partial(brick_kernel, count), out_shape=[chunk]...  3.4 us
    ppermute x1, starting transfers between devices, per_device(): left = lax.ppermute(last_x, 'section', ring('section', 1))  3.06 us
    ppermute x1, starting transfers between devices, per_device(): bottom = lax.ppermute(first_y, 'sim', ring('sim', -1))  2.64 us
    ppermute x1, waiting for transfers between devices, per_device(): lax.ppermute(labels, 'section', ring('section', d))  2.49 us
    ppermute x1, starting transfers between devices, per_device(): right = lax.ppermute(first_x, 'section', ring('section', -1))  2.09 us
  transfers between devices with their start and end apart: 13, of which 6 were waited for; matrix products, arithmetic and copies ran while one was open for 0% of the time, Pallas kernels for 12%

commit v1 on v0

--- a/solution.py
+++ b/solution.py
@@ -264,7 +264,7 @@
 def brick_kernel(count, *refs):
     inside, down, up, columns, matrix = refs[:5]
     outs, refs = refs[5 : 5 + count], refs[5 + count :]
-    blocks, rim_a, rim_d, rim_u, across, edges, folded, split, coefficients, staged = refs
+    blocks, rim_a, rim_d, rim_u, across, edges, split, coefficients, staged = refs
     total, y, width = inside.shape
     depth = total // FIELDS
     nb = y // 4
@@ -275,39 +275,26 @@
             edges[side, f] = value
 
     step = 24
-
-    def join_rows(i, carry):
-        r = pl.ds(pl.multiple_of(i * step, 8), step)
-        padded = pl.ds(pl.multiple_of(i * step + PAD, PAD), step)
+    for start in range(0, y, step):
         for f in range(FIELDS):
-            low, high = edges[0, f, r, :], edges[1, f, r, :]
+            low, high = edges[0, f, start : start + step, :], edges[1, f, start : start + step, :]
             for z in range(depth):
                 j = f * depth + z
-                across[j, padded, :] = inside[j, r, :] + beside(low, high, z)
-        return carry
-
-    lax.fori_loop(0, y // step, join_rows, 0)
-
-    def predict_rows(j, carry):
-        for k, value in enumerate(fold_rows(across, down, up, j, PAD, nb, 4)):
-            folded[j, k * nb : (k + 1) * nb, :] = value
+                value = inside[j, start : start + step, :] + beside(low, high, z)
+                across[j, PAD + start : PAD + start + step, :] = value
+    for j in range(total):
         for source, rim in ((across, rim_a), (down, rim_d), (up, rim_u)):
             rim[j, 0:8, :] = source[j, PAD : PAD + 8, :]
             rim[j, 8:16, :] = source[j, y : y + 8, :]
-        return carry
-
-    lax.fori_loop(0, total, predict_rows, 0)
-
-    piece = 32
-
-    def transform_field(f, carry):
-        for start in range(0, y, piece):
-            values = [folded[f * depth + z, start : start + piece, :] for z in range(4)]
-            for k, value in enumerate(butterfly(*values)):
-                high, low = halves(value)
-                split[k * y + start : k * y + start + piece, 0:width] = high
-                split[k * y + start : k * y + start + piece, width : 2 * width] = low
-        product = jnp.dot(split[...], matrix[...], preferred_element_type=jnp.float32)
+
+    for f in range(FIELDS):
+        rows_of = [fold_rows(across, down, up, f * depth + z, PAD, nb, 4) for z in range(4)]
+        mixed = [butterfly(*[rows_of[z][m] for z in range(4)]) for m in range(4)]
+        for k in range(4):
+            high, low = halves(jnp.concatenate([mixed[m][k] for m in range(4)], axis=0))
+            split[f, k * y : (k + 1) * y, 0:width] = high
+            split[f, k * y : (k + 1) * y, width : 2 * width] = low
+        product = jnp.dot(split[f], matrix[...], preferred_element_type=jnp.float32)
         result = product[:, 0:width] + product[:, width : 2 * width]
         peak = None
         for k in range(4):
@@ -317,9 +304,6 @@
                 size = jnp.abs(value)
                 peak = size if peak is None else jnp.maximum(peak, size)
         blocks[f] = over_lanes(peak)
-        return carry
-
-    lax.fori_loop(0, FIELDS, transform_field, 0)
 
     me = lax.axis_index("section")
     if rows % 8 == 0:
@@ -350,8 +334,7 @@
         scratch_shapes=[
             pltpu.VMEM((total, tall, width), jnp.float32),
             pltpu.VMEM((2, FIELDS, y, width), jnp.float32),
-            pltpu.VMEM((total, y, width), jnp.float32),
-            pltpu.VMEM((depth * y, 2 * width), jnp.bfloat16),
+            pltpu.VMEM((FIELDS, depth * y, 2 * width), jnp.bfloat16),
             pltpu.VMEM((total, y, width), jnp.float32),
             pltpu.VMEM((1, 1, 8, LANES) if rows % 8 == 0 else (count, total, rows, width), jnp.float32),
         ],

time: 44.4 us -> 44.4 us (level)
  Pallas kernels: 8.23 us -> 6.62 us
  starting transfers between devices: 16.1 us -> 17.3 us
    pallas_call x1, Pallas kernels: 3.4 us -> 1.79 us  [transform_bricks(): pl.pallas_call(functools.partial(brick_kernel, count), out_shape=[chunk]...]
    ppermute x5, starting transfers between devices: 3.79 us -> 5.05 us  [with_others(): lax.ppermute(value, axis, exchange_pairs(count, k))]
  transfers between devices with their start and end apart: 13 -> 13, of which waited for: 6 -> 6; matrix products, arithmetic and copies ran while one was open for 0% -> 0% of each run, Pallas kernels for 12% -> 9%
where the time goes in v1:
time: 44.4 us; the launch traced here: 44.3 us
  waiting for transfers between devices  18.3 us (41%)
  starting transfers between devices  17.3 us (39%)
  Pallas kernels  6.62 us (15%)
  other arithmetic  1.31 us (3%)
  between operations  0.74 us (2%)
    ppermute x5, waiting for transfers between devices, with_others(): lax.ppermute(value, axis, exchange_pairs(count, k))  15.8 us
    ppermute x5, starting transfers between devices, with_others(): lax.ppermute(value, axis, exchange_pairs(count, k))  5.05 us
    ppermute x3, starting transfers between devices, per_device(): moved[k] = lax.ppermute(chunks[k], 'section', exchange_pairs(count, k))  3.55 us
    ppermute x1, starting transfers between devices, per_device(): left = lax.ppermute(last_x, 'section', ring('section', 1))  3.06 us
    ppermute x1, starting transfers between devices, per_device(): bottom = lax.ppermute(first_y, 'sim', ring('sim', -1))  2.64 us
    ppermute x1, waiting for transfers between devices, per_device(): lax.ppermute(labels, 'section', ring('section', d))  2.49 us
    ppermute x1, starting transfers between devices, per_device(): right = lax.ppermute(first_x, 'section', ring('section', -1))  2.09 us
    pallas_call x1, Pallas kernels, transform_bricks(): pl.pallas_call(functools.partial(brick_kernel, count), out_shape=[chunk]...  1.79 us
  transfers between devices with their start and end apart: 13, of which 6 were waited for; matrix products, arithmetic and copies ran while one was open for 0% of the time, Pallas kernels for 9%

profile of v1, /device:TPU:0, one launch (start us, length us, event | category | flops | bytes accessed | tf_op | source)
XLA Modules:
  0.0 44.3 jit_solution(1252591067438639576)
XLA Ops:
  0.6 0.0 copy-start
  0.6 0.0 copy-start.1
  0.7 1.3 %pad_maximum_fusion.conserved = f32[5,4,96,128]{3,2,1,0:T(8,128)S(1)} fusion(f32[1,4,96,128]{3,2,1,0:T(8,128)} %bitcast.2, f32[3,4,96,128]{3,2,1,0:T(8,128)} %param.6, f32[1,4,96,128]{3,2,1,0:T(8,128)} %bitcast.3), kind=kLoop, calls=%fused_computation | loop fusion | flops 491520 | bytes 1966080 | tf_op jit(solution)/shard_map/concatenate | solution.py:595
  2.0 0.0 copy-done
  2.0 0.0 copy-done.1
  2.0 0.6 %shard_map.68 = (bf16[256,256]{1,0:T(8,128)(2,1)S(1)}, f32[32,128]{1,0:T(8,128)S(1)}, f32[32,128]{1,0:T(8,128)S(1)}, f32[8,128]{1,0:T(8,128)S(1)}) custom-call(f32[5,4,96,128]{3,2,1,0:T(8,128)S(1)} %pad_maximum_fusion.conserved, s32[6,128]{1,0:T(8,128)S(1)} %copy-done, s32[1,4]{1,0:T(1,128)S(1)} %copy-done.1), custom_call_target="tpu_custom_call" | custom-call | tf_op jit(solution)/shard_map/pallas_call | solution.py:114
  2.6 3.1 %collective-permute-start = (f32[32,128]{1,0:T(8,128)S(1)}, f32[32,128]{1,0:T(8,128)S(1)}, u32[]{:S(2)}, u32[]{:S(2)}) collective-permute-start(f32[32,128]{1,0:T(8,128)S(1)} %get-tuple-element.31), channel_id=1, source_target_pairs={{0,1},{1,2},{2,3},{3,0},{4,5},{5,6},{6,7},{7,4},{8,9},{9,10},{10,1... | collective-permute-start | bytes 49160 | tf_op jit(solution)/shard_map/ppermute | solution.py:597
  5.7 2.1 %collective-permute-start.1 = (f32[32,128]{1,0:T(8,128)S(1)}, f32[32,128]{1,0:T(8,128)S(1)}, u32[]{:S(2)}, u32[]{:S(2)}) collective-permute-start(f32[32,128]{1,0:T(8,128)S(1)} %get-tuple-element.32), channel_id=1, source_target_pairs={{0,3},{1,0},{2,1},{3,2},{4,7},{5,4},{6,5},{7,6},{8,11},{9,8},{10,9... | collective-permute-start | bytes 49160 | tf_op jit(solution)/shard_map/ppermute | solution.py:598
  7.7 0.9 %collective-permute-start.2 = (f32[8,128]{1,0:T(8,128)S(1)}, f32[8,128]{1,0:T(8,128)S(1)}, u32[]{:S(2)}, u32[]{:S(2)}) collective-permute-start(f32[8,128]{1,0:T(8,128)S(1)} %get-tuple-element.47.refs_1_.refs_5_), channel_id=1, source_target_pairs={{0,2},{1,3},{2,0},{3,1},{4,6},{5,7},{6,4},{7,5},{8,10},{9,11},{10,... | collective-permute-start | bytes 12296 | tf_op jit(solution)/shard_map/ppermute | solution.py:599
  8.7 0.9 %shard_map.69 = (f32[20,96,128]{2,1,0:T(8,128)S(1)}, f32[20,112,128]{2,1,0:T(8,128)S(1)}, f32[20,112,128]{2,1,0:T(8,128)S(1)}) custom-call(f32[5,4,96,128]{3,2,1,0:T(8,128)S(1)} %pad_maximum_fusion.conserved), custom_call_target="tpu_custom_call" | custom-call | flops 9830400 | bytes 3932160 | tf_op jit(solution)/shard_map/pallas_call | solution.py:226
  9.6 0.0 collective-permute-done.left.refs_2_
  9.7 0.0 collective-permute-done.1.right.refs_4_
  9.7 0.1 shard_map.70
  9.8 2.5 %collective-permute-done.2.refs_3_ = f32[8,128]{1,0:T(8,128)S(1)} collective-permute-done((f32[8,128]{1,0:T(8,128)S(1)}, f32[8,128]{1,0:T(8,128)S(1)}, u32[]{:S(2)}, u32[]{:S(2)}) %collective-permute-start.2) | collective-permute-done | bytes 4128 | tf_op jit(solution)/shard_map/ppermute | solution.py:599
  12.2 0.0 collective-permute-start.3
  12.3 2.6 %collective-permute-start.4 = (f32[88,128]{1,0:T(8,128)S(1)}, f32[88,128]{1,0:T(8,128)S(1)}, u32[]{:S(2)}, u32[]{:S(2)}) collective-permute-start(f32[88,128]{1,0:T(8,128)S(1)} %get-tuple-element.49), channel_id=1, source_target_pairs={{0,28},{4,0},{8,4},{12,8},{16,12},{20,16},{24,20},{28,24},{1,29},{... | collective-permute-start | bytes 135176 | tf_op jit(solution)/shard_map/ppermute | solution.py:605
  14.9 1.8 %shard_map.71 = (f32[5,4,24,128]{3,2,1,0:T(8,128)S(1)}, f32[5,4,24,128]{3,2,1,0:T(8,128)S(1)}, f32[5,4,24,128]{3,2,1,0:T(8,128)S(1)}, f32[5,4,24,128]{3,2,1,0:T(...) custom-call(f32[20,96,128]{2,1,0:T(8,128)S(1)} %get-tuple-element.34, ...), custom_call_target="tpu_custom_call" | custom-call | flops 19660800 | bytes 3932160 | tf_op jit(solution)/shard_map/pallas_call | solution.py:329
  16.7 0.0 collective-permute-done.3.refs_4_
  16.7 0.0 collective-permute-done.4.refs_5_
  16.7 0.8 %shard_map.72 = (f32[5,4,24,128]{3,2,1,0:T(8,128)S(1)}, f32[5,4,24,128]{3,2,1,0:T(8,128)S(1)}, f32[5,4,24,128]{3,2,1,0:T(8,128)S(1)}, f32[5,4,24,128]{3,2,1,0:T(8,128)S(1)}, f32[5,24,128]{2,1,0:T(8,128)S(1)}) custom-call(f32[5,4,24,128]{3,2,1,0:T(8,128)S(1)} %get-tuple-element.41.refs_0_, ...), custom_call_target="tpu_custom_call", output_to_operand_aliasing={{0}: (0, {}), {1}: (1, {}), {2}: (2, {}), {3}: (3, {})} | custom-call | tf_op jit(solution)/shard_map/pallas_call | solution.py:421
  17.5 1.0 %collective-permute-start.5 = (f32[5,4,24,128]{3,2,1,0:T(8,128)S(1)}, f32[5,4,24,128]{3,2,1,0:T(8,128)S(1)}, u32[]{:S(2)}, u32[]{:S(2)}) collective-permute-start(f32[5,4,24,128]{3,2,1,0:T(8,128)S(1)} %get-tuple-element.54), channel_id=1, source_target_pairs={{0,2},{1,3},{2,0},{3,1},{4,6},{5,7},{6,4},{7,5},{8,10},{9,11},{10,... | collective-permute-start | bytes 737288 | tf_op jit(solution)/shard_map/ppermute | solution.py:610
  18.5 1.4 %collective-permute-start.6 = (f32[5,4,24,128]{3,2,1,0:T(8,128)S(1)}, f32[5,4,24,128]{3,2,1,0:T(8,128)S(1)}, u32[]{:S(2)}, u32[]{:S(2)}) collective-permute-start(f32[5,4,24,128]{3,2,1,0:T(8,128)S(1)} %get-tuple-element.55), channel_id=1, source_target_pairs={{0,3},{1,2},{2,1},{3,0},{4,7},{5,6},{6,5},{7,4},{8,11},{9,10},{10,... | collective-permute-start | bytes 737288 | tf_op jit(solution)/shard_map/ppermute | solution.py:610
  19.9 1.2 %collective-permute-start.7 = (f32[5,4,24,128]{3,2,1,0:T(8,128)S(1)}, f32[5,4,24,128]{3,2,1,0:T(8,128)S(1)}, u32[]{:S(2)}, u32[]{:S(2)}) collective-permute-start(f32[5,4,24,128]{3,2,1,0:T(8,128)S(1)} %get-tuple-element.56), channel_id=1, source_target_pairs={{0,1},{1,0},{2,3},{3,2},{4,5},{5,4},{6,7},{7,6},{8,9},{9,8},{10,11... | collective-permute-start | bytes 737288 | tf_op jit(solution)/shard_map/ppermute | solution.py:610
  21.1 1.0 %shard_map.73 = f32[8,128]{1,0:T(8,128)S(1)} custom-call(f32[5,24,128]{2,1,0:T(8,128)S(1)} %get-tuple-element.58.refs_0_, f32[8,128]{1,0:T(8,128)S(1)} %get-tuple-element.47.refs_1_.refs_5_, f32[32,128]{1,0:T(8,128)S(1)} %collective-permute-done.left.refs_2_, f32[8,128]{1,0:T(8,128)S(1)} %collective-permute-done.2.refs_3_, ...), custom_call_target="tpu_custom_call" | custom-call | tf_op jit(solution)/shard_map/pallas_call | solution.py:498
  22.1 0.0 collective-permute-start.8
  22.1 1.2 %collective-permute-done.8 = f32[8,128]{1,0:T(8,128)S(1)} collective-permute-done((f32[8,128]{1,0:T(8,128)S(1)}, f32[8,128]{1,0:T(8,128)S(1)}, u32[]{:S(2)}, u32[]{:S(2)}) %collective-permute-start.8) | collective-permute-done | bytes 4128 | tf_op jit(solution)/shard_map/ppermute | solution.py:588
  23.3 2.0 %collective-permute-start.9 = (f32[8,128]{1,0:T(8,128)S(1)}, f32[8,128]{1,0:T(8,128)S(1)}, u32[]{:S(2)}, u32[]{:S(2)}) collective-permute-start(f32[8,128]{1,0:T(8,128)S(1)} %max.15), channel_id=1, source_target_pairs={{0,8},{4,12},{8,0},{12,4},{16,24},{20,28},{24,16},{28,20},{1,9},{5... | collective-permute-start | bytes 12296 | tf_op jit(solution)/shard_map/ppermute | solution.py:588
  25.3 1.6 %collective-permute-done.9 = f32[8,128]{1,0:T(8,128)S(1)} collective-permute-done((f32[8,128]{1,0:T(8,128)S(1)}, f32[8,128]{1,0:T(8,128)S(1)}, u32[]{:S(2)}, u32[]{:S(2)}) %collective-permute-start.9) | collective-permute-done | bytes 4128 | tf_op jit(solution)/shard_map/ppermute | solution.py:588
  26.9 1.7 %collective-permute-start.10 = (f32[8,128]{1,0:T(8,128)S(1)}, f32[8,128]{1,0:T(8,128)S(1)}, u32[]{:S(2)}, u32[]{:S(2)}) collective-permute-start(f32[8,128]{1,0:T(8,128)S(1)} %max.16), channel_id=1, source_target_pairs={{0,16},{4,20},{8,24},{12,28},{16,0},{20,4},{24,8},{28,12},{1,17},{... | collective-permute-start | bytes 12296 | tf_op jit(solution)/shard_map/ppermute | solution.py:588
  28.6 1.9 %collective-permute-done.10 = f32[8,128]{1,0:T(8,128)S(1)} collective-permute-done((f32[8,128]{1,0:T(8,128)S(1)}, f32[8,128]{1,0:T(8,128)S(1)}, u32[]{:S(2)}, u32[]{:S(2)}) %collective-permute-start.10) | collective-permute-done | bytes 4128 | tf_op jit(solution)/shard_map/ppermute | solution.py:588
  30.5 0.9 %collective-permute-start.11 = (f32[8,128]{1,0:T(8,128)S(1)}, f32[8,128]{1,0:T(8,128)S(1)}, u32[]{:S(2)}, u32[]{:S(2)}) collective-permute-start(f32[8,128]{1,0:T(8,128)S(1)} %max.17), channel_id=1, source_target_pairs={{0,1},{1,0},{2,3},{3,2},{4,5},{5,4},{6,7},{7,6},{8,9},{9,8},{10,11... | collective-permute-start | bytes 12296 | tf_op jit(solution)/shard_map/ppermute | solution.py:588
  31.3 7.0 %collective-permute-done.11 = f32[8,128]{1,0:T(8,128)S(1)} collective-permute-done((f32[8,128]{1,0:T(8,128)S(1)}, f32[8,128]{1,0:T(8,128)S(1)}, u32[]{:S(2)}, u32[]{:S(2)}) %collective-permute-start.11) | collective-permute-done | bytes 4128 | tf_op jit(solution)/shard_map/ppermute | solution.py:588
  38.4 0.5 %collective-permute-start.12 = (f32[8,128]{1,0:T(8,128)S(1)}, f32[8,128]{1,0:T(8,128)S(1)}, u32[]{:S(2)}, u32[]{:S(2)}) collective-permute-start(f32[8,128]{1,0:T(8,128)S(1)} %max.18), channel_id=1, source_target_pairs={{0,2},{1,3},{2,0},{3,1},{4,6},{5,7},{6,4},{7,5},{8,10},{9,11},{10,... | collective-permute-start | bytes 12296 | tf_op jit(solution)/shard_map/ppermute | solution.py:588
  38.9 4.0 %collective-permute-done.12 = f32[8,128]{1,0:T(8,128)S(1)} collective-permute-done((f32[8,128]{1,0:T(8,128)S(1)}, f32[8,128]{1,0:T(8,128)S(1)}, u32[]{:S(2)}, u32[]{:S(2)}) %collective-permute-start.12) | collective-permute-done | bytes 4128 | tf_op jit(solution)/shard_map/ppermute | solution.py:588
  42.9 0.0 collective-permute-done.5.refs_0_
  42.9 0.0 collective-permute-done.6.refs_1_
  42.9 0.0 collective-permute-done.7.refs_2_
  42.9 1.4 %shard_map.74 = (f32[5,4,24,512]{3,2,1,0:T(8,128)}, f32[5,64]{1,0:T(8,128)}) custom-call(f32[5,4,24,128]{3,2,1,0:T(8,128)S(1)} %collective-permute-done.5.refs_0_, f32[5,4,24,128]{3,2,1,0:T(8,128)S(1)} %collective-permute-done.6.refs_1_, f32[5,4,24,128]{3,2,1,0:T(8,128)S(1)} %collective-permute-done.7.refs_2_, ...), custom_call_target="tpu_custom_call" | custom-call | tf_op jit(solution)/shard_map/pallas_call | solution.py:554
  (5 shorter events, 0.0 us)
Async XLA Ops:
  0.6 1.3 %copy-start = (s32[6,128]{1,0:T(8,128)S(1)}, s32[6,128]{1,0:T(8,128)}, u32[]{:S(2)}) copy-start(s32[6,128]{1,0:T(8,128)} %membership.1) | copy-start | bytes 9220
  0.6 1.3 %copy-start.1 = (s32[1,4]{1,0:T(1,128)S(1)}, s32[1,4]{1,0:T(1,128)}, u32[]{:S(2)}) copy-start(s32[1,4]{1,0:T(1,128)} %slots.1) | copy-start | bytes 52
  2.6 7.1 %collective-permute-start = (f32[32,128]{1,0:T(8,128)S(1)}, f32[32,128]{1,0:T(8,128)S(1)}, u32[]{:S(2)}, u32[]{:S(2)}) collective-permute-start(f32[32,128]{1,0:T(8,128)S(1)} %get-tuple-element.31), channel_id=1, source_target_pairs={{0,1},{1,2},{2,3},{3,0},{4,5},{5,6},{6,7},{7,4},{8,9},{9,10},{10,1... | collective-permute-start | bytes 49160 | tf_op jit(solution)/shard_map/ppermute | solution.py:597
  5.7 4.0 %collective-permute-start.1 = (f32[32,128]{1,0:T(8,128)S(1)}, f32[32,128]{1,0:T(8,128)S(1)}, u32[]{:S(2)}, u32[]{:S(2)}) collective-permute-start(f32[32,128]{1,0:T(8,128)S(1)} %get-tuple-element.32), channel_id=1, source_target_pairs={{0,3},{1,0},{2,1},{3,2},{4,7},{5,4},{6,5},{7,6},{8,11},{9,8},{10,9... | collective-permute-start | bytes 49160 | tf_op jit(solution)/shard_map/ppermute | solution.py:598
  7.7 4.5 %collective-permute-start.2 = (f32[8,128]{1,0:T(8,128)S(1)}, f32[8,128]{1,0:T(8,128)S(1)}, u32[]{:S(2)}, u32[]{:S(2)}) collective-permute-start(f32[8,128]{1,0:T(8,128)S(1)} %get-tuple-element.47.refs_1_.refs_5_), channel_id=1, source_target_pairs={{0,2},{1,3},{2,0},{3,1},{4,6},{5,7},{6,4},{7,5},{8,10},{9,11},{10,... | collective-permute-start | bytes 12296 | tf_op jit(solution)/shard_map/ppermute | solution.py:599
  12.2 4.4 %collective-permute-start.3 = (f32[88,128]{1,0:T(8,128)S(1)}, f32[88,128]{1,0:T(8,128)S(1)}, u32[]{:S(2)}, u32[]{:S(2)}) collective-permute-start(f32[88,128]{1,0:T(8,128)S(1)} %get-tuple-element.48), channel_id=1, source_target_pairs={{0,4},{4,8},{8,12},{12,16},{16,20},{20,24},{24,28},{28,0},{1,5},{5... | collective-permute-start | bytes 135176 | tf_op jit(solution)/shard_map/ppermute | solution.py:604
  12.3 4.4 %collective-permute-start.4 = (f32[88,128]{1,0:T(8,128)S(1)}, f32[88,128]{1,0:T(8,128)S(1)}, u32[]{:S(2)}, u32[]{:S(2)}) collective-permute-start(f32[88,128]{1,0:T(8,128)S(1)} %get-tuple-element.49), channel_id=1, source_target_pairs={{0,28},{4,0},{8,4},{12,8},{16,12},{20,16},{24,20},{28,24},{1,29},{... | collective-permute-start | bytes 135176 | tf_op jit(solution)/shard_map/ppermute | solution.py:605
  17.5 25.4 %collective-permute-start.5 = (f32[5,4,24,128]{3,2,1,0:T(8,128)S(1)}, f32[5,4,24,128]{3,2,1,0:T(8,128)S(1)}, u32[]{:S(2)}, u32[]{:S(2)}) collective-permute-start(f32[5,4,24,128]{3,2,1,0:T(8,128)S(1)} %get-tuple-element.54), channel_id=1, source_target_pairs={{0,2},{1,3},{2,0},{3,1},{4,6},{5,7},{6,4},{7,5},{8,10},{9,11},{10,... | collective-permute-start | bytes 737288 | tf_op jit(solution)/shard_map/ppermute | solution.py:610
  18.5 24.4 %collective-permute-start.6 = (f32[5,4,24,128]{3,2,1,0:T(8,128)S(1)}, f32[5,4,24,128]{3,2,1,0:T(8,128)S(1)}, u32[]{:S(2)}, u32[]{:S(2)}) collective-permute-start(f32[5,4,24,128]{3,2,1,0:T(8,128)S(1)} %get-tuple-element.55), channel_id=1, source_target_pairs={{0,3},{1,2},{2,1},{3,0},{4,7},{5,6},{6,5},{7,4},{8,11},{9,10},{10,... | collective-permute-start | bytes 737288 | tf_op jit(solution)/shard_map/ppermute | solution.py:610
  19.9 23.0 %collective-permute-start.7 = (f32[5,4,24,128]{3,2,1,0:T(8,128)S(1)}, f32[5,4,24,128]{3,2,1,0:T(8,128)S(1)}, u32[]{:S(2)}, u32[]{:S(2)}) collective-permute-start(f32[5,4,24,128]{3,2,1,0:T(8,128)S(1)} %get-tuple-element.56), channel_id=1, source_target_pairs={{0,1},{1,0},{2,3},{3,2},{4,5},{5,4},{6,7},{7,6},{8,9},{9,8},{10,11... | collective-permute-start | bytes 737288 | tf_op jit(solution)/shard_map/ppermute | solution.py:610
  22.1 1.2 %collective-permute-start.8 = (f32[8,128]{1,0:T(8,128)S(1)}, f32[8,128]{1,0:T(8,128)S(1)}, u32[]{:S(2)}, u32[]{:S(2)}) collective-permute-start(f32[8,128]{1,0:T(8,128)S(1)} %shard_map.73), channel_id=1, source_target_pairs={{0,4},{4,0},{8,12},{12,8},{16,20},{20,16},{24,28},{28,24},{1,5},{5... | collective-permute-start | bytes 12296 | tf_op jit(solution)/shard_map/ppermute | solution.py:588
  23.3 3.6 %collective-permute-start.9 = (f32[8,128]{1,0:T(8,128)S(1)}, f32[8,128]{1,0:T(8,128)S(1)}, u32[]{:S(2)}, u32[]{:S(2)}) collective-permute-start(f32[8,128]{1,0:T(8,128)S(1)} %max.15), channel_id=1, source_target_pairs={{0,8},{4,12},{8,0},{12,4},{16,24},{20,28},{24,16},{28,20},{1,9},{5... | collective-permute-start | bytes 12296 | tf_op jit(solution)/shard_map/ppermute | solution.py:588
  26.9 3.6 %collective-permute-start.10 = (f32[8,128]{1,0:T(8,128)S(1)}, f32[8,128]{1,0:T(8,128)S(1)}, u32[]{:S(2)}, u32[]{:S(2)}) collective-permute-start(f32[8,128]{1,0:T(8,128)S(1)} %max.16), channel_id=1, source_target_pairs={{0,16},{4,20},{8,24},{12,28},{16,0},{20,4},{24,8},{28,12},{1,17},{... | collective-permute-start | bytes 12296 | tf_op jit(solution)/shard_map/ppermute | solution.py:588
  30.5 7.9 %collective-permute-start.11 = (f32[8,128]{1,0:T(8,128)S(1)}, f32[8,128]{1,0:T(8,128)S(1)}, u32[]{:S(2)}, u32[]{:S(2)}) collective-permute-start(f32[8,128]{1,0:T(8,128)S(1)} %max.17), channel_id=1, source_target_pairs={{0,1},{1,0},{2,3},{3,2},{4,5},{5,4},{6,7},{7,6},{8,9},{9,8},{10,11... | collective-permute-start | bytes 12296 | tf_op jit(solution)/shard_map/ppermute | solution.py:588
  38.4 4.5 %collective-permute-start.12 = (f32[8,128]{1,0:T(8,128)S(1)}, f32[8,128]{1,0:T(8,128)S(1)}, u32[]{:S(2)}, u32[]{:S(2)}) collective-permute-start(f32[8,128]{1,0:T(8,128)S(1)} %max.18), channel_id=1, source_target_pairs={{0,2},{1,3},{2,0},{3,1},{4,6},{5,7},{6,4},{7,5},{8,10},{9,11},{10,... | collective-permute-start | bytes 12296 | tf_op jit(solution)/shard_map/ppermute | solution.py:588

commit v2 on v1

--- a/solution.py
+++ b/solution.py
@@ -189,6 +189,17 @@
     return jnp.maximum(peak, pltpu.roll(peak, 32, 1))
 
 
+def leaving_order(count, odd):
+    return [*range(1, count)] if odd else [*range(2, count), 1]
+
+
+def exchange_of(i, count):
+    if i == count - 1:
+        return 0
+    odd = lax.rem(lax.axis_index("sim"), 2)
+    return jnp.where(odd == 1, leaving_order(count, True)[i], leaving_order(count, False)[i])
+
+
 def partner_of(me, k, count):
     if count & (count - 1) == 0:
         return me ^ k
@@ -307,17 +318,17 @@
 
     me = lax.axis_index("section")
     if rows % 8 == 0:
-        for k in range(count):
-            p = partner_of(me, k, count)
+        for i in range(count):
+            p = partner_of(me, exchange_of(i, count), count)
             for j in range(total):
-                outs[k][j // depth, j % depth] = coefficients[j, pl.ds(pl.multiple_of(p * rows, 8), rows), :]
+                outs[i][j // depth, j % depth] = coefficients[j, pl.ds(pl.multiple_of(p * rows, 8), rows), :]
     else:
         for p in range(count):
             staged[p] = coefficients[:, p * rows : (p + 1) * rows, :]
-        for k in range(count):
-            p = partner_of(me, k, count)
+        for i in range(count):
+            p = partner_of(me, exchange_of(i, count), count)
             for j in range(total):
-                outs[k][j // depth, j % depth] = staged[p, j]
+                outs[i][j // depth, j % depth] = staged[p, j]
 
 
 def transform_bricks(count, inside, down, up, columns, matrix):
@@ -342,10 +353,6 @@
         cost_estimate=pl.CostEstimate(flops=80 * total * y * width, bytes_accessed=16 * total * y * width, transcendentals=0),
     )(inside, down, up, columns, matrix)
     return results[:count], results[count], results[count + 1 :]
-
-
-def leaving_order(count):
-    return [*range(2, count), 1, 0]
 
 
 def mend_kernel(count, *refs):
@@ -404,8 +411,8 @@
             mended[f, row : row + 1, :] = peak
 
     me = lax.axis_index("section")
-    for i, k in enumerate(leaving_order(count)):
-        p = partner_of(me, k, count)
+    for i in range(count):
+        p = partner_of(me, exchange_of(i, count), count)
         for side, start in ((0, 0), (1, rows - 4)):
 
             @pl.when(p == side * (count - 1))
@@ -436,8 +443,8 @@
             pltpu.VMEM((2, total, 4, width), jnp.float32),
         ],
         compiler_params=kernel_params(),
-    )(*[chunks[k] for k in leaving_order(count)], top, bottom, blocks, *rims, matrix)
-    return dict(zip(leaving_order(count), results)), results[count]
+    )(*chunks, top, bottom, blocks, *rims, matrix)
+    return results[:count], results[count]
 
 
 def group_kernel(count, groups, own_rows, *refs):
@@ -525,8 +532,8 @@
         [jnp.broadcast_to(inverse[f : f + 1, g * LANES : (g + 1) * LANES], (8, LANES)) for g in range(high // LANES)]
         for f in range(fields)
     ]
-    for i, k in enumerate(leaving_order(count)):
-        slot = slot_of(labels, sender_of(me, k, count))
+    for i in range(count):
+        slot = slot_of(labels, sender_of(me, exchange_of(i, count), count))
         tile = own_labels
         if count > 4:
             tile = pltpu.roll(tile, lax.rem(LABEL_ROWS - lax.div(slot, 4) * nb, LABEL_ROWS), 0)
@@ -574,6 +581,14 @@
     return [(i, (i + k) % count) for i in range(count)]
 
 
+def leaving_pairs(count, i):
+    pairs = []
+    for sim in range(lax.axis_size("sim")):
+        k = leaving_order(count, sim % 2 == 1)[i]
+        pairs += [(sim * count + a, sim * count + b) for a, b in exchange_pairs(count, k)]
+    return pairs
+
+
 def steps_over(axis):
     count = lax.axis_size(axis)
     span, shifts = 1, []
@@ -605,15 +620,19 @@
     bottom = lax.ppermute(first_y, "sim", ring("sim", -1))
     chunks, blocks, rims = transform_bricks(count, inside, down, up, columns, matrix)
     chunks, blocks = mend(count, chunks, top, bottom, blocks, rims, matrix)
-    moved = {0: chunks[0]}
-    for k in leaving_order(count)[:-1]:
-        moved[k] = lax.ppermute(chunks[k], "section", exchange_pairs(count, k))
+    moved = [
+        lax.ppermute(chunks[i], ("sim", "section"), leaving_pairs(count, i)) for i in range(count - 1)
+    ]
     peaks = group_maxima(count, groups, membership.shape[0], blocks, [labels, left, *far, right])
     for shift in steps_over("sim"):
         peaks = with_others(peaks, "sim", [shift])
-    for shift in steps_over("section"):
-        peaks = with_others(peaks, "section", [shift])
-    return tuple(scale(count, groups, [moved[k] for k in leaving_order(count)], peaks, labels))
+    peaks, moved[0] = lax.optimization_barrier((peaks, moved[0]))
+    if count <= 4:
+        peaks = with_others(peaks, "section", range(1, count))
+    else:
+        for shift in steps_over("section"):
+            peaks = with_others(peaks, "section", [shift])
+    return tuple(scale(count, groups, [*moved, chunks[count - 1]], peaks, labels))
 
 
 def solution(mesh):

time: 44.4 us -> 45.9 us (1.034)
  starting transfers between devices: 17.3 us -> 21.1 us
  waiting for transfers between devices: 18.3 us -> 16 us
    ppermute x5 -> x6, waiting for transfers between devices: 15.8 us -> 7.23 us  [with_others(): lax.ppermute(value, axis, exchange_pairs(count, k))]
    ppermute x3, waiting for transfers between devices: 0.01 us -> 6.28 us  [per_device(): lax.ppermute(chunks[i], ('sim', 'section'), leaving_pairs(count, i))]
    ppermute x5 -> x6, starting transfers between devices: 5.05 us -> 8.8 us  [with_others(): lax.ppermute(value, axis, exchange_pairs(count, k))]
  transfers between devices with their start and end apart: 13 -> 14, of which waited for: 6 -> 7; matrix products, arithmetic and copies ran while one was open for 0% -> 0% of each run, Pallas kernels for 9% -> 8%
where the time goes in v2:
time: 45.9 us; the launch traced here: 45.8 us
  starting transfers between devices  21.1 us (46%)
  waiting for transfers between devices  16 us (35%)
  Pallas kernels  6.62 us (14%)
  other arithmetic  1.31 us (3%)
  between operations  0.74 us (2%)
    ppermute x6, starting transfers between devices, with_others(): lax.ppermute(value, axis, exchange_pairs(count, k))  8.8 us
    ppermute x6, waiting for transfers between devices, with_others(): lax.ppermute(value, axis, exchange_pairs(count, k))  7.23 us
    ppermute x3, waiting for transfers between devices, per_device(): lax.ppermute(chunks[i], ('sim', 'section'), leaving_pairs(count, i))  6.28 us
    ppermute x3, starting transfers between devices, per_device(): lax.ppermute(chunks[i], ('sim', 'section'), leaving_pairs(count, i))  3.55 us
    ppermute x1, starting transfers between devices, per_device(): left = lax.ppermute(last_x, 'section', ring('section', 1))  3.06 us
    ppermute x1, starting transfers between devices, per_device(): bottom = lax.ppermute(first_y, 'sim', ring('sim', -1))  2.64 us
    ppermute x1, waiting for transfers between devices, per_device(): lax.ppermute(labels, 'section', ring('section', d))  2.49 us
    ppermute x1, starting transfers between devices, per_device(): right = lax.ppermute(first_x, 'section', ring('section', -1))  2.09 us
  transfers between devices with their start and end apart: 14, of which 7 were waited for; matrix products, arithmetic and copies ran while one was open for 0% of the time, Pallas kernels for 8%

profile of v2, /device:TPU:0, one launch (start us, length us, event | category | flops | bytes accessed | tf_op | source)
XLA Modules:
  0.0 45.8 jit_solution(4865724191414925046)
XLA Ops:
  0.6 0.0 copy-start
  0.6 0.0 copy-start.1
  0.7 1.3 %pad_maximum_fusion.conserved = f32[5,4,96,128]{3,2,1,0:T(8,128)S(1)} fusion(f32[1,4,96,128]{3,2,1,0:T(8,128)} %bitcast.2, f32[3,4,96,128]{3,2,1,0:T(8,128)} %param.6, f32[1,4,96,128]{3,2,1,0:T(8,128)} %bitcast.3), kind=kLoop, calls=%fused_computation | loop fusion | flops 491520 | bytes 1966080 | tf_op jit(solution)/shard_map/concatenate | solution.py:610
  2.0 0.0 copy-done
  2.0 0.0 copy-done.1
  2.0 0.6 %shard_map.68 = (bf16[256,256]{1,0:T(8,128)(2,1)S(1)}, f32[32,128]{1,0:T(8,128)S(1)}, f32[32,128]{1,0:T(8,128)S(1)}, f32[8,128]{1,0:T(8,128)S(1)}) custom-call(f32[5,4,96,128]{3,2,1,0:T(8,128)S(1)} %pad_maximum_fusion.conserved, s32[6,128]{1,0:T(8,128)S(1)} %copy-done, s32[1,4]{1,0:T(1,128)S(1)} %copy-done.1), custom_call_target="tpu_custom_call" | custom-call | tf_op jit(solution)/shard_map/pallas_call | solution.py:114
  2.6 3.1 %collective-permute-start = (f32[32,128]{1,0:T(8,128)S(1)}, f32[32,128]{1,0:T(8,128)S(1)}, u32[]{:S(2)}, u32[]{:S(2)}) collective-permute-start(f32[32,128]{1,0:T(8,128)S(1)} %get-tuple-element.33), channel_id=1, source_target_pairs={{0,1},{1,2},{2,3},{3,0},{4,5},{5,6},{6,7},{7,4},{8,9},{9,10},{10,1... | collective-permute-start | bytes 49160 | tf_op jit(solution)/shard_map/ppermute | solution.py:612
  5.7 2.1 %collective-permute-start.1 = (f32[32,128]{1,0:T(8,128)S(1)}, f32[32,128]{1,0:T(8,128)S(1)}, u32[]{:S(2)}, u32[]{:S(2)}) collective-permute-start(f32[32,128]{1,0:T(8,128)S(1)} %get-tuple-element.34), channel_id=1, source_target_pairs={{0,3},{1,0},{2,1},{3,2},{4,7},{5,4},{6,5},{7,6},{8,11},{9,8},{10,9... | collective-permute-start | bytes 49160 | tf_op jit(solution)/shard_map/ppermute | solution.py:613
  7.7 0.9 %collective-permute-start.2 = (f32[8,128]{1,0:T(8,128)S(1)}, f32[8,128]{1,0:T(8,128)S(1)}, u32[]{:S(2)}, u32[]{:S(2)}) collective-permute-start(f32[8,128]{1,0:T(8,128)S(1)} %get-tuple-element.49.refs_1_.refs_5_), channel_id=1, source_target_pairs={{0,2},{1,3},{2,0},{3,1},{4,6},{5,7},{6,4},{7,5},{8,10},{9,11},{10,... | collective-permute-start | bytes 12296 | tf_op jit(solution)/shard_map/ppermute | solution.py:614
  8.7 0.9 %shard_map.69 = (f32[20,96,128]{2,1,0:T(8,128)S(1)}, f32[20,112,128]{2,1,0:T(8,128)S(1)}, f32[20,112,128]{2,1,0:T(8,128)S(1)}) custom-call(f32[5,4,96,128]{3,2,1,0:T(8,128)S(1)} %pad_maximum_fusion.conserved), custom_call_target="tpu_custom_call" | custom-call | flops 9830400 | bytes 3932160 | tf_op jit(solution)/shard_map/pallas_call | solution.py:237
  9.6 0.0 collective-permute-done.left.refs_2_
  9.7 0.0 collective-permute-done.1.right.refs_4_
  9.7 0.1 shard_map.70
  9.8 2.5 %collective-permute-done.2.refs_3_ = f32[8,128]{1,0:T(8,128)S(1)} collective-permute-done((f32[8,128]{1,0:T(8,128)S(1)}, f32[8,128]{1,0:T(8,128)S(1)}, u32[]{:S(2)}, u32[]{:S(2)}) %collective-permute-start.2) | collective-permute-done | bytes 4128 | tf_op jit(solution)/shard_map/ppermute | solution.py:614
  12.2 0.0 collective-permute-start.3
  12.3 2.6 %collective-permute-start.4 = (f32[88,128]{1,0:T(8,128)S(1)}, f32[88,128]{1,0:T(8,128)S(1)}, u32[]{:S(2)}, u32[]{:S(2)}) collective-permute-start(f32[88,128]{1,0:T(8,128)S(1)} %get-tuple-element.51), channel_id=1, source_target_pairs={{0,28},{4,0},{8,4},{12,8},{16,12},{20,16},{24,20},{28,24},{1,29},{... | collective-permute-start | bytes 135176 | tf_op jit(solution)/shard_map/ppermute | solution.py:620
  14.9 1.8 %shard_map.71 = (f32[5,4,24,128]{3,2,1,0:T(8,128)S(1)}, f32[5,4,24,128]{3,2,1,0:T(8,128)S(1)}, f32[5,4,24,128]{3,2,1,0:T(8,128)S(1)}, f32[5,4,24,128]{3,2,1,0:T(...) custom-call(f32[20,96,128]{2,1,0:T(8,128)S(1)} %get-tuple-element.36, ...), custom_call_target="tpu_custom_call" | custom-call | flops 19660800 | bytes 3932160 | tf_op jit(solution)/shard_map/pallas_call | solution.py:340
  16.7 0.0 collective-permute-done.3.refs_4_
  16.7 0.0 collective-permute-done.4.refs_5_
  16.7 0.8 %shard_map.72 = (f32[5,4,24,128]{3,2,1,0:T(8,128)S(1)}, f32[5,4,24,128]{3,2,1,0:T(8,128)S(1)}, f32[5,4,24,128]{3,2,1,0:T(8,128)S(1)}, f32[5,4,24,128]{3,2,1,0:T(8,128)S(1)}, f32[5,24,128]{2,1,0:T(8,128)S(1)}) custom-call(f32[5,4,24,128]{3,2,1,0:T(8,128)S(1)} %get-tuple-element.43.refs_0_, ...), custom_call_target="tpu_custom_call", output_to_operand_aliasing={{0}: (0, {}), {1}: (1, {}), {2}: (2, {}), {3}: (3, {})} | custom-call | tf_op jit(solution)/shard_map/pallas_call | solution.py:428
  17.5 1.0 %collective-permute-start.8 = (f32[5,4,24,128]{3,2,1,0:T(8,128)S(1)}, f32[5,4,24,128]{3,2,1,0:T(8,128)S(1)}, u32[]{:S(2)}, u32[]{:S(2)}) collective-permute-start(f32[5,4,24,128]{3,2,1,0:T(8,128)S(1)} %get-tuple-element.58), channel_id=1, source_target_pairs={{0,2},{1,3},{2,0},{3,1},{4,5},{5,4},{6,7},{7,6},{8,10},{9,11},{10,... | collective-permute-start | bytes 737288 | tf_op jit(solution)/shard_map/ppermute | solution.py:624
  18.5 1.4 %collective-permute-start.9 = (f32[5,4,24,128]{3,2,1,0:T(8,128)S(1)}, f32[5,4,24,128]{3,2,1,0:T(8,128)S(1)}, u32[]{:S(2)}, u32[]{:S(2)}) collective-permute-start(f32[5,4,24,128]{3,2,1,0:T(8,128)S(1)} %get-tuple-element.60), channel_id=1, source_target_pairs={{0,3},{1,2},{2,1},{3,0},{4,6},{5,7},{6,4},{7,5},{8,11},{9,10},{10,... | collective-permute-start | bytes 737288 | tf_op jit(solution)/shard_map/ppermute | solution.py:624
  19.9 1.2 %collective-permute-start.10 = (f32[5,4,24,128]{3,2,1,0:T(8,128)S(1)}, f32[5,4,24,128]{3,2,1,0:T(8,128)S(1)}, u32[]{:S(2)}, u32[]{:S(2)}) collective-permute-start(f32[5,4,24,128]{3,2,1,0:T(8,128)S(1)} %get-tuple-element.61), channel_id=1, source_target_pairs={{0,1},{1,0},{2,3},{3,2},{4,7},{5,6},{6,5},{7,4},{8,9},{9,8},{10,11... | collective-permute-start | bytes 737288 | tf_op jit(solution)/shard_map/ppermute | solution.py:624
  21.1 1.0 %shard_map.73 = f32[8,128]{1,0:T(8,128)S(1)} custom-call(f32[5,24,128]{2,1,0:T(8,128)S(1)} %get-tuple-element.56.refs_0_, f32[8,128]{1,0:T(8,128)S(1)} %get-tuple-element.49.refs_1_.refs_5_, f32[32,128]{1,0:T(8,128)S(1)} %collective-permute-done.left.refs_2_, f32[8,128]{1,0:T(8,128)S(1)} %collective-permute-done.2.refs_3_, ...), custom_call_target="tpu_custom_call" | custom-call | tf_op jit(solution)/shard_map/pallas_call | solution.py:505
  22.1 0.9 %collective-permute-start.5 = (f32[8,128]{1,0:T(8,128)S(1)}, f32[8,128]{1,0:T(8,128)S(1)}, u32[]{:S(2)}, u32[]{:S(2)}) collective-permute-start(f32[8,128]{1,0:T(8,128)S(1)} %shard_map.73), channel_id=1, source_target_pairs={{0,4},{4,0},{8,12},{12,8},{16,20},{20,16},{24,28},{28,24},{1,5},{5... | collective-permute-start | bytes 12296 | tf_op jit(solution)/shard_map/ppermute | solution.py:603
  22.9 0.8 %collective-permute-done.5 = f32[8,128]{1,0:T(8,128)S(1)} collective-permute-done((f32[8,128]{1,0:T(8,128)S(1)}, f32[8,128]{1,0:T(8,128)S(1)}, u32[]{:S(2)}, u32[]{:S(2)}) %collective-permute-start.5) | collective-permute-done | bytes 4128 | tf_op jit(solution)/shard_map/ppermute | solution.py:603
  23.8 2.4 %collective-permute-start.6 = (f32[8,128]{1,0:T(8,128)S(1)}, f32[8,128]{1,0:T(8,128)S(1)}, u32[]{:S(2)}, u32[]{:S(2)}) collective-permute-start(f32[8,128]{1,0:T(8,128)S(1)} %max.18), channel_id=1, source_target_pairs={{0,8},{4,12},{8,0},{12,4},{16,24},{20,28},{24,16},{28,20},{1,9},{5... | collective-permute-start | bytes 12296 | tf_op jit(solution)/shard_map/ppermute | solution.py:603
  26.1 1.6 %collective-permute-done.6 = f32[8,128]{1,0:T(8,128)S(1)} collective-permute-done((f32[8,128]{1,0:T(8,128)S(1)}, f32[8,128]{1,0:T(8,128)S(1)}, u32[]{:S(2)}, u32[]{:S(2)}) %collective-permute-start.6) | collective-permute-done | bytes 4128 | tf_op jit(solution)/shard_map/ppermute | solution.py:603
  27.7 1.2 %collective-permute-start.7 = (f32[8,128]{1,0:T(8,128)S(1)}, f32[8,128]{1,0:T(8,128)S(1)}, u32[]{:S(2)}, u32[]{:S(2)}) collective-permute-start(f32[8,128]{1,0:T(8,128)S(1)} %max.19), channel_id=1, source_target_pairs={{0,16},{4,20},{8,24},{12,28},{16,0},{20,4},{24,8},{28,12},{1,17},{... | collective-permute-start | bytes 12296 | tf_op jit(solution)/shard_map/ppermute | solution.py:603
  28.9 2.5 %collective-permute-done.7 = f32[8,128]{1,0:T(8,128)S(1)} collective-permute-done((f32[8,128]{1,0:T(8,128)S(1)}, f32[8,128]{1,0:T(8,128)S(1)}, u32[]{:S(2)}, u32[]{:S(2)}) %collective-permute-start.7) | collective-permute-done | bytes 4128 | tf_op jit(solution)/shard_map/ppermute | solution.py:603
  31.3 6.3 %collective-permute-done.8.refs_0_ = f32[5,4,24,128]{3,2,1,0:T(8,128)S(1)} collective-permute-done((f32[5,4,24,128]{3,2,1,0:T(8,128)S(1)}, f32[5,4,24,128]{3,2,1,0:T(8,128)S(1)}, u32[]{:S(2)}, u32[]{:S(2)}) %collective-permute-start.8) | collective-permute-done | bytes 245792 | tf_op jit(solution)/shard_map/ppermute | solution.py:624
  37.6 2.2 %collective-permute-start.13 = (f32[8,128]{1,0:T(8,128)S(1)}, f32[8,128]{1,0:T(8,128)S(1)}, u32[]{:S(2)}, u32[]{:S(2)}) collective-permute-start(f32[8,128]{1,0:T(8,128)S(1)} %max.20), channel_id=1, source_target_pairs={{0,3},{1,2},{2,1},{3,0},{4,7},{5,6},{6,5},{7,4},{8,11},{9,10},{10,... | collective-permute-start | bytes 12296 | tf_op jit(solution)/shard_map/ppermute | solution.py:603
  39.9 0.0 collective-permute-start.12
  39.9 2.1 %collective-permute-start.11 = (f32[8,128]{1,0:T(8,128)S(1)}, f32[8,128]{1,0:T(8,128)S(1)}, u32[]{:S(2)}, u32[]{:S(2)}) collective-permute-start(f32[8,128]{1,0:T(8,128)S(1)} %max.20), channel_id=1, source_target_pairs={{0,1},{1,0},{2,3},{3,2},{4,5},{5,4},{6,7},{7,6},{8,9},{9,8},{10,11... | collective-permute-start | bytes 12296 | tf_op jit(solution)/shard_map/ppermute | solution.py:603
  42.0 1.0 %collective-permute-done.13 = f32[8,128]{1,0:T(8,128)S(1)} collective-permute-done((f32[8,128]{1,0:T(8,128)S(1)}, f32[8,128]{1,0:T(8,128)S(1)}, u32[]{:S(2)}, u32[]{:S(2)}) %collective-permute-start.13) | collective-permute-done | bytes 4128 | tf_op jit(solution)/shard_map/ppermute | solution.py:603
  43.0 1.4 %collective-permute-done.12 = f32[8,128]{1,0:T(8,128)S(1)} collective-permute-done((f32[8,128]{1,0:T(8,128)S(1)}, f32[8,128]{1,0:T(8,128)S(1)}, u32[]{:S(2)}, u32[]{:S(2)}) %collective-permute-start.12) | collective-permute-done | bytes 4128 | tf_op jit(solution)/shard_map/ppermute | solution.py:603
  44.4 0.0 collective-permute-done.11
  44.4 0.0 collective-permute-done.9.refs_1_
  44.4 0.0 collective-permute-done.10.refs_2_
  44.4 1.4 %shard_map.74 = (f32[5,4,24,512]{3,2,1,0:T(8,128)}, f32[5,64]{1,0:T(8,128)}) custom-call(f32[5,4,24,128]{3,2,1,0:T(8,128)S(1)} %collective-permute-done.8.refs_0_, f32[5,4,24,128]{3,2,1,0:T(8,128)S(1)} %collective-permute-done.9.refs_1_, f32[5,4,24,128]{3,2,1,0:T(8,128)S(1)} %collective-permute-done.10.refs_2_, ...), custom_call_target="tpu_custom_call" | custom-call | tf_op jit(solution)/shard_map/pallas_call | solution.py:561
  (4 shorter events, 0.0 us)
Async XLA Ops:
  0.6 1.3 %copy-start = (s32[6,128]{1,0:T(8,128)S(1)}, s32[6,128]{1,0:T(8,128)}, u32[]{:S(2)}) copy-start(s32[6,128]{1,0:T(8,128)} %membership.1) | copy-start | bytes 9220
  0.6 1.3 %copy-start.1 = (s32[1,4]{1,0:T(1,128)S(1)}, s32[1,4]{1,0:T(1,128)}, u32[]{:S(2)}) copy-start(s32[1,4]{1,0:T(1,128)} %slots.1) | copy-start | bytes 52
  2.6 7.1 %collective-permute-start = (f32[32,128]{1,0:T(8,128)S(1)}, f32[32,128]{1,0:T(8,128)S(1)}, u32[]{:S(2)}, u32[]{:S(2)}) collective-permute-start(f32[32,128]{1,0:T(8,128)S(1)} %get-tuple-element.33), channel_id=1, source_target_pairs={{0,1},{1,2},{2,3},{3,0},{4,5},{5,6},{6,7},{7,4},{8,9},{9,10},{10,1... | collective-permute-start | bytes 49160 | tf_op jit(solution)/shard_map/ppermute | solution.py:612
  5.7 4.0 %collective-permute-start.1 = (f32[32,128]{1,0:T(8,128)S(1)}, f32[32,128]{1,0:T(8,128)S(1)}, u32[]{:S(2)}, u32[]{:S(2)}) collective-permute-start(f32[32,128]{1,0:T(8,128)S(1)} %get-tuple-element.34), channel_id=1, source_target_pairs={{0,3},{1,0},{2,1},{3,2},{4,7},{5,4},{6,5},{7,6},{8,11},{9,8},{10,9... | collective-permute-start | bytes 49160 | tf_op jit(solution)/shard_map/ppermute | solution.py:613
  7.7 4.5 %collective-permute-start.2 = (f32[8,128]{1,0:T(8,128)S(1)}, f32[8,128]{1,0:T(8,128)S(1)}, u32[]{:S(2)}, u32[]{:S(2)}) collective-permute-start(f32[8,128]{1,0:T(8,128)S(1)} %get-tuple-element.49.refs_1_.refs_5_), channel_id=1, source_target_pairs={{0,2},{1,3},{2,0},{3,1},{4,6},{5,7},{6,4},{7,5},{8,10},{9,11},{10,... | collective-permute-start | bytes 12296 | tf_op jit(solution)/shard_map/ppermute | solution.py:614
  12.2 4.4 %collective-permute-start.3 = (f32[88,128]{1,0:T(8,128)S(1)}, f32[88,128]{1,0:T(8,128)S(1)}, u32[]{:S(2)}, u32[]{:S(2)}) collective-permute-start(f32[88,128]{1,0:T(8,128)S(1)} %get-tuple-element.50), channel_id=1, source_target_pairs={{0,4},{4,8},{8,12},{12,16},{16,20},{20,24},{24,28},{28,0},{1,5},{5... | collective-permute-start | bytes 135176 | tf_op jit(solution)/shard_map/ppermute | solution.py:619
  12.3 4.4 %collective-permute-start.4 = (f32[88,128]{1,0:T(8,128)S(1)}, f32[88,128]{1,0:T(8,128)S(1)}, u32[]{:S(2)}, u32[]{:S(2)}) collective-permute-start(f32[88,128]{1,0:T(8,128)S(1)} %get-tuple-element.51), channel_id=1, source_target_pairs={{0,28},{4,0},{8,4},{12,8},{16,12},{20,16},{24,20},{28,24},{1,29},{... | collective-permute-start | bytes 135176 | tf_op jit(solution)/shard_map/ppermute | solution.py:620
  17.5 20.1 %collective-permute-start.8 = (f32[5,4,24,128]{3,2,1,0:T(8,128)S(1)}, f32[5,4,24,128]{3,2,1,0:T(8,128)S(1)}, u32[]{:S(2)}, u32[]{:S(2)}) collective-permute-start(f32[5,4,24,128]{3,2,1,0:T(8,128)S(1)} %get-tuple-element.58), channel_id=1, source_target_pairs={{0,2},{1,3},{2,0},{3,1},{4,5},{5,4},{6,7},{7,6},{8,10},{9,11},{10,... | collective-permute-start | bytes 737288 | tf_op jit(solution)/shard_map/ppermute | solution.py:624
  18.5 25.9 %collective-permute-start.9 = (f32[5,4,24,128]{3,2,1,0:T(8,128)S(1)}, f32[5,4,24,128]{3,2,1,0:T(8,128)S(1)}, u32[]{:S(2)}, u32[]{:S(2)}) collective-permute-start(f32[5,4,24,128]{3,2,1,0:T(8,128)S(1)} %get-tuple-element.60), channel_id=1, source_target_pairs={{0,3},{1,2},{2,1},{3,0},{4,6},{5,7},{6,4},{7,5},{8,11},{9,10},{10,... | collective-permute-start | bytes 737288 | tf_op jit(solution)/shard_map/ppermute | solution.py:624
  19.9 24.5 %collective-permute-start.10 = (f32[5,4,24,128]{3,2,1,0:T(8,128)S(1)}, f32[5,4,24,128]{3,2,1,0:T(8,128)S(1)}, u32[]{:S(2)}, u32[]{:S(2)}) collective-permute-start(f32[5,4,24,128]{3,2,1,0:T(8,128)S(1)} %get-tuple-element.61), channel_id=1, source_target_pairs={{0,1},{1,0},{2,3},{3,2},{4,7},{5,6},{6,5},{7,4},{8,9},{9,8},{10,11... | collective-permute-start | bytes 737288 | tf_op jit(solution)/shard_map/ppermute | solution.py:624
  22.1 1.7 %collective-permute-start.5 = (f32[8,128]{1,0:T(8,128)S(1)}, f32[8,128]{1,0:T(8,128)S(1)}, u32[]{:S(2)}, u32[]{:S(2)}) collective-permute-start(f32[8,128]{1,0:T(8,128)S(1)} %shard_map.73), channel_id=1, source_target_pairs={{0,4},{4,0},{8,12},{12,8},{16,20},{20,16},{24,28},{28,24},{1,5},{5... | collective-permute-start | bytes 12296 | tf_op jit(solution)/shard_map/ppermute | solution.py:603
  23.8 4.0 %collective-permute-start.6 = (f32[8,128]{1,0:T(8,128)S(1)}, f32[8,128]{1,0:T(8,128)S(1)}, u32[]{:S(2)}, u32[]{:S(2)}) collective-permute-start(f32[8,128]{1,0:T(8,128)S(1)} %max.18), channel_id=1, source_target_pairs={{0,8},{4,12},{8,0},{12,4},{16,24},{20,28},{24,16},{28,20},{1,9},{5... | collective-permute-start | bytes 12296 | tf_op jit(solution)/shard_map/ppermute | solution.py:603
  27.7 3.6 %collective-permute-start.7 = (f32[8,128]{1,0:T(8,128)S(1)}, f32[8,128]{1,0:T(8,128)S(1)}, u32[]{:S(2)}, u32[]{:S(2)}) collective-permute-start(f32[8,128]{1,0:T(8,128)S(1)} %max.19), channel_id=1, source_target_pairs={{0,16},{4,20},{8,24},{12,28},{16,0},{20,4},{24,8},{28,12},{1,17},{... | collective-permute-start | bytes 12296 | tf_op jit(solution)/shard_map/ppermute | solution.py:603
  37.6 5.4 %collective-permute-start.13 = (f32[8,128]{1,0:T(8,128)S(1)}, f32[8,128]{1,0:T(8,128)S(1)}, u32[]{:S(2)}, u32[]{:S(2)}) collective-permute-start(f32[8,128]{1,0:T(8,128)S(1)} %max.20), channel_id=1, source_target_pairs={{0,3},{1,2},{2,1},{3,0},{4,7},{5,6},{6,5},{7,4},{8,11},{9,10},{10,... | collective-permute-start | bytes 12296 | tf_op jit(solution)/shard_map/ppermute | solution.py:603
  39.9 4.5 %collective-permute-start.12 = (f32[8,128]{1,0:T(8,128)S(1)}, f32[8,128]{1,0:T(8,128)S(1)}, u32[]{:S(2)}, u32[]{:S(2)}) collective-permute-start(f32[8,128]{1,0:T(8,128)S(1)} %max.20), channel_id=1, source_target_pairs={{0,2},{1,3},{2,0},{3,1},{4,6},{5,7},{6,4},{7,5},{8,10},{9,11},{10,... | collective-permute-start | bytes 12296 | tf_op jit(solution)/shard_map/ppermute | solution.py:603
  39.9 4.5 %collective-permute-start.11 = (f32[8,128]{1,0:T(8,128)S(1)}, f32[8,128]{1,0:T(8,128)S(1)}, u32[]{:S(2)}, u32[]{:S(2)}) collective-permute-start(f32[8,128]{1,0:T(8,128)S(1)} %max.20), channel_id=1, source_target_pairs={{0,1},{1,0},{2,3},{3,2},{4,5},{5,4},{6,7},{7,6},{8,9},{9,8},{10,11... | collective-permute-start | bytes 12296 | tf_op jit(solution)/shard_map/ppermute | solution.py:603

commit v3 on v1

--- a/solution.py
+++ b/solution.py
@@ -189,6 +189,38 @@
     return jnp.maximum(peak, pltpu.roll(peak, 32, 1))
 
 
+def rounds_of(count):
+    if count == 4:
+        return [(None, 2), (2, 1), (3, 3), (1, None)]
+    return [(k, k) for k in range(1, count)]
+
+
+def arrivals_of(count):
+    if count == 4:
+        return [((0, 2), (3, 1)), ((1, 1), (1, 2)), ((2, 3), (2, 3))]
+    return [((k - 1, k), (k - 1, k)) for k in range(1, count)]
+
+
+def early_rounds(count):
+    return 1 if count == 4 else 0
+
+
+def is_inner(me, count):
+    return jnp.logical_and(me > 0, me < count - 1)
+
+
+def either(inner, outer, me, count):
+    return inner if inner == outer else jnp.where(is_inner(me, count), inner, outer)
+
+
+def leaving_for(me, i, count):
+    if i == len(rounds_of(count)):
+        return me
+    inner, outer = rounds_of(count)[i]
+    k = either(outer if inner is None else inner, inner if outer is None else outer, me, count)
+    return partner_of(me, k, count)
+
+
 def partner_of(me, k, count):
     if count & (count - 1) == 0:
         return me ^ k
@@ -263,7 +295,8 @@
 
 def brick_kernel(count, *refs):
     inside, down, up, columns, matrix = refs[:5]
-    outs, refs = refs[5 : 5 + count], refs[5 + count :]
+    number = len(rounds_of(count)) + 1
+    outs, refs = refs[5 : 5 + number], refs[5 + number :]
     blocks, rim_a, rim_d, rim_u, across, edges, split, coefficients, staged = refs
     total, y, width = inside.shape
     depth = total // FIELDS
@@ -307,17 +340,17 @@
 
     me = lax.axis_index("section")
     if rows % 8 == 0:
-        for k in range(count):
-            p = partner_of(me, k, count)
+        for i in range(number):
+            p = leaving_for(me, i, count)
             for j in range(total):
-                outs[k][j // depth, j % depth] = coefficients[j, pl.ds(pl.multiple_of(p * rows, 8), rows), :]
+                outs[i][j // depth, j % depth] = coefficients[j, pl.ds(pl.multiple_of(p * rows, 8), rows), :]
     else:
         for p in range(count):
             staged[p] = coefficients[:, p * rows : (p + 1) * rows, :]
-        for k in range(count):
-            p = partner_of(me, k, count)
+        for i in range(number):
+            p = leaving_for(me, i, count)
             for j in range(total):
-                outs[k][j // depth, j % depth] = staged[p, j]
+                outs[i][j // depth, j % depth] = staged[p, j]
 
 
 def transform_bricks(count, inside, down, up, columns, matrix):
@@ -325,12 +358,13 @@
     depth = total // FIELDS
     rows, tall = y // count, y + 2 * PAD
     chunk = array((FIELDS, depth, rows, width))
+    number = len(rounds_of(count)) + 1
     rim = array((total, 2 * PAD, width))
     results = pl.pallas_call(
         functools.partial(brick_kernel, count),
-        out_shape=[chunk] * count + [array((FIELDS, y // 4, width))] + [rim] * 3,
+        out_shape=[chunk] * number + [array((FIELDS, y // 4, width))] + [rim] * 3,
         in_specs=[vmem()] * 5,
-        out_specs=[vmem()] * (count + 4),
+        out_specs=[vmem()] * (number + 4),
         scratch_shapes=[
             pltpu.VMEM((total, tall, width), jnp.float32),
             pltpu.VMEM((2, FIELDS, y, width), jnp.float32),
@@ -341,17 +375,15 @@
         compiler_params=kernel_params(),
         cost_estimate=pl.CostEstimate(flops=80 * total * y * width, bytes_accessed=16 * total * y * width, transcendentals=0),
     )(inside, down, up, columns, matrix)
-    return results[:count], results[count], results[count + 1 :]
-
-
-def leaving_order(count):
-    return [*range(2, count), 1, 0]
+    return results[:number], results[number], results[number + 1 :]
 
 
 def mend_kernel(count, *refs):
-    chunks, refs = refs[:count], refs[count:]
+    early = early_rounds(count)
+    number = len(rounds_of(count)) + 1 - early
+    chunks, refs = refs[:number], refs[number:]
     top, bottom, blocks, rim_a, rim_d, rim_u, matrix = refs[:7]
-    outs, mended, refs = refs[7 : 7 + count], refs[7 + count], refs[8 + count :]
+    outs, mended, refs = refs[7 : 7 + number], refs[7 + number], refs[8 + number :]
     halo, columns, across, down, up, folded, split, result, fixed = refs
     fields, depth, rows, width = chunks[0].shape
     total = fields * depth
@@ -404,8 +436,8 @@
             mended[f, row : row + 1, :] = peak
 
     me = lax.axis_index("section")
-    for i, k in enumerate(leaving_order(count)):
-        p = partner_of(me, k, count)
+    for i in range(number):
+        p = leaving_for(me, i + early, count)
         for side, start in ((0, 0), (1, rows - 4)):
 
             @pl.when(p == side * (count - 1))
@@ -415,15 +447,16 @@
 
 
 def mend(count, chunks, top, bottom, blocks, rims, matrix):
+    number = len(chunks)
     fields, depth, rows, width = chunks[0].shape
     total = fields * depth
     tall = pltpu.VMEM((total, 4 * PAD, width), jnp.float32)
     results = pl.pallas_call(
         functools.partial(mend_kernel, count),
-        out_shape=[array(chunks[0].shape)] * count + [array(blocks.shape)],
-        in_specs=[vmem()] * (count + 7),
-        out_specs=[vmem()] * (count + 1),
-        input_output_aliases={k: k for k in range(count)},
+        out_shape=[array(chunks[0].shape)] * number + [array(blocks.shape)],
+        in_specs=[vmem()] * (number + 7),
+        out_specs=[vmem()] * (number + 1),
+        input_output_aliases={i: i for i in range(number)},
         scratch_shapes=[
             pltpu.VMEM((total, 2 * PAD, width), jnp.float32),
             pltpu.VMEM((2, 2 * PAD, width), jnp.float32),
@@ -436,8 +469,8 @@
             pltpu.VMEM((2, total, 4, width), jnp.float32),
         ],
         compiler_params=kernel_params(),
-    )(*[chunks[k] for k in leaving_order(count)], top, bottom, blocks, *rims, matrix)
-    return dict(zip(leaving_order(count), results)), results[count]
+    )(*chunks, top, bottom, blocks, *rims, matrix)
+    return results[:number], results[number]
 
 
 def group_kernel(count, groups, own_rows, *refs):
@@ -511,7 +544,8 @@
 
 
 def scale_kernel(count, groups, *refs):
-    chunks, refs = refs[:count], refs[count:]
+    number = len(rounds_of(count)) + 1
+    chunks, refs = refs[:number], refs[number:]
     peaks, labels, coded, group_peak, wide = refs
     fields, depth, rows, width = chunks[0].shape
     nb = rows // 4
@@ -525,8 +559,9 @@
         [jnp.broadcast_to(inverse[f : f + 1, g * LANES : (g + 1) * LANES], (8, LANES)) for g in range(high // LANES)]
         for f in range(fields)
     ]
-    for i, k in enumerate(leaving_order(count)):
-        slot = slot_of(labels, sender_of(me, k, count))
+    own_chunk = (number - 1, 0)
+    for i, (inner, outer) in enumerate([*arrivals_of(count), (own_chunk, own_chunk)]):
+        slot = slot_of(labels, sender_of(me, either(inner[1], outer[1], me, count), count))
         tile = own_labels
         if count > 4:
             tile = pltpu.roll(tile, lax.rem(LABEL_ROWS - lax.div(slot, 4) * nb, LABEL_ROWS), 0)
@@ -546,7 +581,10 @@
                 wide[i, f, pl.ds(m, nb, stride=4), :] = found[0:nb]
             factor = wide[i, f]
             for z in range(depth):
-                coded[f, z, :, place] = chunks[i][f, z] * factor
+                value = chunks[inner[0]][f, z]
+                if inner[0] != outer[0]:
+                    value = jnp.where(is_inner(me, count), value, chunks[outer[0]][f, z])
+                coded[f, z, :, place] = value * factor
 
 
 def scale(count, groups, chunks, peaks, labels):
@@ -554,7 +592,7 @@
     return pl.pallas_call(
         functools.partial(scale_kernel, count, groups),
         out_shape=[array((fields, depth, rows, width * count)), array((fields, groups))],
-        in_specs=[vmem()] * (count + 2),
+        in_specs=[vmem()] * (len(chunks) + 2),
         out_specs=[vmem()] * 2,
         scratch_shapes=[
             pltpu.VMEM((count, fields, rows, width), jnp.float32),
@@ -572,6 +610,16 @@
     if count & (count - 1) == 0:
         return [(i, i ^ k) for i in range(count)]
     return [(i, (i + k) % count) for i in range(count)]
+
+
+def round_pairs(count, i):
+    inner, outer = rounds_of(count)[i]
+    pairs = []
+    for a in range(count):
+        k = inner if 0 < a < count - 1 else outer
+        if k is not None:
+            pairs.append(exchange_pairs(count, k)[a])
+    return pairs
 
 
 def steps_over(axis):
@@ -604,16 +652,24 @@
     top = lax.ppermute(last_y, "sim", ring("sim", 1))
     bottom = lax.ppermute(first_y, "sim", ring("sim", -1))
     chunks, blocks, rims = transform_bricks(count, inside, down, up, columns, matrix)
-    chunks, blocks = mend(count, chunks, top, bottom, blocks, rims, matrix)
-    moved = {0: chunks[0]}
-    for k in leaving_order(count)[:-1]:
-        moved[k] = lax.ppermute(chunks[k], "section", exchange_pairs(count, k))
+    early = early_rounds(count)
+    moved = [lax.ppermute(chunks[i], "section", round_pairs(count, i)) for i in range(early)]
+    top = lax.ppermute(last_y, "sim", ring("sim", 1))
+    bottom = lax.ppermute(first_y, "sim", ring("sim", -1))
+    chunks, blocks = mend(count, chunks[early:], top, bottom, blocks, rims, matrix)
+    last = len(rounds_of(count)) - 1
+    for i in range(early, last):
+        moved.append(lax.ppermute(chunks[i - early], "section", round_pairs(count, i)))
     peaks = group_maxima(count, groups, membership.shape[0], blocks, [labels, left, *far, right])
-    for shift in steps_over("sim"):
+    for i, shift in enumerate(steps_over("sim")):
+        if i == 1:
+            peaks, leaving = lax.optimization_barrier((peaks, chunks[last - early]))
+            moved.append(lax.ppermute(leaving, "section", round_pairs(count, last)))
         peaks = with_others(peaks, "sim", [shift])
+    peaks, moved[0] = lax.optimization_barrier((peaks, moved[0]))
     for shift in steps_over("section"):
         peaks = with_others(peaks, "section", [shift])
-    return tuple(scale(count, groups, [moved[k] for k in leaving_order(count)], peaks, labels))
+    return tuple(scale(count, groups, [*moved, chunks[-1]], peaks, labels))
 
 
 def solution(mesh):

time: 44.4 us -> 48.3 us (1.088)
  starting transfers between devices: 17.3 us -> 19.7 us
  waiting for transfers between devices: 18.3 us -> 19.7 us
    ppermute x3 -> x4, starting transfers between devices: 3.55 us -> 5.63 us  [the longest x1 2.86 us: per_device(): lax.ppermute(chunks[i], 'section', round_pairs(count, i))]
    ppermute x5, waiting for transfers between devices: 15.8 us -> 17.2 us  [with_others(): lax.ppermute(value, axis, exchange_pairs(count, k))]
  transfers between devices with their start and end apart: 13 -> 14, of which waited for: 6 -> 5; matrix products, arithmetic and copies ran while one was open for 0% -> 0% of each run, Pallas kernels for 9% -> 10%
where the time goes in v3:
time: 48.3 us; the launch traced here: 48.1 us
  starting transfers between devices  19.7 us (41%)
  waiting for transfers between devices  19.7 us (41%)
  Pallas kernels  6.63 us (14%)
  other arithmetic  1.31 us (3%)
  between operations  0.77 us (2%)
    ppermute x5, waiting for transfers between devices, with_others(): lax.ppermute(value, axis, exchange_pairs(count, k))  17.2 us
    ppermute x5, starting transfers between devices, with_others(): lax.ppermute(value, axis, exchange_pairs(count, k))  5.32 us
    ppermute x1, starting transfers between devices, per_device(): left = lax.ppermute(last_x, 'section', ring('section', 1))  3.06 us
    ppermute x1, starting transfers between devices, per_device(): lax.ppermute(chunks[i], 'section', round_pairs(count, i))  2.86 us
    ppermute x1, starting transfers between devices, per_device(): bottom = lax.ppermute(first_y, 'sim', ring('sim', -1))  2.64 us
    ppermute x1, waiting for transfers between devices, per_device(): lax.ppermute(labels, 'section', ring('section', d))  2.49 us
    ppermute x1, starting transfers between devices, per_device(): right = lax.ppermute(first_x, 'section', ring('section', -1))  2.09 us
    pallas_call x1, Pallas kernels, transform_bricks(): pl.pallas_call(functools.partial(brick_kernel, count), out_shape=[chunk]...  1.79 us
  transfers between devices with their start and end apart: 14, of which 5 were waited for; matrix products, arithmetic and copies ran while one was open for 0% of the time, Pallas kernels for 10%

profile of v3, /device:TPU:0, one launch (start us, length us, event | category | flops | bytes accessed | tf_op | source)
XLA Modules:
  0.0 48.1 jit_solution(9042438304545999537)
XLA Ops:
  0.6 0.0 copy-start
  0.6 0.0 copy-start.1
  0.7 1.3 %pad_maximum_fusion.conserved = f32[5,4,96,128]{3,2,1,0:T(8,128)S(1)} fusion(f32[1,4,96,128]{3,2,1,0:T(8,128)} %bitcast.2, f32[3,4,96,128]{3,2,1,0:T(8,128)} %param.6, f32[1,4,96,128]{3,2,1,0:T(8,128)} %bitcast.3), kind=kLoop, calls=%fused_computation | loop fusion | flops 491520 | bytes 1966080 | tf_op jit(solution)/shard_map/concatenate | solution.py:643
  2.0 0.0 copy-done
  2.0 0.0 copy-done.1
  2.0 0.6 %shard_map.68 = (bf16[256,256]{1,0:T(8,128)(2,1)S(1)}, f32[32,128]{1,0:T(8,128)S(1)}, f32[32,128]{1,0:T(8,128)S(1)}, f32[8,128]{1,0:T(8,128)S(1)}) custom-call(f32[5,4,96,128]{3,2,1,0:T(8,128)S(1)} %pad_maximum_fusion.conserved, s32[6,128]{1,0:T(8,128)S(1)} %copy-done, s32[1,4]{1,0:T(1,128)S(1)} %copy-done.1), custom_call_target="tpu_custom_call" | custom-call | tf_op jit(solution)/shard_map/pallas_call | solution.py:114
  2.6 3.1 %collective-permute-start = (f32[32,128]{1,0:T(8,128)S(1)}, f32[32,128]{1,0:T(8,128)S(1)}, u32[]{:S(2)}, u32[]{:S(2)}) collective-permute-start(f32[32,128]{1,0:T(8,128)S(1)} %get-tuple-element.36), channel_id=1, source_target_pairs={{0,1},{1,2},{2,3},{3,0},{4,5},{5,6},{6,7},{7,4},{8,9},{9,10},{10,1... | collective-permute-start | bytes 49160 | tf_op jit(solution)/shard_map/ppermute | solution.py:645
  5.7 2.1 %collective-permute-start.1 = (f32[32,128]{1,0:T(8,128)S(1)}, f32[32,128]{1,0:T(8,128)S(1)}, u32[]{:S(2)}, u32[]{:S(2)}) collective-permute-start(f32[32,128]{1,0:T(8,128)S(1)} %get-tuple-element.37), channel_id=1, source_target_pairs={{0,3},{1,0},{2,1},{3,2},{4,7},{5,4},{6,5},{7,6},{8,11},{9,8},{10,9... | collective-permute-start | bytes 49160 | tf_op jit(solution)/shard_map/ppermute | solution.py:646
  7.7 0.9 %collective-permute-start.2 = (f32[8,128]{1,0:T(8,128)S(1)}, f32[8,128]{1,0:T(8,128)S(1)}, u32[]{:S(2)}, u32[]{:S(2)}) collective-permute-start(f32[8,128]{1,0:T(8,128)S(1)} %get-tuple-element.52.refs_1_.refs_6_), channel_id=1, source_target_pairs={{0,2},{1,3},{2,0},{3,1},{4,6},{5,7},{6,4},{7,5},{8,10},{9,11},{10,... | collective-permute-start | bytes 12296 | tf_op jit(solution)/shard_map/ppermute | solution.py:647
  8.7 0.9 %shard_map.69 = (f32[20,96,128]{2,1,0:T(8,128)S(1)}, f32[20,112,128]{2,1,0:T(8,128)S(1)}, f32[20,112,128]{2,1,0:T(8,128)S(1)}) custom-call(f32[5,4,96,128]{3,2,1,0:T(8,128)S(1)} %pad_maximum_fusion.conserved), custom_call_target="tpu_custom_call" | custom-call | flops 9830400 | bytes 3932160 | tf_op jit(solution)/shard_map/pallas_call | solution.py:258
  9.6 0.0 collective-permute-done.left.refs_2_
  9.7 0.0 collective-permute-done.1.right.refs_4_
  9.7 0.1 shard_map.70
  9.8 2.5 %collective-permute-done.2.refs_3_ = f32[8,128]{1,0:T(8,128)S(1)} collective-permute-done((f32[8,128]{1,0:T(8,128)S(1)}, f32[8,128]{1,0:T(8,128)S(1)}, u32[]{:S(2)}, u32[]{:S(2)}) %collective-permute-start.2) | collective-permute-done | bytes 4128 | tf_op jit(solution)/shard_map/ppermute | solution.py:647
  12.2 0.0 collective-permute-start.3
  12.3 2.6 %collective-permute-start.4 = (f32[88,128]{1,0:T(8,128)S(1)}, f32[88,128]{1,0:T(8,128)S(1)}, u32[]{:S(2)}, u32[]{:S(2)}) collective-permute-start(f32[88,128]{1,0:T(8,128)S(1)} %get-tuple-element.54), channel_id=1, source_target_pairs={{0,28},{4,0},{8,4},{12,8},{16,12},{20,16},{24,20},{28,24},{1,29},{... | collective-permute-start | bytes 135176 | tf_op jit(solution)/shard_map/ppermute | solution.py:658
  14.9 1.8 %shard_map.71 = (f32[5,4,24,128]{3,2,1,0:T(8,128)S(1)}, f32[5,4,24,128]{3,2,1,0:T(8,128)S(1)}, f32[5,4,24,128]{3,2,1,0:T(8,128)S(1)}, f32[5,4,24,128]{3,2,1,0:T(...) custom-call(f32[20,96,128]{2,1,0:T(8,128)S(1)} %get-tuple-element.39, ...), custom_call_target="tpu_custom_call" | custom-call | flops 19660800 | bytes 3932160 | tf_op jit(solution)/shard_map/pallas_call | solution.py:363
  16.7 2.9 %collective-permute-start.8 = (f32[5,4,24,128]{3,2,1,0:T(8,128)S(1)}, f32[5,4,24,128]{3,2,1,0:T(8,128)S(1)}, u32[]{:S(2)}, u32[]{:S(2)}) collective-permute-start(f32[5,4,24,128]{3,2,1,0:T(8,128)S(1)} %get-tuple-element.63), channel_id=1, source_target_pairs={{0,2},{3,1},{4,6},{7,5},{8,10},{11,9},{12,14},{15,13},{16,18},{19,... | collective-permute-start | bytes 737288 | tf_op jit(solution)/shard_map/ppermute | solution.py:656
  19.6 0.0 collective-permute-done.3.refs_4_
  19.6 0.0 collective-permute-done.4.refs_5_
  19.6 0.8 %shard_map.72 = (f32[5,4,24,128]{3,2,1,0:T(8,128)S(1)}, f32[5,4,24,128]{3,2,1,0:T(8,128)S(1)}, f32[5,4,24,128]{3,2,1,0:T(8,128)S(1)}, f32[5,4,24,128]{3,2,1,0:T(8,128)S(1)}, f32[5,24,128]{2,1,0:T(8,128)S(1)}) custom-call(f32[5,4,24,128]{3,2,1,0:T(8,128)S(1)} %get-tuple-element.46.refs_0_, ...), custom_call_target="tpu_custom_call", output_to_operand_aliasing={{0}: (0, {}), {1}: (1, {}), {2}: (2, {}), {3}: (3, {})} | custom-call | tf_op jit(solution)/shard_map/pallas_call | solution.py:454
  20.4 1.0 %shard_map.73 = f32[8,128]{1,0:T(8,128)S(1)} custom-call(f32[5,24,128]{2,1,0:T(8,128)S(1)} %get-tuple-element.59.refs_0_, f32[8,128]{1,0:T(8,128)S(1)} %get-tuple-element.52.refs_1_.refs_6_, f32[32,128]{1,0:T(8,128)S(1)} %collective-permute-done.left.refs_2_, f32[8,128]{1,0:T(8,128)S(1)} %collective-permute-done.2.refs_3_, ...), custom_call_target="tpu_custom_call" | custom-call | tf_op jit(solution)/shard_map/pallas_call | solution.py:531
  21.4 0.0 collective-permute-start.5
  21.4 0.1 collective-permute-start.9
  21.5 1.4 %collective-permute-start.10 = (f32[5,4,24,128]{3,2,1,0:T(8,128)S(1)}, f32[5,4,24,128]{3,2,1,0:T(8,128)S(1)}, u32[]{:S(2)}, u32[]{:S(2)}) collective-permute-start(f32[5,4,24,128]{3,2,1,0:T(8,128)S(1)} %get-tuple-element.66), channel_id=1, source_target_pairs={{0,3},{1,2},{2,1},{3,0},{4,7},{5,6},{6,5},{7,4},{8,11},{9,10},{10,... | collective-permute-start | bytes 737288 | tf_op jit(solution)/shard_map/ppermute | solution.py:662
  22.9 0.0 collective-permute-done.5
  22.9 1.3 %collective-permute-start.11 = (f32[5,4,24,128]{3,2,1,0:T(8,128)S(1)}, f32[5,4,24,128]{3,2,1,0:T(8,128)S(1)}, u32[]{:S(2)}, u32[]{:S(2)}) collective-permute-start(f32[5,4,24,128]{3,2,1,0:T(8,128)S(1)} %get-tuple-element.67), channel_id=1, source_target_pairs={{1,0},{2,3},{5,4},{6,7},{9,8},{10,11},{13,12},{14,15},{17,16},{18,... | collective-permute-start | bytes 737288 | tf_op jit(solution)/shard_map/ppermute | solution.py:667
  24.2 1.1 %collective-permute-start.6 = (f32[8,128]{1,0:T(8,128)S(1)}, f32[8,128]{1,0:T(8,128)S(1)}, u32[]{:S(2)}, u32[]{:S(2)}) collective-permute-start(f32[8,128]{1,0:T(8,128)S(1)} %max.15), channel_id=1, source_target_pairs={{0,8},{4,12},{8,0},{12,4},{16,24},{20,28},{24,16},{28,20},{1,9},{5... | collective-permute-start | bytes 12296 | tf_op jit(solution)/shard_map/ppermute | solution.py:636
  25.3 2.6 %collective-permute-done.6 = f32[8,128]{1,0:T(8,128)S(1)} collective-permute-done((f32[8,128]{1,0:T(8,128)S(1)}, f32[8,128]{1,0:T(8,128)S(1)}, u32[]{:S(2)}, u32[]{:S(2)}) %collective-permute-start.6) | collective-permute-done | bytes 4128 | tf_op jit(solution)/shard_map/ppermute | solution.py:636
  27.9 1.5 %collective-permute-start.7 = (f32[8,128]{1,0:T(8,128)S(1)}, f32[8,128]{1,0:T(8,128)S(1)}, u32[]{:S(2)}, u32[]{:S(2)}) collective-permute-start(f32[8,128]{1,0:T(8,128)S(1)} %max.16), channel_id=1, source_target_pairs={{0,16},{4,20},{8,24},{12,28},{16,0},{20,4},{24,8},{28,12},{1,17},{... | collective-permute-start | bytes 12296 | tf_op jit(solution)/shard_map/ppermute | solution.py:636
  29.4 2.1 %collective-permute-done.7 = f32[8,128]{1,0:T(8,128)S(1)} collective-permute-done((f32[8,128]{1,0:T(8,128)S(1)}, f32[8,128]{1,0:T(8,128)S(1)}, u32[]{:S(2)}, u32[]{:S(2)}) %collective-permute-start.7) | collective-permute-done | bytes 4128 | tf_op jit(solution)/shard_map/ppermute | solution.py:636
  31.5 0.0 collective-permute-done.8.refs_0_
  31.5 2.7 %collective-permute-start.12 = (f32[8,128]{1,0:T(8,128)S(1)}, f32[8,128]{1,0:T(8,128)S(1)}, u32[]{:S(2)}, u32[]{:S(2)}) collective-permute-start(f32[8,128]{1,0:T(8,128)S(1)} %max.17), channel_id=1, source_target_pairs={{0,1},{1,0},{2,3},{3,2},{4,5},{5,4},{6,7},{7,6},{8,9},{9,8},{10,11... | collective-permute-start | bytes 12296 | tf_op jit(solution)/shard_map/ppermute | solution.py:636
  34.2 8.0 %collective-permute-done.12 = f32[8,128]{1,0:T(8,128)S(1)} collective-permute-done((f32[8,128]{1,0:T(8,128)S(1)}, f32[8,128]{1,0:T(8,128)S(1)}, u32[]{:S(2)}, u32[]{:S(2)}) %collective-permute-start.12) | collective-permute-done | bytes 4128 | tf_op jit(solution)/shard_map/ppermute | solution.py:636
  42.2 0.0 collective-permute-start.13
  42.2 4.5 %collective-permute-done.13 = f32[8,128]{1,0:T(8,128)S(1)} collective-permute-done((f32[8,128]{1,0:T(8,128)S(1)}, f32[8,128]{1,0:T(8,128)S(1)}, u32[]{:S(2)}, u32[]{:S(2)}) %collective-permute-start.13) | collective-permute-done | bytes 4128 | tf_op jit(solution)/shard_map/ppermute | solution.py:636
  46.7 0.0 collective-permute-done.9.refs_1_
  46.7 0.0 collective-permute-done.10.refs_2_
  46.7 0.0 collective-permute-done.11.refs_3_
  46.7 1.4 %shard_map.74 = (f32[5,4,24,512]{3,2,1,0:T(8,128)}, f32[5,64]{1,0:T(8,128)}) custom-call(f32[5,4,24,128]{3,2,1,0:T(8,128)S(1)} %collective-permute-done.8.refs_0_, f32[5,4,24,128]{3,2,1,0:T(8,128)S(1)} %collective-permute-done.9.refs_1_, f32[5,4,24,128]{3,2,1,0:T(8,128)S(1)} %collective-permute-done.10.refs_2_, ...), custom_call_target="tpu_custom_call" | custom-call | tf_op jit(solution)/shard_map/pallas_call | solution.py:592
  (5 shorter events, 0.0 us)
Async XLA Ops:
  0.6 1.3 %copy-start = (s32[6,128]{1,0:T(8,128)S(1)}, s32[6,128]{1,0:T(8,128)}, u32[]{:S(2)}) copy-start(s32[6,128]{1,0:T(8,128)} %membership.1) | copy-start | bytes 9220
  0.6 1.3 %copy-start.1 = (s32[1,4]{1,0:T(1,128)S(1)}, s32[1,4]{1,0:T(1,128)}, u32[]{:S(2)}) copy-start(s32[1,4]{1,0:T(1,128)} %slots.1) | copy-start | bytes 52
  2.6 7.1 %collective-permute-start = (f32[32,128]{1,0:T(8,128)S(1)}, f32[32,128]{1,0:T(8,128)S(1)}, u32[]{:S(2)}, u32[]{:S(2)}) collective-permute-start(f32[32,128]{1,0:T(8,128)S(1)} %get-tuple-element.36), channel_id=1, source_target_pairs={{0,1},{1,2},{2,3},{3,0},{4,5},{5,6},{6,7},{7,4},{8,9},{9,10},{10,1... | collective-permute-start | bytes 49160 | tf_op jit(solution)/shard_map/ppermute | solution.py:645
  5.7 4.0 %collective-permute-start.1 = (f32[32,128]{1,0:T(8,128)S(1)}, f32[32,128]{1,0:T(8,128)S(1)}, u32[]{:S(2)}, u32[]{:S(2)}) collective-permute-start(f32[32,128]{1,0:T(8,128)S(1)} %get-tuple-element.37), channel_id=1, source_target_pairs={{0,3},{1,0},{2,1},{3,2},{4,7},{5,4},{6,5},{7,6},{8,11},{9,8},{10,9... | collective-permute-start | bytes 49160 | tf_op jit(solution)/shard_map/ppermute | solution.py:646
  7.7 4.5 %collective-permute-start.2 = (f32[8,128]{1,0:T(8,128)S(1)}, f32[8,128]{1,0:T(8,128)S(1)}, u32[]{:S(2)}, u32[]{:S(2)}) collective-permute-start(f32[8,128]{1,0:T(8,128)S(1)} %get-tuple-element.52.refs_1_.refs_6_), channel_id=1, source_target_pairs={{0,2},{1,3},{2,0},{3,1},{4,6},{5,7},{6,4},{7,5},{8,10},{9,11},{10,... | collective-permute-start | bytes 12296 | tf_op jit(solution)/shard_map/ppermute | solution.py:647
  12.2 7.3 %collective-permute-start.3 = (f32[88,128]{1,0:T(8,128)S(1)}, f32[88,128]{1,0:T(8,128)S(1)}, u32[]{:S(2)}, u32[]{:S(2)}) collective-permute-start(f32[88,128]{1,0:T(8,128)S(1)} %get-tuple-element.53), channel_id=1, source_target_pairs={{0,4},{4,8},{8,12},{12,16},{16,20},{20,24},{24,28},{28,0},{1,5},{5... | collective-permute-start | bytes 135176 | tf_op jit(solution)/shard_map/ppermute | solution.py:657
  12.3 7.3 %collective-permute-start.4 = (f32[88,128]{1,0:T(8,128)S(1)}, f32[88,128]{1,0:T(8,128)S(1)}, u32[]{:S(2)}, u32[]{:S(2)}) collective-permute-start(f32[88,128]{1,0:T(8,128)S(1)} %get-tuple-element.54), channel_id=1, source_target_pairs={{0,28},{4,0},{8,4},{12,8},{16,12},{20,16},{24,20},{28,24},{1,29},{... | collective-permute-start | bytes 135176 | tf_op jit(solution)/shard_map/ppermute | solution.py:658
  16.7 14.8 %collective-permute-start.8 = (f32[5,4,24,128]{3,2,1,0:T(8,128)S(1)}, f32[5,4,24,128]{3,2,1,0:T(8,128)S(1)}, u32[]{:S(2)}, u32[]{:S(2)}) collective-permute-start(f32[5,4,24,128]{3,2,1,0:T(8,128)S(1)} %get-tuple-element.63), channel_id=1, source_target_pairs={{0,2},{3,1},{4,6},{7,5},{8,10},{11,9},{12,14},{15,13},{16,18},{19,... | collective-permute-start | bytes 737288 | tf_op jit(solution)/shard_map/ppermute | solution.py:656
  21.4 1.6 %collective-permute-start.5 = (f32[8,128]{1,0:T(8,128)S(1)}, f32[8,128]{1,0:T(8,128)S(1)}, u32[]{:S(2)}, u32[]{:S(2)}) collective-permute-start(f32[8,128]{1,0:T(8,128)S(1)} %shard_map.73), channel_id=1, source_target_pairs={{0,4},{4,0},{8,12},{12,8},{16,20},{20,16},{24,28},{28,24},{1,5},{5... | collective-permute-start | bytes 12296 | tf_op jit(solution)/shard_map/ppermute | solution.py:636
  21.4 25.3 %collective-permute-start.9 = (f32[5,4,24,128]{3,2,1,0:T(8,128)S(1)}, f32[5,4,24,128]{3,2,1,0:T(8,128)S(1)}, u32[]{:S(2)}, u32[]{:S(2)}) collective-permute-start(f32[5,4,24,128]{3,2,1,0:T(8,128)S(1)} %get-tuple-element.65), channel_id=1, source_target_pairs={{0,1},{1,3},{2,0},{3,2},{4,5},{5,7},{6,4},{7,6},{8,9},{9,11},{10,8... | collective-permute-start | bytes 737288 | tf_op jit(solution)/shard_map/ppermute | solution.py:662
  21.5 25.2 %collective-permute-start.10 = (f32[5,4,24,128]{3,2,1,0:T(8,128)S(1)}, f32[5,4,24,128]{3,2,1,0:T(8,128)S(1)}, u32[]{:S(2)}, u32[]{:S(2)}) collective-permute-start(f32[5,4,24,128]{3,2,1,0:T(8,128)S(1)} %get-tuple-element.66), channel_id=1, source_target_pairs={{0,3},{1,2},{2,1},{3,0},{4,7},{5,6},{6,5},{7,4},{8,11},{9,10},{10,... | collective-permute-start | bytes 737288 | tf_op jit(solution)/shard_map/ppermute | solution.py:662
  22.9 23.8 %collective-permute-start.11 = (f32[5,4,24,128]{3,2,1,0:T(8,128)S(1)}, f32[5,4,24,128]{3,2,1,0:T(8,128)S(1)}, u32[]{:S(2)}, u32[]{:S(2)}) collective-permute-start(f32[5,4,24,128]{3,2,1,0:T(8,128)S(1)} %get-tuple-element.67), channel_id=1, source_target_pairs={{1,0},{2,3},{5,4},{6,7},{9,8},{10,11},{13,12},{14,15},{17,16},{18,... | collective-permute-start | bytes 737288 | tf_op jit(solution)/shard_map/ppermute | solution.py:667
  24.2 3.7 %collective-permute-start.6 = (f32[8,128]{1,0:T(8,128)S(1)}, f32[8,128]{1,0:T(8,128)S(1)}, u32[]{:S(2)}, u32[]{:S(2)}) collective-permute-start(f32[8,128]{1,0:T(8,128)S(1)} %max.15), channel_id=1, source_target_pairs={{0,8},{4,12},{8,0},{12,4},{16,24},{20,28},{24,16},{28,20},{1,9},{5... | collective-permute-start | bytes 12296 | tf_op jit(solution)/shard_map/ppermute | solution.py:636
  27.9 3.6 %collective-permute-start.7 = (f32[8,128]{1,0:T(8,128)S(1)}, f32[8,128]{1,0:T(8,128)S(1)}, u32[]{:S(2)}, u32[]{:S(2)}) collective-permute-start(f32[8,128]{1,0:T(8,128)S(1)} %max.16), channel_id=1, source_target_pairs={{0,16},{4,20},{8,24},{12,28},{16,0},{20,4},{24,8},{28,12},{1,17},{... | collective-permute-start | bytes 12296 | tf_op jit(solution)/shard_map/ppermute | solution.py:636
  31.5 10.6 %collective-permute-start.12 = (f32[8,128]{1,0:T(8,128)S(1)}, f32[8,128]{1,0:T(8,128)S(1)}, u32[]{:S(2)}, u32[]{:S(2)}) collective-permute-start(f32[8,128]{1,0:T(8,128)S(1)} %max.17), channel_id=1, source_target_pairs={{0,1},{1,0},{2,3},{3,2},{4,5},{5,4},{6,7},{7,6},{8,9},{9,8},{10,11... | collective-permute-start | bytes 12296 | tf_op jit(solution)/shard_map/ppermute | solution.py:636
  42.2 4.5 %collective-permute-start.13 = (f32[8,128]{1,0:T(8,128)S(1)}, f32[8,128]{1,0:T(8,128)S(1)}, u32[]{:S(2)}, u32[]{:S(2)}) collective-permute-start(f32[8,128]{1,0:T(8,128)S(1)} %max.18), channel_id=1, source_target_pairs={{0,2},{1,3},{2,0},{3,1},{4,6},{5,7},{6,4},{7,5},{8,10},{9,11},{10,... | collective-permute-start | bytes 12296 | tf_op jit(solution)/shard_map/ppermute | solution.py:636

commit v4 on v1

--- a/solution.py
+++ b/solution.py
@@ -77,7 +77,7 @@
     return jax.ShapeDtypeStruct(shape, dtype)
 
 
-def pack_kernel(conserved, membership, slots, matrix, first_x, last_x, labels):
+def pack_kernel(conserved, membership, slots, first_x, last_x, labels):
     fields, depth, y, width = conserved.shape
     quarter = y // 4
     lane = lanes_of((y, width))
@@ -100,13 +100,11 @@
             packed = packed + pltpu.roll(column[c * quarter : (c + 1) * quarter], 32 * c, 1)
         out[0:quarter, :] = packed
         out[quarter:, :] = own
-    write_matrix(matrix, width)
 
 
 def pack(conserved, membership, slots):
     y, width = conserved.shape[2:]
     shapes = [
-        array((2 * width, 2 * width), jnp.bfloat16),
         array((y // 4 + LABEL_ROWS, width)),
         array((y // 4 + LABEL_ROWS, width)),
         array((LABEL_ROWS, width)),
@@ -115,7 +113,7 @@
         pack_kernel,
         out_shape=shapes,
         in_specs=[vmem()] * 3,
-        out_specs=[vmem()] * 4,
+        out_specs=[vmem()] * 3,
         compiler_params=kernel_params(),
     )(conserved, membership, slots)
 
@@ -201,8 +199,9 @@
     return lax.rem(me - k + count, count)
 
 
-def flux_kernel(conserved, across, down, up):
+def flux_kernel(conserved, across, down, up, matrix):
     fields, depth, y, width = conserved.shape
+    write_matrix(matrix, width)
     step = 16
 
     def flux_rows(i, carry):
@@ -225,9 +224,9 @@
     tall = array((total, y + 2 * PAD, width))
     return pl.pallas_call(
         flux_kernel,
-        out_shape=[array((total, y, width)), tall, tall],
+        out_shape=[array((total, y, width)), tall, tall, array((2 * width, 2 * width), jnp.bfloat16)],
         in_specs=[vmem()],
-        out_specs=[vmem()] * 3,
+        out_specs=[vmem()] * 4,
         compiler_params=kernel_params(),
         cost_estimate=pl.CostEstimate(flops=40 * total * y * width, bytes_accessed=16 * total * y * width, transcendentals=0),
     )(conserved)
@@ -512,7 +511,7 @@
 
 def scale_kernel(count, groups, *refs):
     chunks, refs = refs[:count], refs[count:]
-    peaks, labels, coded, group_peak, wide = refs
+    peaks, labels, coded, group_peak, done, wide, sems = refs
     fields, depth, rows, width = chunks[0].shape
     nb = rows // 4
     high = peaks.shape[1]
@@ -521,43 +520,52 @@
     own_labels = labels[...].astype(jnp.int32)
     lane = lanes_of((8, LANES))
     inverse = 1.0 / (peaks[...] + EPSILON)
-    tables = [
-        [jnp.broadcast_to(inverse[f : f + 1, g * LANES : (g + 1) * LANES], (8, LANES)) for g in range(high // LANES)]
-        for f in range(fields)
-    ]
-    for i, k in enumerate(leaving_order(count)):
+    places, owns = [], []
+    for k in leaving_order(count):
         slot = slot_of(labels, sender_of(me, k, count))
         tile = own_labels
         if count > 4:
             tile = pltpu.roll(tile, lax.rem(LABEL_ROWS - lax.div(slot, 4) * nb, LABEL_ROWS), 0)
         within = lax.rem(slot, 4) * 32 + lax.rem(lane, 32)
-        own = jnp.take_along_axis(tile, within, axis=1)
-        place = pl.ds(pl.multiple_of(slot * width, width), width)
-        for f in range(fields):
+        owns.append(jnp.take_along_axis(tile, within, axis=1))
+        places.append(pl.ds(pl.multiple_of(slot * width, width), width))
+    copies = []
+    for f in range(fields):
+        tables = [
+            jnp.broadcast_to(inverse[f : f + 1, g * LANES : (g + 1) * LANES], (8, LANES)) for g in range(high // LANES)
+        ]
+        for i in range(count):
             if high == LANES:
-                found = jnp.take_along_axis(tables[f][0], own, axis=1)
+                found = jnp.take_along_axis(tables[0], owns[i], axis=1)
             else:
                 found = jnp.zeros((8, LANES), jnp.float32)
-                inside = lax.rem(own, LANES)
+                inside = lax.rem(owns[i], LANES)
                 for g in range(high // LANES):
-                    here = jnp.take_along_axis(tables[f][g], inside, axis=1)
-                    found = jnp.where(lax.div(own, LANES) == g, here, found)
+                    here = jnp.take_along_axis(tables[g], inside, axis=1)
+                    found = jnp.where(lax.div(owns[i], LANES) == g, here, found)
             for m in range(4):
                 wide[i, f, pl.ds(m, nb, stride=4), :] = found[0:nb]
             factor = wide[i, f]
             for z in range(depth):
-                coded[f, z, :, place] = chunks[i][f, z] * factor
+                done[f, z, :, places[i]] = chunks[i][f, z] * factor
+        copies.append(pltpu.make_async_copy(done.at[f], coded.at[f], sems.at[f]))
+        copies[-1].start()
+    for copy in copies:
+        copy.wait()
 
 
 def scale(count, groups, chunks, peaks, labels):
     fields, depth, rows, width = chunks[0].shape
+    whole = (fields, depth, rows, width * count)
     return pl.pallas_call(
         functools.partial(scale_kernel, count, groups),
-        out_shape=[array((fields, depth, rows, width * count)), array((fields, groups))],
+        out_shape=[array(whole), array((fields, groups))],
         in_specs=[vmem()] * (count + 2),
-        out_specs=[vmem()] * 2,
+        out_specs=[pl.BlockSpec(memory_space=pl.ANY), vmem()],
         scratch_shapes=[
+            pltpu.VMEM(whole, jnp.float32),
             pltpu.VMEM((count, fields, rows, width), jnp.float32),
+            pltpu.SemaphoreType.DMA((fields,)),
         ],
         compiler_params=kernel_params(),
     )(*chunks, peaks, labels)
@@ -593,17 +601,17 @@
     count = lax.axis_size("section")
     groups = 2 * lax.axis_size("sim") * count
     conserved = jnp.concatenate([density[None], momentum, energy[None]], axis=0)
-    matrix, first_x, last_x, labels = pack(conserved, membership, slot_of_brick)
+    first_x, last_x, labels = pack(conserved, membership, slot_of_brick)
     left = lax.ppermute(last_x, "section", ring("section", 1))
     right = lax.ppermute(first_x, "section", ring("section", -1))
     far = [lax.ppermute(labels, "section", ring("section", d)) for d in range(2, count - 1)]
-    inside, down, up = own_fluxes(conserved)
+    inside, down, up, matrix = own_fluxes(conserved)
     left, right, inside = lax.optimization_barrier((left, right, inside))
     first_y, last_y, columns = edge_rows(conserved, left, right)
-    first_y, last_y, *far = lax.optimization_barrier((first_y, last_y, *far))
     top = lax.ppermute(last_y, "sim", ring("sim", 1))
     bottom = lax.ppermute(first_y, "sim", ring("sim", -1))
     chunks, blocks, rims = transform_bricks(count, inside, down, up, columns, matrix)
+    blocks, *far = lax.optimization_barrier((blocks, *far))
     chunks, blocks = mend(count, chunks, top, bottom, blocks, rims, matrix)
     moved = {0: chunks[0]}
     for k in leaving_order(count)[:-1]:

time: 44.4 us -> 43.2 us (0.973)
  waiting for transfers between devices: 18.3 us -> 14 us
  starting transfers between devices: 17.3 us -> 19.9 us
  Pallas kernels: 6.62 us -> 7.16 us
    ppermute x5, waiting for transfers between devices: 15.8 us -> 12.8 us  [with_others(): lax.ppermute(value, axis, exchange_pairs(count, k))]
    ppermute x1, waiting for transfers between devices: 2.49 us -> 0.3 us  [per_device(): lax.ppermute(labels, 'section', ring('section', d))]
    ppermute x1, starting transfers between devices: 0.95 us -> 2.41 us  [per_device(): lax.ppermute(labels, 'section', ring('section', d))]
    ppermute x3, starting transfers between devices: 3.55 us -> 4.35 us  [per_device(): moved[k] = lax.ppermute(chunks[k], 'section', exchange_pairs(count, k))]
    ppermute x1, waiting for transfers between devices: 0.01 us -> 0.77 us  [per_device(): left = lax.ppermute(last_x, 'section', ring('section', 1))]
    pallas_call x1, Pallas kernels: 1.38 us -> 1.88 us  [scale(): pl.pallas_call(functools.partial(scale_kernel, count, groups), out_shape=...]
  transfers between devices with their start and end apart: 13 -> 13, of which waited for: 6 -> 8; matrix products, arithmetic and copies ran while one was open for 0% -> 0% of each run, Pallas kernels for 9% -> 9%
where the time goes in v4:
time: 43.2 us; the launch traced here: 43.1 us
  starting transfers between devices  19.9 us (46%)
  waiting for transfers between devices  14 us (32%)
  Pallas kernels  7.16 us (17%)
  other arithmetic  1.31 us (3%)
  between operations  0.73 us (2%)
    ppermute x5, waiting for transfers between devices, with_others(): lax.ppermute(value, axis, exchange_pairs(count, k))  12.8 us
    ppermute x5, starting transfers between devices, with_others(): lax.ppermute(value, axis, exchange_pairs(count, k))  5.3 us
    ppermute x3, starting transfers between devices, per_device(): moved[k] = lax.ppermute(chunks[k], 'section', exchange_pairs(count, k))  4.35 us
    ppermute x1, starting transfers between devices, per_device(): left = lax.ppermute(last_x, 'section', ring('section', 1))  3.06 us
    ppermute x1, starting transfers between devices, per_device(): bottom = lax.ppermute(first_y, 'sim', ring('sim', -1))  2.63 us
    ppermute x1, starting transfers between devices, per_device(): lax.ppermute(labels, 'section', ring('section', d))  2.41 us
    ppermute x1, starting transfers between devices, per_device(): right = lax.ppermute(first_x, 'section', ring('section', -1))  2.09 us
    pallas_call x1, Pallas kernels, scale(): pl.pallas_call(functools.partial(scale_kernel, count, groups), out_shape=...  1.88 us
  transfers between devices with their start and end apart: 13, of which 8 were waited for; matrix products, arithmetic and copies ran while one was open for 0% of the time, Pallas kernels for 9%

profile of v4, /device:TPU:0, one launch (start us, length us, event | category | flops | bytes accessed | tf_op | source)
XLA Modules:
  0.0 43.1 jit_solution(10508387634298112513)
XLA Ops:
  0.6 0.0 copy-start
  0.6 0.0 copy-start.1
  0.7 1.3 %pad_maximum_fusion.conserved = f32[5,4,96,128]{3,2,1,0:T(8,128)S(1)} fusion(f32[1,4,96,128]{3,2,1,0:T(8,128)} %bitcast.2, f32[3,4,96,128]{3,2,1,0:T(8,128)} %param.6, f32[1,4,96,128]{3,2,1,0:T(8,128)} %bitcast.3), kind=kLoop, calls=%fused_computation | loop fusion | flops 491520 | bytes 1966080 | tf_op jit(solution)/shard_map/concatenate | solution.py:603
  2.0 0.0 copy-done
  2.0 0.0 copy-done.1
  2.0 0.6 %shard_map.68 = (f32[32,128]{1,0:T(8,128)S(1)}, f32[32,128]{1,0:T(8,128)S(1)}, f32[8,128]{1,0:T(8,128)S(1)}) custom-call(f32[5,4,96,128]{3,2,1,0:T(8,128)S(1)} %pad_maximum_fusion.conserved, s32[6,128]{1,0:T(8,128)S(1)} %copy-done, s32[1,4]{1,0:T(1,128)S(1)} %copy-done.1), custom_call_target="tpu_custom_call" | custom-call | tf_op jit(solution)/shard_map/pallas_call | solution.py:112
  2.6 3.1 %collective-permute-start = (f32[32,128]{1,0:T(8,128)S(1)}, f32[32,128]{1,0:T(8,128)S(1)}, u32[]{:S(2)}, u32[]{:S(2)}) collective-permute-start(f32[32,128]{1,0:T(8,128)S(1)} %get-tuple-element.30), channel_id=1, source_target_pairs={{0,1},{1,2},{2,3},{3,0},{4,5},{5,6},{6,7},{7,4},{8,9},{9,10},{10,1... | collective-permute-start | bytes 49160 | tf_op jit(solution)/shard_map/ppermute | solution.py:605
  5.7 2.1 %collective-permute-start.1 = (f32[32,128]{1,0:T(8,128)S(1)}, f32[32,128]{1,0:T(8,128)S(1)}, u32[]{:S(2)}, u32[]{:S(2)}) collective-permute-start(f32[32,128]{1,0:T(8,128)S(1)} %get-tuple-element.31), channel_id=1, source_target_pairs={{0,3},{1,0},{2,1},{3,2},{4,7},{5,4},{6,5},{7,6},{8,11},{9,8},{10,9... | collective-permute-start | bytes 49160 | tf_op jit(solution)/shard_map/ppermute | solution.py:606
  7.7 1.0 %shard_map.69 = (f32[20,96,128]{2,1,0:T(8,128)S(1)}, f32[20,112,128]{2,1,0:T(8,128)S(1)}, f32[20,112,128]{2,1,0:T(8,128)S(1)}, bf16[256,256]{1,0:T(8,128)(2,1)S(1)}) custom-call(f32[5,4,96,128]{3,2,1,0:T(8,128)S(1)} %pad_maximum_fusion.conserved), custom_call_target="tpu_custom_call" | custom-call | flops 9830400 | bytes 3932160 | tf_op jit(solution)/shard_map/pallas_call | solution.py:225
  8.7 0.8 %collective-permute-done.left.refs_2_ = f32[32,128]{1,0:T(8,128)S(1)} collective-permute-done((f32[32,128]{1,0:T(8,128)S(1)}, f32[32,128]{1,0:T(8,128)S(1)}, u32[]{:S(2)}, u32[]{:S(2)}) %collective-permute-start) | collective-permute-done | bytes 16416 | tf_op jit(solution)/shard_map/ppermute | solution.py:605
  9.5 0.1 collective-permute-done.1.right.refs_4_
  9.6 0.1 shard_map.70
  9.7 0.1 collective-permute-start.2
  9.7 2.6 %collective-permute-start.3 = (f32[88,128]{1,0:T(8,128)S(1)}, f32[88,128]{1,0:T(8,128)S(1)}, u32[]{:S(2)}, u32[]{:S(2)}) collective-permute-start(f32[88,128]{1,0:T(8,128)S(1)} %get-tuple-element.45), channel_id=1, source_target_pairs={{0,28},{4,0},{8,4},{12,8},{16,12},{20,16},{24,20},{28,24},{1,29},{... | collective-permute-start | bytes 135176 | tf_op jit(solution)/shard_map/ppermute | solution.py:612
  12.4 2.4 %collective-permute-start.4 = (f32[8,128]{1,0:T(8,128)S(1)}, f32[8,128]{1,0:T(8,128)S(1)}, u32[]{:S(2)}, u32[]{:S(2)}) collective-permute-start(f32[8,128]{1,0:T(8,128)S(1)} %get-tuple-element.47.refs_1_.refs_5_), channel_id=1, source_target_pairs={{0,2},{1,3},{2,0},{3,1},{4,6},{5,7},{6,4},{7,5},{8,10},{9,11},{10,... | collective-permute-start | bytes 12296 | tf_op jit(solution)/shard_map/ppermute | solution.py:607
  14.8 1.8 %shard_map.71 = (f32[5,4,24,128]{3,2,1,0:T(8,128)S(1)}, f32[5,4,24,128]{3,2,1,0:T(8,128)S(1)}, f32[5,4,24,128]{3,2,1,0:T(8,128)S(1)}, f32[5,4,24,128]{3,2,1,0:T(...) custom-call(f32[20,96,128]{2,1,0:T(8,128)S(1)} %get-tuple-element.33, ...), custom_call_target="tpu_custom_call" | custom-call | flops 19660800 | bytes 3932160 | tf_op jit(solution)/shard_map/pallas_call | solution.py:328
  16.6 0.3 collective-permute-done.4.refs_3_
  16.9 0.0 collective-permute-done.2.refs_4_
  16.9 0.0 collective-permute-done.3.refs_5_
  16.9 0.8 %shard_map.72 = (f32[5,4,24,128]{3,2,1,0:T(8,128)S(1)}, f32[5,4,24,128]{3,2,1,0:T(8,128)S(1)}, f32[5,4,24,128]{3,2,1,0:T(8,128)S(1)}, f32[5,4,24,128]{3,2,1,0:T(8,128)S(1)}, f32[5,24,128]{2,1,0:T(8,128)S(1)}) custom-call(f32[5,4,24,128]{3,2,1,0:T(8,128)S(1)} %get-tuple-element.40.refs_0_, ...), custom_call_target="tpu_custom_call", output_to_operand_aliasing={{0}: (0, {}), {1}: (1, {}), {2}: (2, {}), {3}: (3, {})} | custom-call | tf_op jit(solution)/shard_map/pallas_call | solution.py:420
  17.7 2.5 %collective-permute-start.5 = (f32[5,4,24,128]{3,2,1,0:T(8,128)S(1)}, f32[5,4,24,128]{3,2,1,0:T(8,128)S(1)}, u32[]{:S(2)}, u32[]{:S(2)}) collective-permute-start(f32[5,4,24,128]{3,2,1,0:T(8,128)S(1)} %get-tuple-element.52), channel_id=1, source_target_pairs={{0,2},{1,3},{2,0},{3,1},{4,6},{5,7},{6,4},{7,5},{8,10},{9,11},{10,... | collective-permute-start | bytes 737288 | tf_op jit(solution)/shard_map/ppermute | solution.py:618
  20.2 1.6 %collective-permute-start.6 = (f32[5,4,24,128]{3,2,1,0:T(8,128)S(1)}, f32[5,4,24,128]{3,2,1,0:T(8,128)S(1)}, u32[]{:S(2)}, u32[]{:S(2)}) collective-permute-start(f32[5,4,24,128]{3,2,1,0:T(8,128)S(1)} %get-tuple-element.53), channel_id=1, source_target_pairs={{0,3},{1,2},{2,1},{3,0},{4,7},{5,6},{6,5},{7,4},{8,11},{9,10},{10,... | collective-permute-start | bytes 737288 | tf_op jit(solution)/shard_map/ppermute | solution.py:618
  21.7 0.3 collective-permute-start.7
  22.0 1.0 %shard_map.73 = f32[8,128]{1,0:T(8,128)S(1)} custom-call(f32[5,24,128]{2,1,0:T(8,128)S(1)} %get-tuple-element.56.refs_0_, f32[8,128]{1,0:T(8,128)S(1)} %get-tuple-element.47.refs_1_.refs_5_, f32[32,128]{1,0:T(8,128)S(1)} %collective-permute-done.left.refs_2_, f32[8,128]{1,0:T(8,128)S(1)} %collective-permute-done.4.refs_3_, ...), custom_call_target="tpu_custom_call" | custom-call | tf_op jit(solution)/shard_map/pallas_call | solution.py:497
  23.0 0.0 collective-permute-start.8
  23.1 1.2 %collective-permute-done.8 = f32[8,128]{1,0:T(8,128)S(1)} collective-permute-done((f32[8,128]{1,0:T(8,128)S(1)}, f32[8,128]{1,0:T(8,128)S(1)}, u32[]{:S(2)}, u32[]{:S(2)}) %collective-permute-start.8) | collective-permute-done | bytes 4128 | tf_op jit(solution)/shard_map/ppermute | solution.py:596
  24.2 0.7 %collective-permute-start.9 = (f32[8,128]{1,0:T(8,128)S(1)}, f32[8,128]{1,0:T(8,128)S(1)}, u32[]{:S(2)}, u32[]{:S(2)}) collective-permute-start(f32[8,128]{1,0:T(8,128)S(1)} %max.15), channel_id=1, source_target_pairs={{0,8},{4,12},{8,0},{12,4},{16,24},{20,28},{24,16},{28,20},{1,9},{5... | collective-permute-start | bytes 12296 | tf_op jit(solution)/shard_map/ppermute | solution.py:596
  25.0 2.9 %collective-permute-done.9 = f32[8,128]{1,0:T(8,128)S(1)} collective-permute-done((f32[8,128]{1,0:T(8,128)S(1)}, f32[8,128]{1,0:T(8,128)S(1)}, u32[]{:S(2)}, u32[]{:S(2)}) %collective-permute-start.9) | collective-permute-done | bytes 4128 | tf_op jit(solution)/shard_map/ppermute | solution.py:596
  27.8 1.7 %collective-permute-start.10 = (f32[8,128]{1,0:T(8,128)S(1)}, f32[8,128]{1,0:T(8,128)S(1)}, u32[]{:S(2)}, u32[]{:S(2)}) collective-permute-start(f32[8,128]{1,0:T(8,128)S(1)} %max.16), channel_id=1, source_target_pairs={{0,16},{4,20},{8,24},{12,28},{16,0},{20,4},{24,8},{28,12},{1,17},{... | collective-permute-start | bytes 12296 | tf_op jit(solution)/shard_map/ppermute | solution.py:596
  29.5 1.9 %collective-permute-done.10 = f32[8,128]{1,0:T(8,128)S(1)} collective-permute-done((f32[8,128]{1,0:T(8,128)S(1)}, f32[8,128]{1,0:T(8,128)S(1)}, u32[]{:S(2)}, u32[]{:S(2)}) %collective-permute-start.10) | collective-permute-done | bytes 4128 | tf_op jit(solution)/shard_map/ppermute | solution.py:596
  31.4 1.7 %collective-permute-start.11 = (f32[8,128]{1,0:T(8,128)S(1)}, f32[8,128]{1,0:T(8,128)S(1)}, u32[]{:S(2)}, u32[]{:S(2)}) collective-permute-start(f32[8,128]{1,0:T(8,128)S(1)} %max.17), channel_id=1, source_target_pairs={{0,1},{1,0},{2,3},{3,2},{4,5},{5,4},{6,7},{7,6},{8,9},{9,8},{10,11... | collective-permute-start | bytes 12296 | tf_op jit(solution)/shard_map/ppermute | solution.py:596
  33.1 3.5 %collective-permute-done.11 = f32[8,128]{1,0:T(8,128)S(1)} collective-permute-done((f32[8,128]{1,0:T(8,128)S(1)}, f32[8,128]{1,0:T(8,128)S(1)}, u32[]{:S(2)}, u32[]{:S(2)}) %collective-permute-start.11) | collective-permute-done | bytes 4128 | tf_op jit(solution)/shard_map/ppermute | solution.py:596
  36.7 1.1 %collective-permute-start.12 = (f32[8,128]{1,0:T(8,128)S(1)}, f32[8,128]{1,0:T(8,128)S(1)}, u32[]{:S(2)}, u32[]{:S(2)}) collective-permute-start(f32[8,128]{1,0:T(8,128)S(1)} %max.18), channel_id=1, source_target_pairs={{0,2},{1,3},{2,0},{3,1},{4,6},{5,7},{6,4},{7,5},{8,10},{9,11},{10,... | collective-permute-start | bytes 12296 | tf_op jit(solution)/shard_map/ppermute | solution.py:596
  37.8 3.4 %collective-permute-done.12 = f32[8,128]{1,0:T(8,128)S(1)} collective-permute-done((f32[8,128]{1,0:T(8,128)S(1)}, f32[8,128]{1,0:T(8,128)S(1)}, u32[]{:S(2)}, u32[]{:S(2)}) %collective-permute-start.12) | collective-permute-done | bytes 4128 | tf_op jit(solution)/shard_map/ppermute | solution.py:596
  41.2 0.0 collective-permute-done.5.refs_0_
  41.2 0.0 collective-permute-done.6.refs_1_
  41.2 0.0 collective-permute-done.7.refs_2_
  41.2 1.9 %shard_map.74 = (f32[5,4,24,512]{3,2,1,0:T(8,128)}, f32[5,64]{1,0:T(8,128)}) custom-call(f32[5,4,24,128]{3,2,1,0:T(8,128)S(1)} %collective-permute-done.5.refs_0_, f32[5,4,24,128]{3,2,1,0:T(8,128)S(1)} %collective-permute-done.6.refs_1_, f32[5,4,24,128]{3,2,1,0:T(8,128)S(1)} %collective-permute-done.7.refs_2_, ...), custom_call_target="tpu_custom_call" | custom-call | tf_op jit(solution)/shard_map/pallas_call | solution.py:560
  (5 shorter events, 0.0 us)
Async XLA Ops:
  0.6 1.3 %copy-start = (s32[6,128]{1,0:T(8,128)S(1)}, s32[6,128]{1,0:T(8,128)}, u32[]{:S(2)}) copy-start(s32[6,128]{1,0:T(8,128)} %membership.1) | copy-start | bytes 9220
  0.6 1.3 %copy-start.1 = (s32[1,4]{1,0:T(1,128)S(1)}, s32[1,4]{1,0:T(1,128)}, u32[]{:S(2)}) copy-start(s32[1,4]{1,0:T(1,128)} %slots.1) | copy-start | bytes 52
  2.6 6.9 %collective-permute-start = (f32[32,128]{1,0:T(8,128)S(1)}, f32[32,128]{1,0:T(8,128)S(1)}, u32[]{:S(2)}, u32[]{:S(2)}) collective-permute-start(f32[32,128]{1,0:T(8,128)S(1)} %get-tuple-element.30), channel_id=1, source_target_pairs={{0,1},{1,2},{2,3},{3,0},{4,5},{5,6},{6,7},{7,4},{8,9},{9,10},{10,1... | collective-permute-start | bytes 49160 | tf_op jit(solution)/shard_map/ppermute | solution.py:605
  5.7 3.9 %collective-permute-start.1 = (f32[32,128]{1,0:T(8,128)S(1)}, f32[32,128]{1,0:T(8,128)S(1)}, u32[]{:S(2)}, u32[]{:S(2)}) collective-permute-start(f32[32,128]{1,0:T(8,128)S(1)} %get-tuple-element.31), channel_id=1, source_target_pairs={{0,3},{1,0},{2,1},{3,2},{4,7},{5,4},{6,5},{7,6},{8,11},{9,8},{10,9... | collective-permute-start | bytes 49160 | tf_op jit(solution)/shard_map/ppermute | solution.py:606
  9.7 7.2 %collective-permute-start.2 = (f32[88,128]{1,0:T(8,128)S(1)}, f32[88,128]{1,0:T(8,128)S(1)}, u32[]{:S(2)}, u32[]{:S(2)}) collective-permute-start(f32[88,128]{1,0:T(8,128)S(1)} %get-tuple-element.44), channel_id=1, source_target_pairs={{0,4},{4,8},{8,12},{12,16},{16,20},{20,24},{24,28},{28,0},{1,5},{5... | collective-permute-start | bytes 135176 | tf_op jit(solution)/shard_map/ppermute | solution.py:611
  9.7 7.1 %collective-permute-start.3 = (f32[88,128]{1,0:T(8,128)S(1)}, f32[88,128]{1,0:T(8,128)S(1)}, u32[]{:S(2)}, u32[]{:S(2)}) collective-permute-start(f32[88,128]{1,0:T(8,128)S(1)} %get-tuple-element.45), channel_id=1, source_target_pairs={{0,28},{4,0},{8,4},{12,8},{16,12},{20,16},{24,20},{28,24},{1,29},{... | collective-permute-start | bytes 135176 | tf_op jit(solution)/shard_map/ppermute | solution.py:612
  12.4 4.5 %collective-permute-start.4 = (f32[8,128]{1,0:T(8,128)S(1)}, f32[8,128]{1,0:T(8,128)S(1)}, u32[]{:S(2)}, u32[]{:S(2)}) collective-permute-start(f32[8,128]{1,0:T(8,128)S(1)} %get-tuple-element.47.refs_1_.refs_5_), channel_id=1, source_target_pairs={{0,2},{1,3},{2,0},{3,1},{4,6},{5,7},{6,4},{7,5},{8,10},{9,11},{10,... | collective-permute-start | bytes 12296 | tf_op jit(solution)/shard_map/ppermute | solution.py:607
  17.7 23.5 %collective-permute-start.5 = (f32[5,4,24,128]{3,2,1,0:T(8,128)S(1)}, f32[5,4,24,128]{3,2,1,0:T(8,128)S(1)}, u32[]{:S(2)}, u32[]{:S(2)}) collective-permute-start(f32[5,4,24,128]{3,2,1,0:T(8,128)S(1)} %get-tuple-element.52), channel_id=1, source_target_pairs={{0,2},{1,3},{2,0},{3,1},{4,6},{5,7},{6,4},{7,5},{8,10},{9,11},{10,... | collective-permute-start | bytes 737288 | tf_op jit(solution)/shard_map/ppermute | solution.py:618
  20.2 21.0 %collective-permute-start.6 = (f32[5,4,24,128]{3,2,1,0:T(8,128)S(1)}, f32[5,4,24,128]{3,2,1,0:T(8,128)S(1)}, u32[]{:S(2)}, u32[]{:S(2)}) collective-permute-start(f32[5,4,24,128]{3,2,1,0:T(8,128)S(1)} %get-tuple-element.53), channel_id=1, source_target_pairs={{0,3},{1,2},{2,1},{3,0},{4,7},{5,6},{6,5},{7,4},{8,11},{9,10},{10,... | collective-permute-start | bytes 737288 | tf_op jit(solution)/shard_map/ppermute | solution.py:618
  21.7 19.5 %collective-permute-start.7 = (f32[5,4,24,128]{3,2,1,0:T(8,128)S(1)}, f32[5,4,24,128]{3,2,1,0:T(8,128)S(1)}, u32[]{:S(2)}, u32[]{:S(2)}) collective-permute-start(f32[5,4,24,128]{3,2,1,0:T(8,128)S(1)} %get-tuple-element.54), channel_id=1, source_target_pairs={{0,1},{1,0},{2,3},{3,2},{4,5},{5,4},{6,7},{7,6},{8,9},{9,8},{10,11... | collective-permute-start | bytes 737288 | tf_op jit(solution)/shard_map/ppermute | solution.py:618
  23.0 1.2 %collective-permute-start.8 = (f32[8,128]{1,0:T(8,128)S(1)}, f32[8,128]{1,0:T(8,128)S(1)}, u32[]{:S(2)}, u32[]{:S(2)}) collective-permute-start(f32[8,128]{1,0:T(8,128)S(1)} %shard_map.73), channel_id=1, source_target_pairs={{0,4},{4,0},{8,12},{12,8},{16,20},{20,16},{24,28},{28,24},{1,5},{5... | collective-permute-start | bytes 12296 | tf_op jit(solution)/shard_map/ppermute | solution.py:596
  24.2 3.6 %collective-permute-start.9 = (f32[8,128]{1,0:T(8,128)S(1)}, f32[8,128]{1,0:T(8,128)S(1)}, u32[]{:S(2)}, u32[]{:S(2)}) collective-permute-start(f32[8,128]{1,0:T(8,128)S(1)} %max.15), channel_id=1, source_target_pairs={{0,8},{4,12},{8,0},{12,4},{16,24},{20,28},{24,16},{28,20},{1,9},{5... | collective-permute-start | bytes 12296 | tf_op jit(solution)/shard_map/ppermute | solution.py:596
  27.8 3.6 %collective-permute-start.10 = (f32[8,128]{1,0:T(8,128)S(1)}, f32[8,128]{1,0:T(8,128)S(1)}, u32[]{:S(2)}, u32[]{:S(2)}) collective-permute-start(f32[8,128]{1,0:T(8,128)S(1)} %max.16), channel_id=1, source_target_pairs={{0,16},{4,20},{8,24},{12,28},{16,0},{20,4},{24,8},{28,12},{1,17},{... | collective-permute-start | bytes 12296 | tf_op jit(solution)/shard_map/ppermute | solution.py:596
  31.4 5.2 %collective-permute-start.11 = (f32[8,128]{1,0:T(8,128)S(1)}, f32[8,128]{1,0:T(8,128)S(1)}, u32[]{:S(2)}, u32[]{:S(2)}) collective-permute-start(f32[8,128]{1,0:T(8,128)S(1)} %max.17), channel_id=1, source_target_pairs={{0,1},{1,0},{2,3},{3,2},{4,5},{5,4},{6,7},{7,6},{8,9},{9,8},{10,11... | collective-permute-start | bytes 12296 | tf_op jit(solution)/shard_map/ppermute | solution.py:596
  36.7 4.5 %collective-permute-start.12 = (f32[8,128]{1,0:T(8,128)S(1)}, f32[8,128]{1,0:T(8,128)S(1)}, u32[]{:S(2)}, u32[]{:S(2)}) collective-permute-start(f32[8,128]{1,0:T(8,128)S(1)} %max.18), channel_id=1, source_target_pairs={{0,2},{1,3},{2,0},{3,1},{4,6},{5,7},{6,4},{7,5},{8,10},{9,11},{10,... | collective-permute-start | bytes 12296 | tf_op jit(solution)/shard_map/ppermute | solution.py:596

commit v5 on v1

--- a/solution.py
+++ b/solution.py
@@ -77,7 +77,7 @@
     return jax.ShapeDtypeStruct(shape, dtype)
 
 
-def pack_kernel(conserved, membership, slots, matrix, first_x, last_x, labels):
+def pack_kernel(conserved, membership, slots, first_x, last_x, labels):
     fields, depth, y, width = conserved.shape
     quarter = y // 4
     lane = lanes_of((y, width))
@@ -100,13 +100,11 @@
             packed = packed + pltpu.roll(column[c * quarter : (c + 1) * quarter], 32 * c, 1)
         out[0:quarter, :] = packed
         out[quarter:, :] = own
-    write_matrix(matrix, width)
 
 
 def pack(conserved, membership, slots):
     y, width = conserved.shape[2:]
     shapes = [
-        array((2 * width, 2 * width), jnp.bfloat16),
         array((y // 4 + LABEL_ROWS, width)),
         array((y // 4 + LABEL_ROWS, width)),
         array((LABEL_ROWS, width)),
@@ -115,7 +113,7 @@
         pack_kernel,
         out_shape=shapes,
         in_specs=[vmem()] * 3,
-        out_specs=[vmem()] * 4,
+        out_specs=[vmem()] * 3,
         compiler_params=kernel_params(),
     )(conserved, membership, slots)
 
@@ -201,8 +199,9 @@
     return lax.rem(me - k + count, count)
 
 
-def flux_kernel(conserved, across, down, up):
+def flux_kernel(conserved, across, down, up, matrix):
     fields, depth, y, width = conserved.shape
+    write_matrix(matrix, width)
     step = 16
 
     def flux_rows(i, carry):
@@ -225,9 +224,9 @@
     tall = array((total, y + 2 * PAD, width))
     return pl.pallas_call(
         flux_kernel,
-        out_shape=[array((total, y, width)), tall, tall],
+        out_shape=[array((total, y, width)), tall, tall, array((2 * width, 2 * width), jnp.bfloat16)],
         in_specs=[vmem()],
-        out_specs=[vmem()] * 3,
+        out_specs=[vmem()] * 4,
         compiler_params=kernel_params(),
         cost_estimate=pl.CostEstimate(flops=40 * total * y * width, bytes_accessed=16 * total * y * width, transcendentals=0),
     )(conserved)
@@ -593,17 +592,17 @@
     count = lax.axis_size("section")
     groups = 2 * lax.axis_size("sim") * count
     conserved = jnp.concatenate([density[None], momentum, energy[None]], axis=0)
-    matrix, first_x, last_x, labels = pack(conserved, membership, slot_of_brick)
+    first_x, last_x, labels = pack(conserved, membership, slot_of_brick)
     left = lax.ppermute(last_x, "section", ring("section", 1))
     right = lax.ppermute(first_x, "section", ring("section", -1))
     far = [lax.ppermute(labels, "section", ring("section", d)) for d in range(2, count - 1)]
-    inside, down, up = own_fluxes(conserved)
+    inside, down, up, matrix = own_fluxes(conserved)
     left, right, inside = lax.optimization_barrier((left, right, inside))
     first_y, last_y, columns = edge_rows(conserved, left, right)
-    first_y, last_y, *far = lax.optimization_barrier((first_y, last_y, *far))
     top = lax.ppermute(last_y, "sim", ring("sim", 1))
     bottom = lax.ppermute(first_y, "sim", ring("sim", -1))
     chunks, blocks, rims = transform_bricks(count, inside, down, up, columns, matrix)
+    blocks, *far = lax.optimization_barrier((blocks, *far))
     chunks, blocks = mend(count, chunks, top, bottom, blocks, rims, matrix)
     moved = {0: chunks[0]}
     for k in leaving_order(count)[:-1]:

time: 44.4 us -> 42.7 us (0.962)
  waiting for transfers between devices: 18.3 us -> 14 us
  starting transfers between devices: 17.3 us -> 19.9 us
    ppermute x5, waiting for transfers between devices: 15.8 us -> 12.8 us  [with_others(): lax.ppermute(value, axis, exchange_pairs(count, k))]
    ppermute x1, waiting for transfers between devices: 2.49 us -> 0.3 us  [per_device(): lax.ppermute(labels, 'section', ring('section', d))]
    ppermute x1, starting transfers between devices: 0.95 us -> 2.41 us  [per_device(): lax.ppermute(labels, 'section', ring('section', d))]
    ppermute x3, starting transfers between devices: 3.55 us -> 4.35 us  [per_device(): moved[k] = lax.ppermute(chunks[k], 'section', exchange_pairs(count, k))]
    ppermute x1, waiting for transfers between devices: 0.01 us -> 0.77 us  [per_device(): left = lax.ppermute(last_x, 'section', ring('section', 1))]
  transfers between devices with their start and end apart: 13 -> 13, of which waited for: 6 -> 8; matrix products, arithmetic and copies ran while one was open for 0% -> 0% of each run, Pallas kernels for 9% -> 9%
where the time goes in v5:
time: 42.7 us; the launch traced here: 42.6 us
  starting transfers between devices  19.9 us (47%)
  waiting for transfers between devices  14 us (33%)
  Pallas kernels  6.65 us (16%)
  other arithmetic  1.31 us (3%)
  between operations  0.73 us (2%)
    ppermute x5, waiting for transfers between devices, with_others(): lax.ppermute(value, axis, exchange_pairs(count, k))  12.8 us
    ppermute x5, starting transfers between devices, with_others(): lax.ppermute(value, axis, exchange_pairs(count, k))  5.3 us
    ppermute x3, starting transfers between devices, per_device(): moved[k] = lax.ppermute(chunks[k], 'section', exchange_pairs(count, k))  4.35 us
    ppermute x1, starting transfers between devices, per_device(): left = lax.ppermute(last_x, 'section', ring('section', 1))  3.06 us
    ppermute x1, starting transfers between devices, per_device(): bottom = lax.ppermute(first_y, 'sim', ring('sim', -1))  2.63 us
    ppermute x1, starting transfers between devices, per_device(): lax.ppermute(labels, 'section', ring('section', d))  2.41 us
    ppermute x1, starting transfers between devices, per_device(): right = lax.ppermute(first_x, 'section', ring('section', -1))  2.09 us
    pallas_call x1, Pallas kernels, transform_bricks(): pl.pallas_call(functools.partial(brick_kernel, count), out_shape=[chunk]...  1.79 us
  transfers between devices with their start and end apart: 13, of which 8 were waited for; matrix products, arithmetic and copies ran while one was open for 0% of the time, Pallas kernels for 9%

profile of v5, /device:TPU:0, one launch (start us, length us, event | category | flops | bytes accessed | tf_op | source)
XLA Modules:
  0.0 42.6 jit_solution(12531767162208120022)
XLA Ops:
  0.6 0.0 copy-start
  0.6 0.0 copy-start.1
  0.7 1.3 %pad_maximum_fusion.conserved = f32[5,4,96,128]{3,2,1,0:T(8,128)S(1)} fusion(f32[1,4,96,128]{3,2,1,0:T(8,128)} %bitcast.2, f32[3,4,96,128]{3,2,1,0:T(8,128)} %param.6, f32[1,4,96,128]{3,2,1,0:T(8,128)} %bitcast.3), kind=kLoop, calls=%fused_computation | loop fusion | flops 491520 | bytes 1966080 | tf_op jit(solution)/shard_map/concatenate | solution.py:594
  2.0 0.0 copy-done
  2.0 0.0 copy-done.1
  2.0 0.6 %shard_map.68 = (f32[32,128]{1,0:T(8,128)S(1)}, f32[32,128]{1,0:T(8,128)S(1)}, f32[8,128]{1,0:T(8,128)S(1)}) custom-call(f32[5,4,96,128]{3,2,1,0:T(8,128)S(1)} %pad_maximum_fusion.conserved, s32[6,128]{1,0:T(8,128)S(1)} %copy-done, s32[1,4]{1,0:T(1,128)S(1)} %copy-done.1), custom_call_target="tpu_custom_call" | custom-call | tf_op jit(solution)/shard_map/pallas_call | solution.py:112
  2.6 3.1 %collective-permute-start = (f32[32,128]{1,0:T(8,128)S(1)}, f32[32,128]{1,0:T(8,128)S(1)}, u32[]{:S(2)}, u32[]{:S(2)}) collective-permute-start(f32[32,128]{1,0:T(8,128)S(1)} %get-tuple-element.30), channel_id=1, source_target_pairs={{0,1},{1,2},{2,3},{3,0},{4,5},{5,6},{6,7},{7,4},{8,9},{9,10},{10,1... | collective-permute-start | bytes 49160 | tf_op jit(solution)/shard_map/ppermute | solution.py:596
  5.7 2.1 %collective-permute-start.1 = (f32[32,128]{1,0:T(8,128)S(1)}, f32[32,128]{1,0:T(8,128)S(1)}, u32[]{:S(2)}, u32[]{:S(2)}) collective-permute-start(f32[32,128]{1,0:T(8,128)S(1)} %get-tuple-element.31), channel_id=1, source_target_pairs={{0,3},{1,0},{2,1},{3,2},{4,7},{5,4},{6,5},{7,6},{8,11},{9,8},{10,9... | collective-permute-start | bytes 49160 | tf_op jit(solution)/shard_map/ppermute | solution.py:597
  7.7 1.0 %shard_map.69 = (f32[20,96,128]{2,1,0:T(8,128)S(1)}, f32[20,112,128]{2,1,0:T(8,128)S(1)}, f32[20,112,128]{2,1,0:T(8,128)S(1)}, bf16[256,256]{1,0:T(8,128)(2,1)S(1)}) custom-call(f32[5,4,96,128]{3,2,1,0:T(8,128)S(1)} %pad_maximum_fusion.conserved), custom_call_target="tpu_custom_call" | custom-call | flops 9830400 | bytes 3932160 | tf_op jit(solution)/shard_map/pallas_call | solution.py:225
  8.7 0.8 %collective-permute-done.left.refs_2_ = f32[32,128]{1,0:T(8,128)S(1)} collective-permute-done((f32[32,128]{1,0:T(8,128)S(1)}, f32[32,128]{1,0:T(8,128)S(1)}, u32[]{:S(2)}, u32[]{:S(2)}) %collective-permute-start) | collective-permute-done | bytes 16416 | tf_op jit(solution)/shard_map/ppermute | solution.py:596
  9.5 0.1 collective-permute-done.1.right.refs_4_
  9.6 0.1 shard_map.70
  9.7 0.1 collective-permute-start.2
  9.7 2.6 %collective-permute-start.3 = (f32[88,128]{1,0:T(8,128)S(1)}, f32[88,128]{1,0:T(8,128)S(1)}, u32[]{:S(2)}, u32[]{:S(2)}) collective-permute-start(f32[88,128]{1,0:T(8,128)S(1)} %get-tuple-element.45), channel_id=1, source_target_pairs={{0,28},{4,0},{8,4},{12,8},{16,12},{20,16},{24,20},{28,24},{1,29},{... | collective-permute-start | bytes 135176 | tf_op jit(solution)/shard_map/ppermute | solution.py:603
  12.4 2.4 %collective-permute-start.4 = (f32[8,128]{1,0:T(8,128)S(1)}, f32[8,128]{1,0:T(8,128)S(1)}, u32[]{:S(2)}, u32[]{:S(2)}) collective-permute-start(f32[8,128]{1,0:T(8,128)S(1)} %get-tuple-element.47.refs_1_.refs_5_), channel_id=1, source_target_pairs={{0,2},{1,3},{2,0},{3,1},{4,6},{5,7},{6,4},{7,5},{8,10},{9,11},{10,... | collective-permute-start | bytes 12296 | tf_op jit(solution)/shard_map/ppermute | solution.py:598
  14.8 1.8 %shard_map.71 = (f32[5,4,24,128]{3,2,1,0:T(8,128)S(1)}, f32[5,4,24,128]{3,2,1,0:T(8,128)S(1)}, f32[5,4,24,128]{3,2,1,0:T(8,128)S(1)}, f32[5,4,24,128]{3,2,1,0:T(...) custom-call(f32[20,96,128]{2,1,0:T(8,128)S(1)} %get-tuple-element.33, ...), custom_call_target="tpu_custom_call" | custom-call | flops 19660800 | bytes 3932160 | tf_op jit(solution)/shard_map/pallas_call | solution.py:328
  16.6 0.3 collective-permute-done.4.refs_3_
  16.9 0.0 collective-permute-done.2.refs_4_
  16.9 0.0 collective-permute-done.3.refs_5_
  16.9 0.8 %shard_map.72 = (f32[5,4,24,128]{3,2,1,0:T(8,128)S(1)}, f32[5,4,24,128]{3,2,1,0:T(8,128)S(1)}, f32[5,4,24,128]{3,2,1,0:T(8,128)S(1)}, f32[5,4,24,128]{3,2,1,0:T(8,128)S(1)}, f32[5,24,128]{2,1,0:T(8,128)S(1)}) custom-call(f32[5,4,24,128]{3,2,1,0:T(8,128)S(1)} %get-tuple-element.40.refs_0_, ...), custom_call_target="tpu_custom_call", output_to_operand_aliasing={{0}: (0, {}), {1}: (1, {}), {2}: (2, {}), {3}: (3, {})} | custom-call | tf_op jit(solution)/shard_map/pallas_call | solution.py:420
  17.7 2.5 %collective-permute-start.5 = (f32[5,4,24,128]{3,2,1,0:T(8,128)S(1)}, f32[5,4,24,128]{3,2,1,0:T(8,128)S(1)}, u32[]{:S(2)}, u32[]{:S(2)}) collective-permute-start(f32[5,4,24,128]{3,2,1,0:T(8,128)S(1)} %get-tuple-element.52), channel_id=1, source_target_pairs={{0,2},{1,3},{2,0},{3,1},{4,6},{5,7},{6,4},{7,5},{8,10},{9,11},{10,... | collective-permute-start | bytes 737288 | tf_op jit(solution)/shard_map/ppermute | solution.py:609
  20.2 1.6 %collective-permute-start.6 = (f32[5,4,24,128]{3,2,1,0:T(8,128)S(1)}, f32[5,4,24,128]{3,2,1,0:T(8,128)S(1)}, u32[]{:S(2)}, u32[]{:S(2)}) collective-permute-start(f32[5,4,24,128]{3,2,1,0:T(8,128)S(1)} %get-tuple-element.53), channel_id=1, source_target_pairs={{0,3},{1,2},{2,1},{3,0},{4,7},{5,6},{6,5},{7,4},{8,11},{9,10},{10,... | collective-permute-start | bytes 737288 | tf_op jit(solution)/shard_map/ppermute | solution.py:609
  21.7 0.3 collective-permute-start.7
  22.0 1.0 %shard_map.73 = f32[8,128]{1,0:T(8,128)S(1)} custom-call(f32[5,24,128]{2,1,0:T(8,128)S(1)} %get-tuple-element.56.refs_0_, f32[8,128]{1,0:T(8,128)S(1)} %get-tuple-element.47.refs_1_.refs_5_, f32[32,128]{1,0:T(8,128)S(1)} %collective-permute-done.left.refs_2_, f32[8,128]{1,0:T(8,128)S(1)} %collective-permute-done.4.refs_3_, ...), custom_call_target="tpu_custom_call" | custom-call | tf_op jit(solution)/shard_map/pallas_call | solution.py:497
  23.0 0.0 collective-permute-start.8
  23.1 1.2 %collective-permute-done.8 = f32[8,128]{1,0:T(8,128)S(1)} collective-permute-done((f32[8,128]{1,0:T(8,128)S(1)}, f32[8,128]{1,0:T(8,128)S(1)}, u32[]{:S(2)}, u32[]{:S(2)}) %collective-permute-start.8) | collective-permute-done | bytes 4128 | tf_op jit(solution)/shard_map/ppermute | solution.py:587
  24.2 0.7 %collective-permute-start.9 = (f32[8,128]{1,0:T(8,128)S(1)}, f32[8,128]{1,0:T(8,128)S(1)}, u32[]{:S(2)}, u32[]{:S(2)}) collective-permute-start(f32[8,128]{1,0:T(8,128)S(1)} %max.15), channel_id=1, source_target_pairs={{0,8},{4,12},{8,0},{12,4},{16,24},{20,28},{24,16},{28,20},{1,9},{5... | collective-permute-start | bytes 12296 | tf_op jit(solution)/shard_map/ppermute | solution.py:587
  25.0 2.9 %collective-permute-done.9 = f32[8,128]{1,0:T(8,128)S(1)} collective-permute-done((f32[8,128]{1,0:T(8,128)S(1)}, f32[8,128]{1,0:T(8,128)S(1)}, u32[]{:S(2)}, u32[]{:S(2)}) %collective-permute-start.9) | collective-permute-done | bytes 4128 | tf_op jit(solution)/shard_map/ppermute | solution.py:587
  27.8 1.7 %collective-permute-start.10 = (f32[8,128]{1,0:T(8,128)S(1)}, f32[8,128]{1,0:T(8,128)S(1)}, u32[]{:S(2)}, u32[]{:S(2)}) collective-permute-start(f32[8,128]{1,0:T(8,128)S(1)} %max.16), channel_id=1, source_target_pairs={{0,16},{4,20},{8,24},{12,28},{16,0},{20,4},{24,8},{28,12},{1,17},{... | collective-permute-start | bytes 12296 | tf_op jit(solution)/shard_map/ppermute | solution.py:587
  29.5 1.9 %collective-permute-done.10 = f32[8,128]{1,0:T(8,128)S(1)} collective-permute-done((f32[8,128]{1,0:T(8,128)S(1)}, f32[8,128]{1,0:T(8,128)S(1)}, u32[]{:S(2)}, u32[]{:S(2)}) %collective-permute-start.10) | collective-permute-done | bytes 4128 | tf_op jit(solution)/shard_map/ppermute | solution.py:587
  31.4 1.7 %collective-permute-start.11 = (f32[8,128]{1,0:T(8,128)S(1)}, f32[8,128]{1,0:T(8,128)S(1)}, u32[]{:S(2)}, u32[]{:S(2)}) collective-permute-start(f32[8,128]{1,0:T(8,128)S(1)} %max.17), channel_id=1, source_target_pairs={{0,1},{1,0},{2,3},{3,2},{4,5},{5,4},{6,7},{7,6},{8,9},{9,8},{10,11... | collective-permute-start | bytes 12296 | tf_op jit(solution)/shard_map/ppermute | solution.py:587
  33.1 3.5 %collective-permute-done.11 = f32[8,128]{1,0:T(8,128)S(1)} collective-permute-done((f32[8,128]{1,0:T(8,128)S(1)}, f32[8,128]{1,0:T(8,128)S(1)}, u32[]{:S(2)}, u32[]{:S(2)}) %collective-permute-start.11) | collective-permute-done | bytes 4128 | tf_op jit(solution)/shard_map/ppermute | solution.py:587
  36.7 1.1 %collective-permute-start.12 = (f32[8,128]{1,0:T(8,128)S(1)}, f32[8,128]{1,0:T(8,128)S(1)}, u32[]{:S(2)}, u32[]{:S(2)}) collective-permute-start(f32[8,128]{1,0:T(8,128)S(1)} %max.18), channel_id=1, source_target_pairs={{0,2},{1,3},{2,0},{3,1},{4,6},{5,7},{6,4},{7,5},{8,10},{9,11},{10,... | collective-permute-start | bytes 12296 | tf_op jit(solution)/shard_map/ppermute | solution.py:587
  37.8 3.4 %collective-permute-done.12 = f32[8,128]{1,0:T(8,128)S(1)} collective-permute-done((f32[8,128]{1,0:T(8,128)S(1)}, f32[8,128]{1,0:T(8,128)S(1)}, u32[]{:S(2)}, u32[]{:S(2)}) %collective-permute-start.12) | collective-permute-done | bytes 4128 | tf_op jit(solution)/shard_map/ppermute | solution.py:587
  41.2 0.0 collective-permute-done.5.refs_0_
  41.2 0.0 collective-permute-done.6.refs_1_
  41.2 0.0 collective-permute-done.7.refs_2_
  41.2 1.4 %shard_map.74 = (f32[5,4,24,512]{3,2,1,0:T(8,128)}, f32[5,64]{1,0:T(8,128)}) custom-call(f32[5,4,24,128]{3,2,1,0:T(8,128)S(1)} %collective-permute-done.5.refs_0_, f32[5,4,24,128]{3,2,1,0:T(8,128)S(1)} %collective-permute-done.6.refs_1_, f32[5,4,24,128]{3,2,1,0:T(8,128)S(1)} %collective-permute-done.7.refs_2_, ...), custom_call_target="tpu_custom_call" | custom-call | tf_op jit(solution)/shard_map/pallas_call | solution.py:553
  (5 shorter events, 0.0 us)
Async XLA Ops:
  0.6 1.3 %copy-start = (s32[6,128]{1,0:T(8,128)S(1)}, s32[6,128]{1,0:T(8,128)}, u32[]{:S(2)}) copy-start(s32[6,128]{1,0:T(8,128)} %membership.1) | copy-start | bytes 9220
  0.6 1.3 %copy-start.1 = (s32[1,4]{1,0:T(1,128)S(1)}, s32[1,4]{1,0:T(1,128)}, u32[]{:S(2)}) copy-start(s32[1,4]{1,0:T(1,128)} %slots.1) | copy-start | bytes 52
  2.6 6.9 %collective-permute-start = (f32[32,128]{1,0:T(8,128)S(1)}, f32[32,128]{1,0:T(8,128)S(1)}, u32[]{:S(2)}, u32[]{:S(2)}) collective-permute-start(f32[32,128]{1,0:T(8,128)S(1)} %get-tuple-element.30), channel_id=1, source_target_pairs={{0,1},{1,2},{2,3},{3,0},{4,5},{5,6},{6,7},{7,4},{8,9},{9,10},{10,1... | collective-permute-start | bytes 49160 | tf_op jit(solution)/shard_map/ppermute | solution.py:596
  5.7 3.9 %collective-permute-start.1 = (f32[32,128]{1,0:T(8,128)S(1)}, f32[32,128]{1,0:T(8,128)S(1)}, u32[]{:S(2)}, u32[]{:S(2)}) collective-permute-start(f32[32,128]{1,0:T(8,128)S(1)} %get-tuple-element.31), channel_id=1, source_target_pairs={{0,3},{1,0},{2,1},{3,2},{4,7},{5,4},{6,5},{7,6},{8,11},{9,8},{10,9... | collective-permute-start | bytes 49160 | tf_op jit(solution)/shard_map/ppermute | solution.py:597
  9.7 7.2 %collective-permute-start.2 = (f32[88,128]{1,0:T(8,128)S(1)}, f32[88,128]{1,0:T(8,128)S(1)}, u32[]{:S(2)}, u32[]{:S(2)}) collective-permute-start(f32[88,128]{1,0:T(8,128)S(1)} %get-tuple-element.44), channel_id=1, source_target_pairs={{0,4},{4,8},{8,12},{12,16},{16,20},{20,24},{24,28},{28,0},{1,5},{5... | collective-permute-start | bytes 135176 | tf_op jit(solution)/shard_map/ppermute | solution.py:602
  9.7 7.1 %collective-permute-start.3 = (f32[88,128]{1,0:T(8,128)S(1)}, f32[88,128]{1,0:T(8,128)S(1)}, u32[]{:S(2)}, u32[]{:S(2)}) collective-permute-start(f32[88,128]{1,0:T(8,128)S(1)} %get-tuple-element.45), channel_id=1, source_target_pairs={{0,28},{4,0},{8,4},{12,8},{16,12},{20,16},{24,20},{28,24},{1,29},{... | collective-permute-start | bytes 135176 | tf_op jit(solution)/shard_map/ppermute | solution.py:603
  12.4 4.5 %collective-permute-start.4 = (f32[8,128]{1,0:T(8,128)S(1)}, f32[8,128]{1,0:T(8,128)S(1)}, u32[]{:S(2)}, u32[]{:S(2)}) collective-permute-start(f32[8,128]{1,0:T(8,128)S(1)} %get-tuple-element.47.refs_1_.refs_5_), channel_id=1, source_target_pairs={{0,2},{1,3},{2,0},{3,1},{4,6},{5,7},{6,4},{7,5},{8,10},{9,11},{10,... | collective-permute-start | bytes 12296 | tf_op jit(solution)/shard_map/ppermute | solution.py:598
  17.7 23.5 %collective-permute-start.5 = (f32[5,4,24,128]{3,2,1,0:T(8,128)S(1)}, f32[5,4,24,128]{3,2,1,0:T(8,128)S(1)}, u32[]{:S(2)}, u32[]{:S(2)}) collective-permute-start(f32[5,4,24,128]{3,2,1,0:T(8,128)S(1)} %get-tuple-element.52), channel_id=1, source_target_pairs={{0,2},{1,3},{2,0},{3,1},{4,6},{5,7},{6,4},{7,5},{8,10},{9,11},{10,... | collective-permute-start | bytes 737288 | tf_op jit(solution)/shard_map/ppermute | solution.py:609
  20.2 21.0 %collective-permute-start.6 = (f32[5,4,24,128]{3,2,1,0:T(8,128)S(1)}, f32[5,4,24,128]{3,2,1,0:T(8,128)S(1)}, u32[]{:S(2)}, u32[]{:S(2)}) collective-permute-start(f32[5,4,24,128]{3,2,1,0:T(8,128)S(1)} %get-tuple-element.53), channel_id=1, source_target_pairs={{0,3},{1,2},{2,1},{3,0},{4,7},{5,6},{6,5},{7,4},{8,11},{9,10},{10,... | collective-permute-start | bytes 737288 | tf_op jit(solution)/shard_map/ppermute | solution.py:609
  21.7 19.5 %collective-permute-start.7 = (f32[5,4,24,128]{3,2,1,0:T(8,128)S(1)}, f32[5,4,24,128]{3,2,1,0:T(8,128)S(1)}, u32[]{:S(2)}, u32[]{:S(2)}) collective-permute-start(f32[5,4,24,128]{3,2,1,0:T(8,128)S(1)} %get-tuple-element.54), channel_id=1, source_target_pairs={{0,1},{1,0},{2,3},{3,2},{4,5},{5,4},{6,7},{7,6},{8,9},{9,8},{10,11... | collective-permute-start | bytes 737288 | tf_op jit(solution)/shard_map/ppermute | solution.py:609
  23.0 1.2 %collective-permute-start.8 = (f32[8,128]{1,0:T(8,128)S(1)}, f32[8,128]{1,0:T(8,128)S(1)}, u32[]{:S(2)}, u32[]{:S(2)}) collective-permute-start(f32[8,128]{1,0:T(8,128)S(1)} %shard_map.73), channel_id=1, source_target_pairs={{0,4},{4,0},{8,12},{12,8},{16,20},{20,16},{24,28},{28,24},{1,5},{5... | collective-permute-start | bytes 12296 | tf_op jit(solution)/shard_map/ppermute | solution.py:587
  24.2 3.6 %collective-permute-start.9 = (f32[8,128]{1,0:T(8,128)S(1)}, f32[8,128]{1,0:T(8,128)S(1)}, u32[]{:S(2)}, u32[]{:S(2)}) collective-permute-start(f32[8,128]{1,0:T(8,128)S(1)} %max.15), channel_id=1, source_target_pairs={{0,8},{4,12},{8,0},{12,4},{16,24},{20,28},{24,16},{28,20},{1,9},{5... | collective-permute-start | bytes 12296 | tf_op jit(solution)/shard_map/ppermute | solution.py:587
  27.8 3.6 %collective-permute-start.10 = (f32[8,128]{1,0:T(8,128)S(1)}, f32[8,128]{1,0:T(8,128)S(1)}, u32[]{:S(2)}, u32[]{:S(2)}) collective-permute-start(f32[8,128]{1,0:T(8,128)S(1)} %max.16), channel_id=1, source_target_pairs={{0,16},{4,20},{8,24},{12,28},{16,0},{20,4},{24,8},{28,12},{1,17},{... | collective-permute-start | bytes 12296 | tf_op jit(solution)/shard_map/ppermute | solution.py:587
  31.4 5.2 %collective-permute-start.11 = (f32[8,128]{1,0:T(8,128)S(1)}, f32[8,128]{1,0:T(8,128)S(1)}, u32[]{:S(2)}, u32[]{:S(2)}) collective-permute-start(f32[8,128]{1,0:T(8,128)S(1)} %max.17), channel_id=1, source_target_pairs={{0,1},{1,0},{2,3},{3,2},{4,5},{5,4},{6,7},{7,6},{8,9},{9,8},{10,11... | collective-permute-start | bytes 12296 | tf_op jit(solution)/shard_map/ppermute | solution.py:587
  36.7 4.5 %collective-permute-start.12 = (f32[8,128]{1,0:T(8,128)S(1)}, f32[8,128]{1,0:T(8,128)S(1)}, u32[]{:S(2)}, u32[]{:S(2)}) collective-permute-start(f32[8,128]{1,0:T(8,128)S(1)} %max.18), channel_id=1, source_target_pairs={{0,2},{1,3},{2,0},{3,1},{4,6},{5,7},{6,4},{7,5},{8,10},{9,11},{10,... | collective-permute-start | bytes 12296 | tf_op jit(solution)/shard_map/ppermute | solution.py:587

commit v6 on v5

--- a/solution.py
+++ b/solution.py
@@ -602,9 +602,10 @@
     top = lax.ppermute(last_y, "sim", ring("sim", 1))
     bottom = lax.ppermute(first_y, "sim", ring("sim", -1))
     chunks, blocks, rims = transform_bricks(count, inside, down, up, columns, matrix)
-    blocks, *far = lax.optimization_barrier((blocks, *far))
     chunks, blocks = mend(count, chunks, top, bottom, blocks, rims, matrix)
     moved = {0: chunks[0]}
+    second = leaving_order(count)[min(1, count - 2)]
+    chunks[second], *far = lax.optimization_barrier((chunks[second], *far))
     for k in leaving_order(count)[:-1]:
         moved[k] = lax.ppermute(chunks[k], "section", exchange_pairs(count, k))
     peaks = group_maxima(count, groups, membership.shape[0], blocks, [labels, left, *far, right])

time: 42.7 us -> 43 us (level)
  waiting for transfers between devices: 14 us -> 14.9 us
  starting transfers between devices: 19.9 us -> 19.2 us
    ppermute x5, waiting for transfers between devices: 12.8 us -> 14 us  [with_others(): lax.ppermute(value, axis, exchange_pairs(count, k))]
    ppermute x5, starting transfers between devices: 5.3 us -> 4.51 us  [with_others(): lax.ppermute(value, axis, exchange_pairs(count, k))]
  transfers between devices with their start and end apart: 13 -> 13, of which waited for: 8 -> 7; matrix products, arithmetic and copies ran while one was open for 0% -> 0% of each run, Pallas kernels for 9% -> 11%
where the time goes in v6:
time: 43 us; the launch traced here: 42.8 us
  starting transfers between devices  19.2 us (45%)
  waiting for transfers between devices  14.9 us (35%)
  Pallas kernels  6.65 us (15%)
  other arithmetic  1.31 us (3%)
  between operations  0.74 us (2%)
    ppermute x5, waiting for transfers between devices, with_others(): lax.ppermute(value, axis, exchange_pairs(count, k))  14 us
    ppermute x5, starting transfers between devices, with_others(): lax.ppermute(value, axis, exchange_pairs(count, k))  4.51 us
    ppermute x3, starting transfers between devices, per_device(): moved[k] = lax.ppermute(chunks[k], 'section', exchange_pairs(count, k))  4.45 us
    ppermute x1, starting transfers between devices, per_device(): left = lax.ppermute(last_x, 'section', ring('section', 1))  3.06 us
    ppermute x1, starting transfers between devices, per_device(): bottom = lax.ppermute(first_y, 'sim', ring('sim', -1))  2.63 us
    ppermute x1, starting transfers between devices, per_device(): lax.ppermute(labels, 'section', ring('section', d))  2.41 us
    ppermute x1, starting transfers between devices, per_device(): right = lax.ppermute(first_x, 'section', ring('section', -1))  2.09 us
    pallas_call x1, Pallas kernels, transform_bricks(): pl.pallas_call(functools.partial(brick_kernel, count), out_shape=[chunk]...  1.79 us
  transfers between devices with their start and end apart: 13, of which 7 were waited for; matrix products, arithmetic and copies ran while one was open for 0% of the time, Pallas kernels for 11%

profile of v6, /device:TPU:0, one launch (start us, length us, event | category | flops | bytes accessed | tf_op | source)
XLA Modules:
  0.0 42.8 jit_solution(9028170611665633218)
XLA Ops:
  0.6 0.0 copy-start
  0.6 0.0 copy-start.1
  0.7 1.3 %pad_maximum_fusion.conserved = f32[5,4,96,128]{3,2,1,0:T(8,128)S(1)} fusion(f32[1,4,96,128]{3,2,1,0:T(8,128)} %bitcast.2, f32[3,4,96,128]{3,2,1,0:T(8,128)} %param.6, f32[1,4,96,128]{3,2,1,0:T(8,128)} %bitcast.3), kind=kLoop, calls=%fused_computation | loop fusion | flops 491520 | bytes 1966080 | tf_op jit(solution)/shard_map/concatenate | solution.py:594
  2.0 0.0 copy-done
  2.0 0.0 copy-done.1
  2.0 0.6 %shard_map.68 = (f32[32,128]{1,0:T(8,128)S(1)}, f32[32,128]{1,0:T(8,128)S(1)}, f32[8,128]{1,0:T(8,128)S(1)}) custom-call(f32[5,4,96,128]{3,2,1,0:T(8,128)S(1)} %pad_maximum_fusion.conserved, s32[6,128]{1,0:T(8,128)S(1)} %copy-done, s32[1,4]{1,0:T(1,128)S(1)} %copy-done.1), custom_call_target="tpu_custom_call" | custom-call | tf_op jit(solution)/shard_map/pallas_call | solution.py:112
  2.6 3.1 %collective-permute-start = (f32[32,128]{1,0:T(8,128)S(1)}, f32[32,128]{1,0:T(8,128)S(1)}, u32[]{:S(2)}, u32[]{:S(2)}) collective-permute-start(f32[32,128]{1,0:T(8,128)S(1)} %get-tuple-element.30), channel_id=1, source_target_pairs={{0,1},{1,2},{2,3},{3,0},{4,5},{5,6},{6,7},{7,4},{8,9},{9,10},{10,1... | collective-permute-start | bytes 49160 | tf_op jit(solution)/shard_map/ppermute | solution.py:596
  5.7 2.1 %collective-permute-start.1 = (f32[32,128]{1,0:T(8,128)S(1)}, f32[32,128]{1,0:T(8,128)S(1)}, u32[]{:S(2)}, u32[]{:S(2)}) collective-permute-start(f32[32,128]{1,0:T(8,128)S(1)} %get-tuple-element.31), channel_id=1, source_target_pairs={{0,3},{1,0},{2,1},{3,2},{4,7},{5,4},{6,5},{7,6},{8,11},{9,8},{10,9... | collective-permute-start | bytes 49160 | tf_op jit(solution)/shard_map/ppermute | solution.py:597
  7.7 1.0 %shard_map.69 = (f32[20,96,128]{2,1,0:T(8,128)S(1)}, f32[20,112,128]{2,1,0:T(8,128)S(1)}, f32[20,112,128]{2,1,0:T(8,128)S(1)}, bf16[256,256]{1,0:T(8,128)(2,1)S(1)}) custom-call(f32[5,4,96,128]{3,2,1,0:T(8,128)S(1)} %pad_maximum_fusion.conserved), custom_call_target="tpu_custom_call" | custom-call | flops 9830400 | bytes 3932160 | tf_op jit(solution)/shard_map/pallas_call | solution.py:225
  8.7 0.8 %collective-permute-done.left.refs_2_ = f32[32,128]{1,0:T(8,128)S(1)} collective-permute-done((f32[32,128]{1,0:T(8,128)S(1)}, f32[32,128]{1,0:T(8,128)S(1)}, u32[]{:S(2)}, u32[]{:S(2)}) %collective-permute-start) | collective-permute-done | bytes 16416 | tf_op jit(solution)/shard_map/ppermute | solution.py:596
  9.5 0.1 collective-permute-done.1.right.refs_4_
  9.6 0.1 shard_map.70
  9.7 0.1 collective-permute-start.2
  9.7 2.6 %collective-permute-start.3 = (f32[88,128]{1,0:T(8,128)S(1)}, f32[88,128]{1,0:T(8,128)S(1)}, u32[]{:S(2)}, u32[]{:S(2)}) collective-permute-start(f32[88,128]{1,0:T(8,128)S(1)} %get-tuple-element.45), channel_id=1, source_target_pairs={{0,28},{4,0},{8,4},{12,8},{16,12},{20,16},{24,20},{28,24},{1,29},{... | collective-permute-start | bytes 135176 | tf_op jit(solution)/shard_map/ppermute | solution.py:603
  12.4 2.4 %collective-permute-start.5 = (f32[8,128]{1,0:T(8,128)S(1)}, f32[8,128]{1,0:T(8,128)S(1)}, u32[]{:S(2)}, u32[]{:S(2)}) collective-permute-start(f32[8,128]{1,0:T(8,128)S(1)} %get-tuple-element.52.refs_1_.refs_5_), channel_id=1, source_target_pairs={{0,2},{1,3},{2,0},{3,1},{4,6},{5,7},{6,4},{7,5},{8,10},{9,11},{10,... | collective-permute-start | bytes 12296 | tf_op jit(solution)/shard_map/ppermute | solution.py:598
  14.8 1.8 %shard_map.71 = (f32[5,4,24,128]{3,2,1,0:T(8,128)S(1)}, f32[5,4,24,128]{3,2,1,0:T(8,128)S(1)}, f32[5,4,24,128]{3,2,1,0:T(8,128)S(1)}, f32[5,4,24,128]{3,2,1,0:T(...) custom-call(f32[20,96,128]{2,1,0:T(8,128)S(1)} %get-tuple-element.33, ...), custom_call_target="tpu_custom_call" | custom-call | flops 19660800 | bytes 3932160 | tf_op jit(solution)/shard_map/pallas_call | solution.py:328
  16.6 0.0 collective-permute-done.2.refs_4_
  16.6 0.0 collective-permute-done.3.refs_5_
  16.6 0.8 %shard_map.72 = (f32[5,4,24,128]{3,2,1,0:T(8,128)S(1)}, f32[5,4,24,128]{3,2,1,0:T(8,128)S(1)}, f32[5,4,24,128]{3,2,1,0:T(8,128)S(1)}, f32[5,4,24,128]{3,2,1,0:T(8,128)S(1)}, f32[5,24,128]{2,1,0:T(8,128)S(1)}) custom-call(f32[5,4,24,128]{3,2,1,0:T(8,128)S(1)} %get-tuple-element.40.refs_0_, ...), custom_call_target="tpu_custom_call", output_to_operand_aliasing={{0}: (0, {}), {1}: (1, {}), {2}: (2, {}), {3}: (3, {})} | custom-call | tf_op jit(solution)/shard_map/pallas_call | solution.py:420
  17.4 0.0 collective-permute-done.5.refs_3_
  17.4 3.2 %collective-permute-start.6 = (f32[5,4,24,128]{3,2,1,0:T(8,128)S(1)}, f32[5,4,24,128]{3,2,1,0:T(8,128)S(1)}, u32[]{:S(2)}, u32[]{:S(2)}) collective-permute-start(f32[5,4,24,128]{3,2,1,0:T(8,128)S(1)} %get-tuple-element.53), channel_id=1, source_target_pairs={{0,3},{1,2},{2,1},{3,0},{4,7},{5,6},{6,5},{7,4},{8,11},{9,10},{10,... | collective-permute-start | bytes 737288 | tf_op jit(solution)/shard_map/ppermute | solution.py:610
  20.6 0.2 collective-permute-start.4
  20.8 1.0 %collective-permute-start.7 = (f32[5,4,24,128]{3,2,1,0:T(8,128)S(1)}, f32[5,4,24,128]{3,2,1,0:T(8,128)S(1)}, u32[]{:S(2)}, u32[]{:S(2)}) collective-permute-start(f32[5,4,24,128]{3,2,1,0:T(8,128)S(1)} %get-tuple-element.54), channel_id=1, source_target_pairs={{0,1},{1,0},{2,3},{3,2},{4,5},{5,4},{6,7},{7,6},{8,9},{9,8},{10,11... | collective-permute-start | bytes 737288 | tf_op jit(solution)/shard_map/ppermute | solution.py:610
  21.9 1.0 %shard_map.73 = f32[8,128]{1,0:T(8,128)S(1)} custom-call(f32[5,24,128]{2,1,0:T(8,128)S(1)} %get-tuple-element.56.refs_0_, f32[8,128]{1,0:T(8,128)S(1)} %get-tuple-element.52.refs_1_.refs_5_, f32[32,128]{1,0:T(8,128)S(1)} %collective-permute-done.left.refs_2_, f32[8,128]{1,0:T(8,128)S(1)} %collective-permute-done.5.refs_3_, ...), custom_call_target="tpu_custom_call" | custom-call | tf_op jit(solution)/shard_map/pallas_call | solution.py:497
  22.8 0.0 collective-permute-start.8
  22.9 1.2 %collective-permute-done.8 = f32[8,128]{1,0:T(8,128)S(1)} collective-permute-done((f32[8,128]{1,0:T(8,128)S(1)}, f32[8,128]{1,0:T(8,128)S(1)}, u32[]{:S(2)}, u32[]{:S(2)}) %collective-permute-start.8) | collective-permute-done | bytes 4128 | tf_op jit(solution)/shard_map/ppermute | solution.py:587
  24.0 0.6 %collective-permute-start.9 = (f32[8,128]{1,0:T(8,128)S(1)}, f32[8,128]{1,0:T(8,128)S(1)}, u32[]{:S(2)}, u32[]{:S(2)}) collective-permute-start(f32[8,128]{1,0:T(8,128)S(1)} %max.15), channel_id=1, source_target_pairs={{0,8},{4,12},{8,0},{12,4},{16,24},{20,28},{24,16},{28,20},{1,9},{5... | collective-permute-start | bytes 12296 | tf_op jit(solution)/shard_map/ppermute | solution.py:587
  24.6 3.0 %collective-permute-done.9 = f32[8,128]{1,0:T(8,128)S(1)} collective-permute-done((f32[8,128]{1,0:T(8,128)S(1)}, f32[8,128]{1,0:T(8,128)S(1)}, u32[]{:S(2)}, u32[]{:S(2)}) %collective-permute-start.9) | collective-permute-done | bytes 4128 | tf_op jit(solution)/shard_map/ppermute | solution.py:587
  27.7 1.5 %collective-permute-start.10 = (f32[8,128]{1,0:T(8,128)S(1)}, f32[8,128]{1,0:T(8,128)S(1)}, u32[]{:S(2)}, u32[]{:S(2)}) collective-permute-start(f32[8,128]{1,0:T(8,128)S(1)} %max.16), channel_id=1, source_target_pairs={{0,16},{4,20},{8,24},{12,28},{16,0},{20,4},{24,8},{28,12},{1,17},{... | collective-permute-start | bytes 12296 | tf_op jit(solution)/shard_map/ppermute | solution.py:587
  29.2 2.1 %collective-permute-done.10 = f32[8,128]{1,0:T(8,128)S(1)} collective-permute-done((f32[8,128]{1,0:T(8,128)S(1)}, f32[8,128]{1,0:T(8,128)S(1)}, u32[]{:S(2)}, u32[]{:S(2)}) %collective-permute-start.10) | collective-permute-done | bytes 4128 | tf_op jit(solution)/shard_map/ppermute | solution.py:587
  31.3 1.0 %collective-permute-start.11 = (f32[8,128]{1,0:T(8,128)S(1)}, f32[8,128]{1,0:T(8,128)S(1)}, u32[]{:S(2)}, u32[]{:S(2)}) collective-permute-start(f32[8,128]{1,0:T(8,128)S(1)} %max.17), channel_id=1, source_target_pairs={{0,1},{1,0},{2,3},{3,2},{4,5},{5,4},{6,7},{7,6},{8,9},{9,8},{10,11... | collective-permute-start | bytes 12296 | tf_op jit(solution)/shard_map/ppermute | solution.py:587
  32.2 3.4 %collective-permute-done.11 = f32[8,128]{1,0:T(8,128)S(1)} collective-permute-done((f32[8,128]{1,0:T(8,128)S(1)}, f32[8,128]{1,0:T(8,128)S(1)}, u32[]{:S(2)}, u32[]{:S(2)}) %collective-permute-start.11) | collective-permute-done | bytes 4128 | tf_op jit(solution)/shard_map/ppermute | solution.py:587
  35.7 1.4 %collective-permute-start.12 = (f32[8,128]{1,0:T(8,128)S(1)}, f32[8,128]{1,0:T(8,128)S(1)}, u32[]{:S(2)}, u32[]{:S(2)}) collective-permute-start(f32[8,128]{1,0:T(8,128)S(1)} %max.18), channel_id=1, source_target_pairs={{0,2},{1,3},{2,0},{3,1},{4,6},{5,7},{6,4},{7,5},{8,10},{9,11},{10,... | collective-permute-start | bytes 12296 | tf_op jit(solution)/shard_map/ppermute | solution.py:587
  37.1 4.3 %collective-permute-done.12 = f32[8,128]{1,0:T(8,128)S(1)} collective-permute-done((f32[8,128]{1,0:T(8,128)S(1)}, f32[8,128]{1,0:T(8,128)S(1)}, u32[]{:S(2)}, u32[]{:S(2)}) %collective-permute-start.12) | collective-permute-done | bytes 4128 | tf_op jit(solution)/shard_map/ppermute | solution.py:587
  41.4 0.0 collective-permute-done.6.refs_1_
  41.4 0.0 collective-permute-done.4.refs_0_
  41.4 0.0 collective-permute-done.7.refs_2_
  41.4 1.4 %shard_map.74 = (f32[5,4,24,512]{3,2,1,0:T(8,128)}, f32[5,64]{1,0:T(8,128)}) custom-call(f32[5,4,24,128]{3,2,1,0:T(8,128)S(1)} %collective-permute-done.4.refs_0_, f32[5,4,24,128]{3,2,1,0:T(8,128)S(1)} %collective-permute-done.6.refs_1_, f32[5,4,24,128]{3,2,1,0:T(8,128)S(1)} %collective-permute-done.7.refs_2_, ...), custom_call_target="tpu_custom_call" | custom-call | tf_op jit(solution)/shard_map/pallas_call | solution.py:553
  (5 shorter events, 0.0 us)
Async XLA Ops:
  0.6 1.3 %copy-start = (s32[6,128]{1,0:T(8,128)S(1)}, s32[6,128]{1,0:T(8,128)}, u32[]{:S(2)}) copy-start(s32[6,128]{1,0:T(8,128)} %membership.1) | copy-start | bytes 9220
  0.6 1.3 %copy-start.1 = (s32[1,4]{1,0:T(1,128)S(1)}, s32[1,4]{1,0:T(1,128)}, u32[]{:S(2)}) copy-start(s32[1,4]{1,0:T(1,128)} %slots.1) | copy-start | bytes 52
  2.6 6.9 %collective-permute-start = (f32[32,128]{1,0:T(8,128)S(1)}, f32[32,128]{1,0:T(8,128)S(1)}, u32[]{:S(2)}, u32[]{:S(2)}) collective-permute-start(f32[32,128]{1,0:T(8,128)S(1)} %get-tuple-element.30), channel_id=1, source_target_pairs={{0,1},{1,2},{2,3},{3,0},{4,5},{5,6},{6,7},{7,4},{8,9},{9,10},{10,1... | collective-permute-start | bytes 49160 | tf_op jit(solution)/shard_map/ppermute | solution.py:596
  5.7 3.9 %collective-permute-start.1 = (f32[32,128]{1,0:T(8,128)S(1)}, f32[32,128]{1,0:T(8,128)S(1)}, u32[]{:S(2)}, u32[]{:S(2)}) collective-permute-start(f32[32,128]{1,0:T(8,128)S(1)} %get-tuple-element.31), channel_id=1, source_target_pairs={{0,3},{1,0},{2,1},{3,2},{4,7},{5,4},{6,5},{7,6},{8,11},{9,8},{10,9... | collective-permute-start | bytes 49160 | tf_op jit(solution)/shard_map/ppermute | solution.py:597
  9.7 6.9 %collective-permute-start.2 = (f32[88,128]{1,0:T(8,128)S(1)}, f32[88,128]{1,0:T(8,128)S(1)}, u32[]{:S(2)}, u32[]{:S(2)}) collective-permute-start(f32[88,128]{1,0:T(8,128)S(1)} %get-tuple-element.44), channel_id=1, source_target_pairs={{0,4},{4,8},{8,12},{12,16},{16,20},{20,24},{24,28},{28,0},{1,5},{5... | collective-permute-start | bytes 135176 | tf_op jit(solution)/shard_map/ppermute | solution.py:602
  9.7 6.8 %collective-permute-start.3 = (f32[88,128]{1,0:T(8,128)S(1)}, f32[88,128]{1,0:T(8,128)S(1)}, u32[]{:S(2)}, u32[]{:S(2)}) collective-permute-start(f32[88,128]{1,0:T(8,128)S(1)} %get-tuple-element.45), channel_id=1, source_target_pairs={{0,28},{4,0},{8,4},{12,8},{16,12},{20,16},{24,20},{28,24},{1,29},{... | collective-permute-start | bytes 135176 | tf_op jit(solution)/shard_map/ppermute | solution.py:603
  12.4 5.0 %collective-permute-start.5 = (f32[8,128]{1,0:T(8,128)S(1)}, f32[8,128]{1,0:T(8,128)S(1)}, u32[]{:S(2)}, u32[]{:S(2)}) collective-permute-start(f32[8,128]{1,0:T(8,128)S(1)} %get-tuple-element.52.refs_1_.refs_5_), channel_id=1, source_target_pairs={{0,2},{1,3},{2,0},{3,1},{4,6},{5,7},{6,4},{7,5},{8,10},{9,11},{10,... | collective-permute-start | bytes 12296 | tf_op jit(solution)/shard_map/ppermute | solution.py:598
  17.4 24.0 %collective-permute-start.6 = (f32[5,4,24,128]{3,2,1,0:T(8,128)S(1)}, f32[5,4,24,128]{3,2,1,0:T(8,128)S(1)}, u32[]{:S(2)}, u32[]{:S(2)}) collective-permute-start(f32[5,4,24,128]{3,2,1,0:T(8,128)S(1)} %get-tuple-element.53), channel_id=1, source_target_pairs={{0,3},{1,2},{2,1},{3,0},{4,7},{5,6},{6,5},{7,4},{8,11},{9,10},{10,... | collective-permute-start | bytes 737288 | tf_op jit(solution)/shard_map/ppermute | solution.py:610
  20.6 20.9 %collective-permute-start.4 = (f32[5,4,24,128]{3,2,1,0:T(8,128)S(1)}, f32[5,4,24,128]{3,2,1,0:T(8,128)S(1)}, u32[]{:S(2)}, u32[]{:S(2)}) collective-permute-start(f32[5,4,24,128]{3,2,1,0:T(8,128)S(1)} %get-tuple-element.50), channel_id=1, source_target_pairs={{0,2},{1,3},{2,0},{3,1},{4,6},{5,7},{6,4},{7,5},{8,10},{9,11},{10,... | collective-permute-start | bytes 737288 | tf_op jit(solution)/shard_map/ppermute | solution.py:610
  20.8 20.6 %collective-permute-start.7 = (f32[5,4,24,128]{3,2,1,0:T(8,128)S(1)}, f32[5,4,24,128]{3,2,1,0:T(8,128)S(1)}, u32[]{:S(2)}, u32[]{:S(2)}) collective-permute-start(f32[5,4,24,128]{3,2,1,0:T(8,128)S(1)} %get-tuple-element.54), channel_id=1, source_target_pairs={{0,1},{1,0},{2,3},{3,2},{4,5},{5,4},{6,7},{7,6},{8,9},{9,8},{10,11... | collective-permute-start | bytes 737288 | tf_op jit(solution)/shard_map/ppermute | solution.py:610
  22.8 1.2 %collective-permute-start.8 = (f32[8,128]{1,0:T(8,128)S(1)}, f32[8,128]{1,0:T(8,128)S(1)}, u32[]{:S(2)}, u32[]{:S(2)}) collective-permute-start(f32[8,128]{1,0:T(8,128)S(1)} %shard_map.73), channel_id=1, source_target_pairs={{0,4},{4,0},{8,12},{12,8},{16,20},{20,16},{24,28},{28,24},{1,5},{5... | collective-permute-start | bytes 12296 | tf_op jit(solution)/shard_map/ppermute | solution.py:587
  24.0 3.6 %collective-permute-start.9 = (f32[8,128]{1,0:T(8,128)S(1)}, f32[8,128]{1,0:T(8,128)S(1)}, u32[]{:S(2)}, u32[]{:S(2)}) collective-permute-start(f32[8,128]{1,0:T(8,128)S(1)} %max.15), channel_id=1, source_target_pairs={{0,8},{4,12},{8,0},{12,4},{16,24},{20,28},{24,16},{28,20},{1,9},{5... | collective-permute-start | bytes 12296 | tf_op jit(solution)/shard_map/ppermute | solution.py:587
  27.7 3.6 %collective-permute-start.10 = (f32[8,128]{1,0:T(8,128)S(1)}, f32[8,128]{1,0:T(8,128)S(1)}, u32[]{:S(2)}, u32[]{:S(2)}) collective-permute-start(f32[8,128]{1,0:T(8,128)S(1)} %max.16), channel_id=1, source_target_pairs={{0,16},{4,20},{8,24},{12,28},{16,0},{20,4},{24,8},{28,12},{1,17},{... | collective-permute-start | bytes 12296 | tf_op jit(solution)/shard_map/ppermute | solution.py:587
  31.3 4.4 %collective-permute-start.11 = (f32[8,128]{1,0:T(8,128)S(1)}, f32[8,128]{1,0:T(8,128)S(1)}, u32[]{:S(2)}, u32[]{:S(2)}) collective-permute-start(f32[8,128]{1,0:T(8,128)S(1)} %max.17), channel_id=1, source_target_pairs={{0,1},{1,0},{2,3},{3,2},{4,5},{5,4},{6,7},{7,6},{8,9},{9,8},{10,11... | collective-permute-start | bytes 12296 | tf_op jit(solution)/shard_map/ppermute | solution.py:587
  35.7 5.7 %collective-permute-start.12 = (f32[8,128]{1,0:T(8,128)S(1)}, f32[8,128]{1,0:T(8,128)S(1)}, u32[]{:S(2)}, u32[]{:S(2)}) collective-permute-start(f32[8,128]{1,0:T(8,128)S(1)} %max.18), channel_id=1, source_target_pairs={{0,2},{1,3},{2,0},{3,1},{4,6},{5,7},{6,4},{7,5},{8,10},{9,11},{10,... | collective-permute-start | bytes 12296 | tf_op jit(solution)/shard_map/ppermute | solution.py:587

commit v7 on v5

--- a/solution.py
+++ b/solution.py
@@ -610,8 +610,12 @@
     peaks = group_maxima(count, groups, membership.shape[0], blocks, [labels, left, *far, right])
     for shift in steps_over("sim"):
         peaks = with_others(peaks, "sim", [shift])
-    for shift in steps_over("section"):
-        peaks = with_others(peaks, "section", [shift])
+    if count <= 4:
+        peaks, moved[1] = lax.optimization_barrier((peaks, moved[1]))
+        peaks = with_others(peaks, "section", range(1, count))
+    else:
+        for shift in steps_over("section"):
+            peaks = with_others(peaks, "section", [shift])
     return tuple(scale(count, groups, [moved[k] for k in leaving_order(count)], peaks, labels))
 
 

time: 42.7 us -> 44.4 us (1.040)
  starting transfers between devices: 19.9 us -> 21.4 us
    ppermute x5 -> x6, starting transfers between devices: 5.3 us -> 6.65 us  [with_others(): lax.ppermute(value, axis, exchange_pairs(count, k))]
    ppermute x5 -> x6, waiting for transfers between devices: 12.8 us -> 13 us  [with_others(): lax.ppermute(value, axis, exchange_pairs(count, k))]
  transfers between devices with their start and end apart: 13 -> 14, of which waited for: 8 -> 7; matrix products, arithmetic and copies ran while one was open for 0% -> 0% of each run, Pallas kernels for 9% -> 8%
where the time goes in v7:
time: 44.4 us; the launch traced here: 44.2 us
  starting transfers between devices  21.4 us (48%)
  waiting for transfers between devices  14.2 us (32%)
  Pallas kernels  6.65 us (15%)
  other arithmetic  1.31 us (3%)
  between operations  0.74 us (2%)
    ppermute x6, waiting for transfers between devices, with_others(): lax.ppermute(value, axis, exchange_pairs(count, k))  13 us
    ppermute x6, starting transfers between devices, with_others(): lax.ppermute(value, axis, exchange_pairs(count, k))  6.65 us
    ppermute x3, starting transfers between devices, per_device(): moved[k] = lax.ppermute(chunks[k], 'section', exchange_pairs(count, k))  4.45 us
    ppermute x1, starting transfers between devices, per_device(): left = lax.ppermute(last_x, 'section', ring('section', 1))  3.06 us
    ppermute x1, starting transfers between devices, per_device(): bottom = lax.ppermute(first_y, 'sim', ring('sim', -1))  2.63 us
    ppermute x1, starting transfers between devices, per_device(): lax.ppermute(labels, 'section', ring('section', d))  2.41 us
    ppermute x1, starting transfers between devices, per_device(): right = lax.ppermute(first_x, 'section', ring('section', -1))  2.09 us
    pallas_call x1, Pallas kernels, transform_bricks(): pl.pallas_call(functools.partial(brick_kernel, count), out_shape=[chunk]...  1.79 us
  transfers between devices with their start and end apart: 14, of which 7 were waited for; matrix products, arithmetic and copies ran while one was open for 0% of the time, Pallas kernels for 8%

profile of v7, /device:TPU:0, one launch (start us, length us, event | category | flops | bytes accessed | tf_op | source)
XLA Modules:
  0.0 44.2 jit_solution(14312571855158896139)
XLA Ops:
  0.6 0.0 copy-start
  0.6 0.0 copy-start.1
  0.7 1.3 %pad_maximum_fusion.conserved = f32[5,4,96,128]{3,2,1,0:T(8,128)S(1)} fusion(f32[1,4,96,128]{3,2,1,0:T(8,128)} %bitcast.2, f32[3,4,96,128]{3,2,1,0:T(8,128)} %param.6, f32[1,4,96,128]{3,2,1,0:T(8,128)} %bitcast.3), kind=kLoop, calls=%fused_computation | loop fusion | flops 491520 | bytes 1966080 | tf_op jit(solution)/shard_map/concatenate | solution.py:594
  2.0 0.0 copy-done
  2.0 0.0 copy-done.1
  2.0 0.6 %shard_map.68 = (f32[32,128]{1,0:T(8,128)S(1)}, f32[32,128]{1,0:T(8,128)S(1)}, f32[8,128]{1,0:T(8,128)S(1)}) custom-call(f32[5,4,96,128]{3,2,1,0:T(8,128)S(1)} %pad_maximum_fusion.conserved, s32[6,128]{1,0:T(8,128)S(1)} %copy-done, s32[1,4]{1,0:T(1,128)S(1)} %copy-done.1), custom_call_target="tpu_custom_call" | custom-call | tf_op jit(solution)/shard_map/pallas_call | solution.py:112
  2.6 3.1 %collective-permute-start = (f32[32,128]{1,0:T(8,128)S(1)}, f32[32,128]{1,0:T(8,128)S(1)}, u32[]{:S(2)}, u32[]{:S(2)}) collective-permute-start(f32[32,128]{1,0:T(8,128)S(1)} %get-tuple-element.32), channel_id=1, source_target_pairs={{0,1},{1,2},{2,3},{3,0},{4,5},{5,6},{6,7},{7,4},{8,9},{9,10},{10,1... | collective-permute-start | bytes 49160 | tf_op jit(solution)/shard_map/ppermute | solution.py:596
  5.7 2.1 %collective-permute-start.1 = (f32[32,128]{1,0:T(8,128)S(1)}, f32[32,128]{1,0:T(8,128)S(1)}, u32[]{:S(2)}, u32[]{:S(2)}) collective-permute-start(f32[32,128]{1,0:T(8,128)S(1)} %get-tuple-element.33), channel_id=1, source_target_pairs={{0,3},{1,0},{2,1},{3,2},{4,7},{5,4},{6,5},{7,6},{8,11},{9,8},{10,9... | collective-permute-start | bytes 49160 | tf_op jit(solution)/shard_map/ppermute | solution.py:597
  7.7 1.0 %shard_map.69 = (f32[20,96,128]{2,1,0:T(8,128)S(1)}, f32[20,112,128]{2,1,0:T(8,128)S(1)}, f32[20,112,128]{2,1,0:T(8,128)S(1)}, bf16[256,256]{1,0:T(8,128)(2,1)S(1)}) custom-call(f32[5,4,96,128]{3,2,1,0:T(8,128)S(1)} %pad_maximum_fusion.conserved), custom_call_target="tpu_custom_call" | custom-call | flops 9830400 | bytes 3932160 | tf_op jit(solution)/shard_map/pallas_call | solution.py:225
  8.7 0.8 %collective-permute-done.left.refs_2_ = f32[32,128]{1,0:T(8,128)S(1)} collective-permute-done((f32[32,128]{1,0:T(8,128)S(1)}, f32[32,128]{1,0:T(8,128)S(1)}, u32[]{:S(2)}, u32[]{:S(2)}) %collective-permute-start) | collective-permute-done | bytes 16416 | tf_op jit(solution)/shard_map/ppermute | solution.py:596
  9.5 0.1 collective-permute-done.1.right.refs_4_
  9.6 0.1 shard_map.70
  9.7 0.1 collective-permute-start.2
  9.7 2.6 %collective-permute-start.3 = (f32[88,128]{1,0:T(8,128)S(1)}, f32[88,128]{1,0:T(8,128)S(1)}, u32[]{:S(2)}, u32[]{:S(2)}) collective-permute-start(f32[88,128]{1,0:T(8,128)S(1)} %get-tuple-element.47), channel_id=1, source_target_pairs={{0,28},{4,0},{8,4},{12,8},{16,12},{20,16},{24,20},{28,24},{1,29},{... | collective-permute-start | bytes 135176 | tf_op jit(solution)/shard_map/ppermute | solution.py:603
  12.4 2.4 %collective-permute-start.4 = (f32[8,128]{1,0:T(8,128)S(1)}, f32[8,128]{1,0:T(8,128)S(1)}, u32[]{:S(2)}, u32[]{:S(2)}) collective-permute-start(f32[8,128]{1,0:T(8,128)S(1)} %get-tuple-element.49.refs_1_.refs_5_), channel_id=1, source_target_pairs={{0,2},{1,3},{2,0},{3,1},{4,6},{5,7},{6,4},{7,5},{8,10},{9,11},{10,... | collective-permute-start | bytes 12296 | tf_op jit(solution)/shard_map/ppermute | solution.py:598
  14.8 1.8 %shard_map.71 = (f32[5,4,24,128]{3,2,1,0:T(8,128)S(1)}, f32[5,4,24,128]{3,2,1,0:T(8,128)S(1)}, f32[5,4,24,128]{3,2,1,0:T(8,128)S(1)}, f32[5,4,24,128]{3,2,1,0:T(...) custom-call(f32[20,96,128]{2,1,0:T(8,128)S(1)} %get-tuple-element.35, ...), custom_call_target="tpu_custom_call" | custom-call | flops 19660800 | bytes 3932160 | tf_op jit(solution)/shard_map/pallas_call | solution.py:328
  16.6 0.3 collective-permute-done.4.refs_3_
  16.9 0.0 collective-permute-done.2.refs_4_
  16.9 0.0 collective-permute-done.3.refs_5_
  16.9 0.8 %shard_map.72 = (f32[5,4,24,128]{3,2,1,0:T(8,128)S(1)}, f32[5,4,24,128]{3,2,1,0:T(8,128)S(1)}, f32[5,4,24,128]{3,2,1,0:T(8,128)S(1)}, f32[5,4,24,128]{3,2,1,0:T(8,128)S(1)}, f32[5,24,128]{2,1,0:T(8,128)S(1)}) custom-call(f32[5,4,24,128]{3,2,1,0:T(8,128)S(1)} %get-tuple-element.42.refs_0_, ...), custom_call_target="tpu_custom_call", output_to_operand_aliasing={{0}: (0, {}), {1}: (1, {}), {2}: (2, {}), {3}: (3, {})} | custom-call | tf_op jit(solution)/shard_map/pallas_call | solution.py:420
  17.7 1.7 %collective-permute-start.10 = (f32[5,4,24,128]{3,2,1,0:T(8,128)S(1)}, f32[5,4,24,128]{3,2,1,0:T(8,128)S(1)}, u32[]{:S(2)}, u32[]{:S(2)}) collective-permute-start(f32[5,4,24,128]{3,2,1,0:T(8,128)S(1)} %get-tuple-element.58), channel_id=1, source_target_pairs={{0,1},{1,0},{2,3},{3,2},{4,5},{5,4},{6,7},{7,6},{8,9},{9,8},{10,11... | collective-permute-start | bytes 737288 | tf_op jit(solution)/shard_map/ppermute | solution.py:609
  19.3 2.7 %collective-permute-start.5 = (f32[5,4,24,128]{3,2,1,0:T(8,128)S(1)}, f32[5,4,24,128]{3,2,1,0:T(8,128)S(1)}, u32[]{:S(2)}, u32[]{:S(2)}) collective-permute-start(f32[5,4,24,128]{3,2,1,0:T(8,128)S(1)} %get-tuple-element.54), channel_id=1, source_target_pairs={{0,2},{1,3},{2,0},{3,1},{4,6},{5,7},{6,4},{7,5},{8,10},{9,11},{10,... | collective-permute-start | bytes 737288 | tf_op jit(solution)/shard_map/ppermute | solution.py:609
  22.0 0.1 collective-permute-start.6
  22.1 1.0 %shard_map.73 = f32[8,128]{1,0:T(8,128)S(1)} custom-call(f32[5,24,128]{2,1,0:T(8,128)S(1)} %get-tuple-element.56.refs_0_, f32[8,128]{1,0:T(8,128)S(1)} %get-tuple-element.49.refs_1_.refs_5_, f32[32,128]{1,0:T(8,128)S(1)} %collective-permute-done.left.refs_2_, f32[8,128]{1,0:T(8,128)S(1)} %collective-permute-done.4.refs_3_, ...), custom_call_target="tpu_custom_call" | custom-call | tf_op jit(solution)/shard_map/pallas_call | solution.py:497
  23.1 0.0 collective-permute-start.7
  23.2 1.2 %collective-permute-done.7 = f32[8,128]{1,0:T(8,128)S(1)} collective-permute-done((f32[8,128]{1,0:T(8,128)S(1)}, f32[8,128]{1,0:T(8,128)S(1)}, u32[]{:S(2)}, u32[]{:S(2)}) %collective-permute-start.7) | collective-permute-done | bytes 4128 | tf_op jit(solution)/shard_map/ppermute | solution.py:587
  24.3 0.6 %collective-permute-start.8 = (f32[8,128]{1,0:T(8,128)S(1)}, f32[8,128]{1,0:T(8,128)S(1)}, u32[]{:S(2)}, u32[]{:S(2)}) collective-permute-start(f32[8,128]{1,0:T(8,128)S(1)} %max.18), channel_id=1, source_target_pairs={{0,8},{4,12},{8,0},{12,4},{16,24},{20,28},{24,16},{28,20},{1,9},{5... | collective-permute-start | bytes 12296 | tf_op jit(solution)/shard_map/ppermute | solution.py:587
  25.0 3.0 %collective-permute-done.8 = f32[8,128]{1,0:T(8,128)S(1)} collective-permute-done((f32[8,128]{1,0:T(8,128)S(1)}, f32[8,128]{1,0:T(8,128)S(1)}, u32[]{:S(2)}, u32[]{:S(2)}) %collective-permute-start.8) | collective-permute-done | bytes 4128 | tf_op jit(solution)/shard_map/ppermute | solution.py:587
  27.9 1.6 %collective-permute-start.9 = (f32[8,128]{1,0:T(8,128)S(1)}, f32[8,128]{1,0:T(8,128)S(1)}, u32[]{:S(2)}, u32[]{:S(2)}) collective-permute-start(f32[8,128]{1,0:T(8,128)S(1)} %max.19), channel_id=1, source_target_pairs={{0,16},{4,20},{8,24},{12,28},{16,0},{20,4},{24,8},{28,12},{1,17},{... | collective-permute-start | bytes 12296 | tf_op jit(solution)/shard_map/ppermute | solution.py:587
  29.5 2.0 %collective-permute-done.9 = f32[8,128]{1,0:T(8,128)S(1)} collective-permute-done((f32[8,128]{1,0:T(8,128)S(1)}, f32[8,128]{1,0:T(8,128)S(1)}, u32[]{:S(2)}, u32[]{:S(2)}) %collective-permute-start.9) | collective-permute-done | bytes 4128 | tf_op jit(solution)/shard_map/ppermute | solution.py:587
  31.6 0.0 collective-permute-done.10.refs_2_
  31.6 0.7 %collective-permute-start.11 = (f32[8,128]{1,0:T(8,128)S(1)}, f32[8,128]{1,0:T(8,128)S(1)}, u32[]{:S(2)}, u32[]{:S(2)}) collective-permute-start(f32[8,128]{1,0:T(8,128)S(1)} %max.20), channel_id=1, source_target_pairs={{0,1},{1,0},{2,3},{3,2},{4,5},{5,4},{6,7},{7,6},{8,9},{9,8},{10,11... | collective-permute-start | bytes 12296 | tf_op jit(solution)/shard_map/ppermute | solution.py:587
  32.3 3.6 %collective-permute-start.12 = (f32[8,128]{1,0:T(8,128)S(1)}, f32[8,128]{1,0:T(8,128)S(1)}, u32[]{:S(2)}, u32[]{:S(2)}) collective-permute-start(f32[8,128]{1,0:T(8,128)S(1)} %max.20), channel_id=1, source_target_pairs={{0,2},{1,3},{2,0},{3,1},{4,6},{5,7},{6,4},{7,5},{8,10},{9,11},{10,... | collective-permute-start | bytes 12296 | tf_op jit(solution)/shard_map/ppermute | solution.py:587
  35.8 0.1 collective-permute-start.13
  35.9 0.0 collective-permute-done.11
  35.9 6.9 %collective-permute-done.12 = f32[8,128]{1,0:T(8,128)S(1)} collective-permute-done((f32[8,128]{1,0:T(8,128)S(1)}, f32[8,128]{1,0:T(8,128)S(1)}, u32[]{:S(2)}, u32[]{:S(2)}) %collective-permute-start.12) | collective-permute-done | bytes 4128 | tf_op jit(solution)/shard_map/ppermute | solution.py:587
  42.8 0.0 collective-permute-done.13
  42.8 0.0 collective-permute-done.5.refs_0_
  42.8 0.0 collective-permute-done.6.refs_1_
  42.9 1.4 %shard_map.74 = (f32[5,4,24,512]{3,2,1,0:T(8,128)}, f32[5,64]{1,0:T(8,128)}) custom-call(f32[5,4,24,128]{3,2,1,0:T(8,128)S(1)} %collective-permute-done.5.refs_0_, f32[5,4,24,128]{3,2,1,0:T(8,128)S(1)} %collective-permute-done.6.refs_1_, f32[5,4,24,128]{3,2,1,0:T(8,128)S(1)} %collective-permute-done.10.refs_2_, ...), custom_call_target="tpu_custom_call" | custom-call | tf_op jit(solution)/shard_map/pallas_call | solution.py:553
  (4 shorter events, 0.0 us)
Async XLA Ops:
  0.6 1.3 %copy-start = (s32[6,128]{1,0:T(8,128)S(1)}, s32[6,128]{1,0:T(8,128)}, u32[]{:S(2)}) copy-start(s32[6,128]{1,0:T(8,128)} %membership.1) | copy-start | bytes 9220
  0.6 1.3 %copy-start.1 = (s32[1,4]{1,0:T(1,128)S(1)}, s32[1,4]{1,0:T(1,128)}, u32[]{:S(2)}) copy-start(s32[1,4]{1,0:T(1,128)} %slots.1) | copy-start | bytes 52
  2.6 6.9 %collective-permute-start = (f32[32,128]{1,0:T(8,128)S(1)}, f32[32,128]{1,0:T(8,128)S(1)}, u32[]{:S(2)}, u32[]{:S(2)}) collective-permute-start(f32[32,128]{1,0:T(8,128)S(1)} %get-tuple-element.32), channel_id=1, source_target_pairs={{0,1},{1,2},{2,3},{3,0},{4,5},{5,6},{6,7},{7,4},{8,9},{9,10},{10,1... | collective-permute-start | bytes 49160 | tf_op jit(solution)/shard_map/ppermute | solution.py:596
  5.7 3.9 %collective-permute-start.1 = (f32[32,128]{1,0:T(8,128)S(1)}, f32[32,128]{1,0:T(8,128)S(1)}, u32[]{:S(2)}, u32[]{:S(2)}) collective-permute-start(f32[32,128]{1,0:T(8,128)S(1)} %get-tuple-element.33), channel_id=1, source_target_pairs={{0,3},{1,0},{2,1},{3,2},{4,7},{5,4},{6,5},{7,6},{8,11},{9,8},{10,9... | collective-permute-start | bytes 49160 | tf_op jit(solution)/shard_map/ppermute | solution.py:597
  9.7 7.2 %collective-permute-start.2 = (f32[88,128]{1,0:T(8,128)S(1)}, f32[88,128]{1,0:T(8,128)S(1)}, u32[]{:S(2)}, u32[]{:S(2)}) collective-permute-start(f32[88,128]{1,0:T(8,128)S(1)} %get-tuple-element.46), channel_id=1, source_target_pairs={{0,4},{4,8},{8,12},{12,16},{16,20},{20,24},{24,28},{28,0},{1,5},{5... | collective-permute-start | bytes 135176 | tf_op jit(solution)/shard_map/ppermute | solution.py:602
  9.7 7.1 %collective-permute-start.3 = (f32[88,128]{1,0:T(8,128)S(1)}, f32[88,128]{1,0:T(8,128)S(1)}, u32[]{:S(2)}, u32[]{:S(2)}) collective-permute-start(f32[88,128]{1,0:T(8,128)S(1)} %get-tuple-element.47), channel_id=1, source_target_pairs={{0,28},{4,0},{8,4},{12,8},{16,12},{20,16},{24,20},{28,24},{1,29},{... | collective-permute-start | bytes 135176 | tf_op jit(solution)/shard_map/ppermute | solution.py:603
  12.4 4.5 %collective-permute-start.4 = (f32[8,128]{1,0:T(8,128)S(1)}, f32[8,128]{1,0:T(8,128)S(1)}, u32[]{:S(2)}, u32[]{:S(2)}) collective-permute-start(f32[8,128]{1,0:T(8,128)S(1)} %get-tuple-element.49.refs_1_.refs_5_), channel_id=1, source_target_pairs={{0,2},{1,3},{2,0},{3,1},{4,6},{5,7},{6,4},{7,5},{8,10},{9,11},{10,... | collective-permute-start | bytes 12296 | tf_op jit(solution)/shard_map/ppermute | solution.py:598
  17.7 13.9 %collective-permute-start.10 = (f32[5,4,24,128]{3,2,1,0:T(8,128)S(1)}, f32[5,4,24,128]{3,2,1,0:T(8,128)S(1)}, u32[]{:S(2)}, u32[]{:S(2)}) collective-permute-start(f32[5,4,24,128]{3,2,1,0:T(8,128)S(1)} %get-tuple-element.58), channel_id=1, source_target_pairs={{0,1},{1,0},{2,3},{3,2},{4,5},{5,4},{6,7},{7,6},{8,9},{9,8},{10,11... | collective-permute-start | bytes 737288 | tf_op jit(solution)/shard_map/ppermute | solution.py:609
  19.3 23.5 %collective-permute-start.5 = (f32[5,4,24,128]{3,2,1,0:T(8,128)S(1)}, f32[5,4,24,128]{3,2,1,0:T(8,128)S(1)}, u32[]{:S(2)}, u32[]{:S(2)}) collective-permute-start(f32[5,4,24,128]{3,2,1,0:T(8,128)S(1)} %get-tuple-element.54), channel_id=1, source_target_pairs={{0,2},{1,3},{2,0},{3,1},{4,6},{5,7},{6,4},{7,5},{8,10},{9,11},{10,... | collective-permute-start | bytes 737288 | tf_op jit(solution)/shard_map/ppermute | solution.py:609
  22.0 20.8 %collective-permute-start.6 = (f32[5,4,24,128]{3,2,1,0:T(8,128)S(1)}, f32[5,4,24,128]{3,2,1,0:T(8,128)S(1)}, u32[]{:S(2)}, u32[]{:S(2)}) collective-permute-start(f32[5,4,24,128]{3,2,1,0:T(8,128)S(1)} %get-tuple-element.55), channel_id=1, source_target_pairs={{0,3},{1,2},{2,1},{3,0},{4,7},{5,6},{6,5},{7,4},{8,11},{9,10},{10,... | collective-permute-start | bytes 737288 | tf_op jit(solution)/shard_map/ppermute | solution.py:609
  23.1 1.2 %collective-permute-start.7 = (f32[8,128]{1,0:T(8,128)S(1)}, f32[8,128]{1,0:T(8,128)S(1)}, u32[]{:S(2)}, u32[]{:S(2)}) collective-permute-start(f32[8,128]{1,0:T(8,128)S(1)} %shard_map.73), channel_id=1, source_target_pairs={{0,4},{4,0},{8,12},{12,8},{16,20},{20,16},{24,28},{28,24},{1,5},{5... | collective-permute-start | bytes 12296 | tf_op jit(solution)/shard_map/ppermute | solution.py:587
  24.3 3.6 %collective-permute-start.8 = (f32[8,128]{1,0:T(8,128)S(1)}, f32[8,128]{1,0:T(8,128)S(1)}, u32[]{:S(2)}, u32[]{:S(2)}) collective-permute-start(f32[8,128]{1,0:T(8,128)S(1)} %max.18), channel_id=1, source_target_pairs={{0,8},{4,12},{8,0},{12,4},{16,24},{20,28},{24,16},{28,20},{1,9},{5... | collective-permute-start | bytes 12296 | tf_op jit(solution)/shard_map/ppermute | solution.py:587
  27.9 3.6 %collective-permute-start.9 = (f32[8,128]{1,0:T(8,128)S(1)}, f32[8,128]{1,0:T(8,128)S(1)}, u32[]{:S(2)}, u32[]{:S(2)}) collective-permute-start(f32[8,128]{1,0:T(8,128)S(1)} %max.19), channel_id=1, source_target_pairs={{0,16},{4,20},{8,24},{12,28},{16,0},{20,4},{24,8},{28,12},{1,17},{... | collective-permute-start | bytes 12296 | tf_op jit(solution)/shard_map/ppermute | solution.py:587
  31.6 4.4 %collective-permute-start.11 = (f32[8,128]{1,0:T(8,128)S(1)}, f32[8,128]{1,0:T(8,128)S(1)}, u32[]{:S(2)}, u32[]{:S(2)}) collective-permute-start(f32[8,128]{1,0:T(8,128)S(1)} %max.20), channel_id=1, source_target_pairs={{0,1},{1,0},{2,3},{3,2},{4,5},{5,4},{6,7},{7,6},{8,9},{9,8},{10,11... | collective-permute-start | bytes 12296 | tf_op jit(solution)/shard_map/ppermute | solution.py:587
  32.3 10.6 %collective-permute-start.12 = (f32[8,128]{1,0:T(8,128)S(1)}, f32[8,128]{1,0:T(8,128)S(1)}, u32[]{:S(2)}, u32[]{:S(2)}) collective-permute-start(f32[8,128]{1,0:T(8,128)S(1)} %max.20), channel_id=1, source_target_pairs={{0,2},{1,3},{2,0},{3,1},{4,6},{5,7},{6,4},{7,5},{8,10},{9,11},{10,... | collective-permute-start | bytes 12296 | tf_op jit(solution)/shard_map/ppermute | solution.py:587
  35.8 7.0 %collective-permute-start.13 = (f32[8,128]{1,0:T(8,128)S(1)}, f32[8,128]{1,0:T(8,128)S(1)}, u32[]{:S(2)}, u32[]{:S(2)}) collective-permute-start(f32[8,128]{1,0:T(8,128)S(1)} %max.20), channel_id=1, source_target_pairs={{0,3},{1,2},{2,1},{3,0},{4,7},{5,6},{6,5},{7,4},{8,11},{9,10},{10,... | collective-permute-start | bytes 12296 | tf_op jit(solution)/shard_map/ppermute | solution.py:587

commit v8 on v5

--- a/solution.py
+++ b/solution.py
@@ -344,7 +344,7 @@
 
 
 def leaving_order(count):
-    return [*range(2, count), 1, 0]
+    return [*range(count - 1, 0, -1), 0]
 
 
 def mend_kernel(count, *refs):

time: 42.7 us -> 43 us (level)
  no operation moved by 1% of the time
where the time goes in v8:
time: 43 us; the launch traced here: 42.8 us
  starting transfers between devices  20.1 us (47%)
  waiting for transfers between devices  14 us (33%)
  Pallas kernels  6.66 us (15%)
  other arithmetic  1.31 us (3%)
  between operations  0.73 us (2%)
    ppermute x5, waiting for transfers between devices, with_others(): lax.ppermute(value, axis, exchange_pairs(count, k))  12.8 us
    ppermute x5, starting transfers between devices, with_others(): lax.ppermute(value, axis, exchange_pairs(count, k))  5.41 us
    ppermute x3, starting transfers between devices, per_device(): moved[k] = lax.ppermute(chunks[k], 'section', exchange_pairs(count, k))  4.45 us
    ppermute x1, starting transfers between devices, per_device(): left = lax.ppermute(last_x, 'section', ring('section', 1))  3.06 us
    ppermute x1, starting transfers between devices, per_device(): bottom = lax.ppermute(first_y, 'sim', ring('sim', -1))  2.63 us
    ppermute x1, starting transfers between devices, per_device(): lax.ppermute(labels, 'section', ring('section', d))  2.41 us
    ppermute x1, starting transfers between devices, per_device(): right = lax.ppermute(first_x, 'section', ring('section', -1))  2.09 us
    pallas_call x1, Pallas kernels, transform_bricks(): pl.pallas_call(functools.partial(brick_kernel, count), out_shape=[chunk]...  1.79 us
  transfers between devices with their start and end apart: 13, of which 8 were waited for; matrix products, arithmetic and copies ran while one was open for 0% of the time, Pallas kernels for 9%

profile of v8, /device:TPU:0, one launch (start us, length us, event | category | flops | bytes accessed | tf_op | source)
XLA Modules:
  0.0 42.8 jit_solution(12813488406148750659)
XLA Ops:
  0.6 0.0 copy-start
  0.6 0.0 copy-start.1
  0.7 1.3 %pad_maximum_fusion.conserved = f32[5,4,96,128]{3,2,1,0:T(8,128)S(1)} fusion(f32[1,4,96,128]{3,2,1,0:T(8,128)} %bitcast.2, f32[3,4,96,128]{3,2,1,0:T(8,128)} %param.6, f32[1,4,96,128]{3,2,1,0:T(8,128)} %bitcast.3), kind=kLoop, calls=%fused_computation | loop fusion | flops 491520 | bytes 1966080 | tf_op jit(solution)/shard_map/concatenate | solution.py:594
  2.0 0.0 copy-done
  2.0 0.0 copy-done.1
  2.0 0.6 %shard_map.68 = (f32[32,128]{1,0:T(8,128)S(1)}, f32[32,128]{1,0:T(8,128)S(1)}, f32[8,128]{1,0:T(8,128)S(1)}) custom-call(f32[5,4,96,128]{3,2,1,0:T(8,128)S(1)} %pad_maximum_fusion.conserved, s32[6,128]{1,0:T(8,128)S(1)} %copy-done, s32[1,4]{1,0:T(1,128)S(1)} %copy-done.1), custom_call_target="tpu_custom_call" | custom-call | tf_op jit(solution)/shard_map/pallas_call | solution.py:112
  2.6 3.1 %collective-permute-start = (f32[32,128]{1,0:T(8,128)S(1)}, f32[32,128]{1,0:T(8,128)S(1)}, u32[]{:S(2)}, u32[]{:S(2)}) collective-permute-start(f32[32,128]{1,0:T(8,128)S(1)} %get-tuple-element.30), channel_id=1, source_target_pairs={{0,1},{1,2},{2,3},{3,0},{4,5},{5,6},{6,7},{7,4},{8,9},{9,10},{10,1... | collective-permute-start | bytes 49160 | tf_op jit(solution)/shard_map/ppermute | solution.py:596
  5.7 2.1 %collective-permute-start.1 = (f32[32,128]{1,0:T(8,128)S(1)}, f32[32,128]{1,0:T(8,128)S(1)}, u32[]{:S(2)}, u32[]{:S(2)}) collective-permute-start(f32[32,128]{1,0:T(8,128)S(1)} %get-tuple-element.31), channel_id=1, source_target_pairs={{0,3},{1,0},{2,1},{3,2},{4,7},{5,4},{6,5},{7,6},{8,11},{9,8},{10,9... | collective-permute-start | bytes 49160 | tf_op jit(solution)/shard_map/ppermute | solution.py:597
  7.7 1.0 %shard_map.69 = (f32[20,96,128]{2,1,0:T(8,128)S(1)}, f32[20,112,128]{2,1,0:T(8,128)S(1)}, f32[20,112,128]{2,1,0:T(8,128)S(1)}, bf16[256,256]{1,0:T(8,128)(2,1)S(1)}) custom-call(f32[5,4,96,128]{3,2,1,0:T(8,128)S(1)} %pad_maximum_fusion.conserved), custom_call_target="tpu_custom_call" | custom-call | flops 9830400 | bytes 3932160 | tf_op jit(solution)/shard_map/pallas_call | solution.py:225
  8.7 0.8 %collective-permute-done.left.refs_2_ = f32[32,128]{1,0:T(8,128)S(1)} collective-permute-done((f32[32,128]{1,0:T(8,128)S(1)}, f32[32,128]{1,0:T(8,128)S(1)}, u32[]{:S(2)}, u32[]{:S(2)}) %collective-permute-start) | collective-permute-done | bytes 16416 | tf_op jit(solution)/shard_map/ppermute | solution.py:596
  9.5 0.1 collective-permute-done.1.right.refs_4_
  9.6 0.1 shard_map.70
  9.7 0.1 collective-permute-start.2
  9.7 2.6 %collective-permute-start.3 = (f32[88,128]{1,0:T(8,128)S(1)}, f32[88,128]{1,0:T(8,128)S(1)}, u32[]{:S(2)}, u32[]{:S(2)}) collective-permute-start(f32[88,128]{1,0:T(8,128)S(1)} %get-tuple-element.45), channel_id=1, source_target_pairs={{0,28},{4,0},{8,4},{12,8},{16,12},{20,16},{24,20},{28,24},{1,29},{... | collective-permute-start | bytes 135176 | tf_op jit(solution)/shard_map/ppermute | solution.py:603
  12.4 2.4 %collective-permute-start.4 = (f32[8,128]{1,0:T(8,128)S(1)}, f32[8,128]{1,0:T(8,128)S(1)}, u32[]{:S(2)}, u32[]{:S(2)}) collective-permute-start(f32[8,128]{1,0:T(8,128)S(1)} %get-tuple-element.47.refs_1_.refs_5_), channel_id=1, source_target_pairs={{0,2},{1,3},{2,0},{3,1},{4,6},{5,7},{6,4},{7,5},{8,10},{9,11},{10,... | collective-permute-start | bytes 12296 | tf_op jit(solution)/shard_map/ppermute | solution.py:598
  14.8 1.8 %shard_map.71 = (f32[5,4,24,128]{3,2,1,0:T(8,128)S(1)}, f32[5,4,24,128]{3,2,1,0:T(8,128)S(1)}, f32[5,4,24,128]{3,2,1,0:T(8,128)S(1)}, f32[5,4,24,128]{3,2,1,0:T(...) custom-call(f32[20,96,128]{2,1,0:T(8,128)S(1)} %get-tuple-element.33, ...), custom_call_target="tpu_custom_call" | custom-call | flops 19660800 | bytes 3932160 | tf_op jit(solution)/shard_map/pallas_call | solution.py:328
  16.6 0.3 collective-permute-done.4.refs_3_
  16.9 0.0 collective-permute-done.2.refs_4_
  16.9 0.0 collective-permute-done.3.refs_5_
  16.9 0.8 %shard_map.72 = (f32[5,4,24,128]{3,2,1,0:T(8,128)S(1)}, f32[5,4,24,128]{3,2,1,0:T(8,128)S(1)}, f32[5,4,24,128]{3,2,1,0:T(8,128)S(1)}, f32[5,4,24,128]{3,2,1,0:T(8,128)S(1)}, f32[5,24,128]{2,1,0:T(8,128)S(1)}) custom-call(f32[5,4,24,128]{3,2,1,0:T(8,128)S(1)} %get-tuple-element.40.refs_0_, ...), custom_call_target="tpu_custom_call", output_to_operand_aliasing={{0}: (0, {}), {1}: (1, {}), {2}: (2, {}), {3}: (3, {})} | custom-call | tf_op jit(solution)/shard_map/pallas_call | solution.py:420
  17.7 3.8 %collective-permute-start.5 = (f32[5,4,24,128]{3,2,1,0:T(8,128)S(1)}, f32[5,4,24,128]{3,2,1,0:T(8,128)S(1)}, u32[]{:S(2)}, u32[]{:S(2)}) collective-permute-start(f32[5,4,24,128]{3,2,1,0:T(8,128)S(1)} %get-tuple-element.52), channel_id=1, source_target_pairs={{0,3},{1,2},{2,1},{3,0},{4,7},{5,6},{6,5},{7,4},{8,11},{9,10},{10,... | collective-permute-start | bytes 737288 | tf_op jit(solution)/shard_map/ppermute | solution.py:609
  21.4 0.0 collective-permute-start.6
  21.5 0.7 %collective-permute-start.7 = (f32[5,4,24,128]{3,2,1,0:T(8,128)S(1)}, f32[5,4,24,128]{3,2,1,0:T(8,128)S(1)}, u32[]{:S(2)}, u32[]{:S(2)}) collective-permute-start(f32[5,4,24,128]{3,2,1,0:T(8,128)S(1)} %get-tuple-element.54), channel_id=1, source_target_pairs={{0,1},{1,0},{2,3},{3,2},{4,5},{5,4},{6,7},{7,6},{8,9},{9,8},{10,11... | collective-permute-start | bytes 737288 | tf_op jit(solution)/shard_map/ppermute | solution.py:609
  22.2 1.0 %shard_map.73 = f32[8,128]{1,0:T(8,128)S(1)} custom-call(f32[5,24,128]{2,1,0:T(8,128)S(1)} %get-tuple-element.56.refs_0_, f32[8,128]{1,0:T(8,128)S(1)} %get-tuple-element.47.refs_1_.refs_5_, f32[32,128]{1,0:T(8,128)S(1)} %collective-permute-done.left.refs_2_, f32[8,128]{1,0:T(8,128)S(1)} %collective-permute-done.4.refs_3_, ...), custom_call_target="tpu_custom_call" | custom-call | tf_op jit(solution)/shard_map/pallas_call | solution.py:497
  23.1 0.0 collective-permute-start.8
  23.2 1.2 %collective-permute-done.8 = f32[8,128]{1,0:T(8,128)S(1)} collective-permute-done((f32[8,128]{1,0:T(8,128)S(1)}, f32[8,128]{1,0:T(8,128)S(1)}, u32[]{:S(2)}, u32[]{:S(2)}) %collective-permute-start.8) | collective-permute-done | bytes 4128 | tf_op jit(solution)/shard_map/ppermute | solution.py:587
  24.3 0.7 %collective-permute-start.9 = (f32[8,128]{1,0:T(8,128)S(1)}, f32[8,128]{1,0:T(8,128)S(1)}, u32[]{:S(2)}, u32[]{:S(2)}) collective-permute-start(f32[8,128]{1,0:T(8,128)S(1)} %max.15), channel_id=1, source_target_pairs={{0,8},{4,12},{8,0},{12,4},{16,24},{20,28},{24,16},{28,20},{1,9},{5... | collective-permute-start | bytes 12296 | tf_op jit(solution)/shard_map/ppermute | solution.py:587
  25.0 2.9 %collective-permute-done.9 = f32[8,128]{1,0:T(8,128)S(1)} collective-permute-done((f32[8,128]{1,0:T(8,128)S(1)}, f32[8,128]{1,0:T(8,128)S(1)}, u32[]{:S(2)}, u32[]{:S(2)}) %collective-permute-start.9) | collective-permute-done | bytes 4128 | tf_op jit(solution)/shard_map/ppermute | solution.py:587
  28.0 1.6 %collective-permute-start.10 = (f32[8,128]{1,0:T(8,128)S(1)}, f32[8,128]{1,0:T(8,128)S(1)}, u32[]{:S(2)}, u32[]{:S(2)}) collective-permute-start(f32[8,128]{1,0:T(8,128)S(1)} %max.16), channel_id=1, source_target_pairs={{0,16},{4,20},{8,24},{12,28},{16,0},{20,4},{24,8},{28,12},{1,17},{... | collective-permute-start | bytes 12296 | tf_op jit(solution)/shard_map/ppermute | solution.py:587
  29.6 2.0 %collective-permute-done.10 = f32[8,128]{1,0:T(8,128)S(1)} collective-permute-done((f32[8,128]{1,0:T(8,128)S(1)}, f32[8,128]{1,0:T(8,128)S(1)}, u32[]{:S(2)}, u32[]{:S(2)}) %collective-permute-start.10) | collective-permute-done | bytes 4128 | tf_op jit(solution)/shard_map/ppermute | solution.py:587
  31.6 1.3 %collective-permute-start.11 = (f32[8,128]{1,0:T(8,128)S(1)}, f32[8,128]{1,0:T(8,128)S(1)}, u32[]{:S(2)}, u32[]{:S(2)}) collective-permute-start(f32[8,128]{1,0:T(8,128)S(1)} %max.17), channel_id=1, source_target_pairs={{0,1},{1,0},{2,3},{3,2},{4,5},{5,4},{6,7},{7,6},{8,9},{9,8},{10,11... | collective-permute-start | bytes 12296 | tf_op jit(solution)/shard_map/ppermute | solution.py:587
  32.9 2.8 %collective-permute-done.11 = f32[8,128]{1,0:T(8,128)S(1)} collective-permute-done((f32[8,128]{1,0:T(8,128)S(1)}, f32[8,128]{1,0:T(8,128)S(1)}, u32[]{:S(2)}, u32[]{:S(2)}) %collective-permute-start.11) | collective-permute-done | bytes 4128 | tf_op jit(solution)/shard_map/ppermute | solution.py:587
  35.7 1.7 %collective-permute-start.12 = (f32[8,128]{1,0:T(8,128)S(1)}, f32[8,128]{1,0:T(8,128)S(1)}, u32[]{:S(2)}, u32[]{:S(2)}) collective-permute-start(f32[8,128]{1,0:T(8,128)S(1)} %max.18), channel_id=1, source_target_pairs={{0,2},{1,3},{2,0},{3,1},{4,6},{5,7},{6,4},{7,5},{8,10},{9,11},{10,... | collective-permute-start | bytes 12296 | tf_op jit(solution)/shard_map/ppermute | solution.py:587
  37.4 4.0 %collective-permute-done.12 = f32[8,128]{1,0:T(8,128)S(1)} collective-permute-done((f32[8,128]{1,0:T(8,128)S(1)}, f32[8,128]{1,0:T(8,128)S(1)}, u32[]{:S(2)}, u32[]{:S(2)}) %collective-permute-start.12) | collective-permute-done | bytes 4128 | tf_op jit(solution)/shard_map/ppermute | solution.py:587
  41.4 0.0 collective-permute-done.5.refs_0_
  41.4 0.0 collective-permute-done.6.refs_1_
  41.4 0.0 collective-permute-done.7.refs_2_
  41.4 1.4 %shard_map.74 = (f32[5,4,24,512]{3,2,1,0:T(8,128)}, f32[5,64]{1,0:T(8,128)}) custom-call(f32[5,4,24,128]{3,2,1,0:T(8,128)S(1)} %collective-permute-done.5.refs_0_, f32[5,4,24,128]{3,2,1,0:T(8,128)S(1)} %collective-permute-done.6.refs_1_, f32[5,4,24,128]{3,2,1,0:T(8,128)S(1)} %collective-permute-done.7.refs_2_, ...), custom_call_target="tpu_custom_call" | custom-call | tf_op jit(solution)/shard_map/pallas_call | solution.py:553
  (5 shorter events, 0.0 us)
Async XLA Ops:
  0.6 1.3 %copy-start = (s32[6,128]{1,0:T(8,128)S(1)}, s32[6,128]{1,0:T(8,128)}, u32[]{:S(2)}) copy-start(s32[6,128]{1,0:T(8,128)} %membership.1) | copy-start | bytes 9220
  0.6 1.3 %copy-start.1 = (s32[1,4]{1,0:T(1,128)S(1)}, s32[1,4]{1,0:T(1,128)}, u32[]{:S(2)}) copy-start(s32[1,4]{1,0:T(1,128)} %slots.1) | copy-start | bytes 52
  2.6 6.9 %collective-permute-start = (f32[32,128]{1,0:T(8,128)S(1)}, f32[32,128]{1,0:T(8,128)S(1)}, u32[]{:S(2)}, u32[]{:S(2)}) collective-permute-start(f32[32,128]{1,0:T(8,128)S(1)} %get-tuple-element.30), channel_id=1, source_target_pairs={{0,1},{1,2},{2,3},{3,0},{4,5},{5,6},{6,7},{7,4},{8,9},{9,10},{10,1... | collective-permute-start | bytes 49160 | tf_op jit(solution)/shard_map/ppermute | solution.py:596
  5.7 3.9 %collective-permute-start.1 = (f32[32,128]{1,0:T(8,128)S(1)}, f32[32,128]{1,0:T(8,128)S(1)}, u32[]{:S(2)}, u32[]{:S(2)}) collective-permute-start(f32[32,128]{1,0:T(8,128)S(1)} %get-tuple-element.31), channel_id=1, source_target_pairs={{0,3},{1,0},{2,1},{3,2},{4,7},{5,4},{6,5},{7,6},{8,11},{9,8},{10,9... | collective-permute-start | bytes 49160 | tf_op jit(solution)/shard_map/ppermute | solution.py:597
  9.7 7.2 %collective-permute-start.2 = (f32[88,128]{1,0:T(8,128)S(1)}, f32[88,128]{1,0:T(8,128)S(1)}, u32[]{:S(2)}, u32[]{:S(2)}) collective-permute-start(f32[88,128]{1,0:T(8,128)S(1)} %get-tuple-element.44), channel_id=1, source_target_pairs={{0,4},{4,8},{8,12},{12,16},{16,20},{20,24},{24,28},{28,0},{1,5},{5... | collective-permute-start | bytes 135176 | tf_op jit(solution)/shard_map/ppermute | solution.py:602
  9.7 7.1 %collective-permute-start.3 = (f32[88,128]{1,0:T(8,128)S(1)}, f32[88,128]{1,0:T(8,128)S(1)}, u32[]{:S(2)}, u32[]{:S(2)}) collective-permute-start(f32[88,128]{1,0:T(8,128)S(1)} %get-tuple-element.45), channel_id=1, source_target_pairs={{0,28},{4,0},{8,4},{12,8},{16,12},{20,16},{24,20},{28,24},{1,29},{... | collective-permute-start | bytes 135176 | tf_op jit(solution)/shard_map/ppermute | solution.py:603
  12.4 4.5 %collective-permute-start.4 = (f32[8,128]{1,0:T(8,128)S(1)}, f32[8,128]{1,0:T(8,128)S(1)}, u32[]{:S(2)}, u32[]{:S(2)}) collective-permute-start(f32[8,128]{1,0:T(8,128)S(1)} %get-tuple-element.47.refs_1_.refs_5_), channel_id=1, source_target_pairs={{0,2},{1,3},{2,0},{3,1},{4,6},{5,7},{6,4},{7,5},{8,10},{9,11},{10,... | collective-permute-start | bytes 12296 | tf_op jit(solution)/shard_map/ppermute | solution.py:598
  17.7 23.7 %collective-permute-start.5 = (f32[5,4,24,128]{3,2,1,0:T(8,128)S(1)}, f32[5,4,24,128]{3,2,1,0:T(8,128)S(1)}, u32[]{:S(2)}, u32[]{:S(2)}) collective-permute-start(f32[5,4,24,128]{3,2,1,0:T(8,128)S(1)} %get-tuple-element.52), channel_id=1, source_target_pairs={{0,3},{1,2},{2,1},{3,0},{4,7},{5,6},{6,5},{7,4},{8,11},{9,10},{10,... | collective-permute-start | bytes 737288 | tf_op jit(solution)/shard_map/ppermute | solution.py:609
  21.4 20.0 %collective-permute-start.6 = (f32[5,4,24,128]{3,2,1,0:T(8,128)S(1)}, f32[5,4,24,128]{3,2,1,0:T(8,128)S(1)}, u32[]{:S(2)}, u32[]{:S(2)}) collective-permute-start(f32[5,4,24,128]{3,2,1,0:T(8,128)S(1)} %get-tuple-element.53), channel_id=1, source_target_pairs={{0,2},{1,3},{2,0},{3,1},{4,6},{5,7},{6,4},{7,5},{8,10},{9,11},{10,... | collective-permute-start | bytes 737288 | tf_op jit(solution)/shard_map/ppermute | solution.py:609
  21.5 20.0 %collective-permute-start.7 = (f32[5,4,24,128]{3,2,1,0:T(8,128)S(1)}, f32[5,4,24,128]{3,2,1,0:T(8,128)S(1)}, u32[]{:S(2)}, u32[]{:S(2)}) collective-permute-start(f32[5,4,24,128]{3,2,1,0:T(8,128)S(1)} %get-tuple-element.54), channel_id=1, source_target_pairs={{0,1},{1,0},{2,3},{3,2},{4,5},{5,4},{6,7},{7,6},{8,9},{9,8},{10,11... | collective-permute-start | bytes 737288 | tf_op jit(solution)/shard_map/ppermute | solution.py:609
  23.1 1.2 %collective-permute-start.8 = (f32[8,128]{1,0:T(8,128)S(1)}, f32[8,128]{1,0:T(8,128)S(1)}, u32[]{:S(2)}, u32[]{:S(2)}) collective-permute-start(f32[8,128]{1,0:T(8,128)S(1)} %shard_map.73), channel_id=1, source_target_pairs={{0,4},{4,0},{8,12},{12,8},{16,20},{20,16},{24,28},{28,24},{1,5},{5... | collective-permute-start | bytes 12296 | tf_op jit(solution)/shard_map/ppermute | solution.py:587
  24.3 3.6 %collective-permute-start.9 = (f32[8,128]{1,0:T(8,128)S(1)}, f32[8,128]{1,0:T(8,128)S(1)}, u32[]{:S(2)}, u32[]{:S(2)}) collective-permute-start(f32[8,128]{1,0:T(8,128)S(1)} %max.15), channel_id=1, source_target_pairs={{0,8},{4,12},{8,0},{12,4},{16,24},{20,28},{24,16},{28,20},{1,9},{5... | collective-permute-start | bytes 12296 | tf_op jit(solution)/shard_map/ppermute | solution.py:587
  28.0 3.6 %collective-permute-start.10 = (f32[8,128]{1,0:T(8,128)S(1)}, f32[8,128]{1,0:T(8,128)S(1)}, u32[]{:S(2)}, u32[]{:S(2)}) collective-permute-start(f32[8,128]{1,0:T(8,128)S(1)} %max.16), channel_id=1, source_target_pairs={{0,16},{4,20},{8,24},{12,28},{16,0},{20,4},{24,8},{28,12},{1,17},{... | collective-permute-start | bytes 12296 | tf_op jit(solution)/shard_map/ppermute | solution.py:587
  31.6 4.1 %collective-permute-start.11 = (f32[8,128]{1,0:T(8,128)S(1)}, f32[8,128]{1,0:T(8,128)S(1)}, u32[]{:S(2)}, u32[]{:S(2)}) collective-permute-start(f32[8,128]{1,0:T(8,128)S(1)} %max.17), channel_id=1, source_target_pairs={{0,1},{1,0},{2,3},{3,2},{4,5},{5,4},{6,7},{7,6},{8,9},{9,8},{10,11... | collective-permute-start | bytes 12296 | tf_op jit(solution)/shard_map/ppermute | solution.py:587
  35.7 5.7 %collective-permute-start.12 = (f32[8,128]{1,0:T(8,128)S(1)}, f32[8,128]{1,0:T(8,128)S(1)}, u32[]{:S(2)}, u32[]{:S(2)}) collective-permute-start(f32[8,128]{1,0:T(8,128)S(1)} %max.18), channel_id=1, source_target_pairs={{0,2},{1,3},{2,0},{3,1},{4,6},{5,7},{6,4},{7,5},{8,10},{9,11},{10,... | collective-permute-start | bytes 12296 | tf_op jit(solution)/shard_map/ppermute | solution.py:587
